TPU v7x, 32 devices: a whole 2x2x4 slice. The times are simulated.
32 devices in a mesh: groups: 2 (over y), epoch: 4 (over z), tile: 4 (over x, core).
Axes of the slice: x: 2, y: 2, z: 4, core: 2. Of those that a mesh axis runs over, the one named last changes fastest.
Arguments:
- frames: bfloat16 [8, 128, 16, 384], P('epoch', ('groups', 'tile')), parts along dimension 1, may hold values from -6 to 6
- valid: int32 [8, 128, 16], P('epoch', ('groups', 'tile')), parts along dimension 1, may hold values 0 or 1
- days: int32 [16], P('groups'), parts along dimension 0, may hold values from 0 to 239, as said below
- dw_kernel: float32 [7, 7, 384], replicated, may hold values from -0.875 to 0.875
- dw_bias: float32 [384], replicated, may hold values from -3 to 3
- norm_gain: float32 [384], replicated, may hold values from 0.5 to 1.5
- norm_shift: float32 [384], replicated, may hold values from -1.75 to 1.75
- w_expand: bfloat16 [384, 1536], replicated, may hold values from -0.3125 to 0.3125
- b_expand: float32 [1536], replicated, may hold values from -3 to 3
- w_reduce: bfloat16 [1536, 384], replicated, may hold values from -0.15625 to 0.15625
- layer_scale: float32 [384], replicated, may hold values from 0.3 to 1
- w_gates: bfloat16 [3, 3, 384, 1536], replicated, may hold values from -0.109375 to 0.109375
- b_gates: float32 [1536], replicated, may hold values from -3 to 3
- forget_rate: float32 [384], replicated, may hold values from 0.0625 to 1
- attn_gain: float32 [384], replicated, may hold values from 0.5 to 1.5
- w_query: bfloat16 [384, 384], replicated, as said below
- w_key: bfloat16 [384, 384], replicated, as said below
- w_value: bfloat16 [384, 384], replicated, may hold values from -0.3125 to 0.3125
- w_out: bfloat16 [384, 384], replicated, may hold values from -0.3125 to 0.3125
- head_slope: float32 [8], replicated, may hold values from 0.02 to 1
Outputs:
- memory: bfloat16 [8, 128, 16, 384], P('epoch', ('groups', 'tile')), parts along dimension 1
- change: bfloat16 [8, 8, 1, 384], P('epoch', ('groups', 'tile')), parts along dimension 1
There are 2 independent parts, one for each index of `groups`. A program takes and returns all parts, laid end to end along the dimension named above; an argument that names none is the same for every part. Nothing has to cross between parts.
Inputs may be any that keep to these rules, and one draw needn't show every extreme that they name: days[t] lies between 30 t and 30 t + 29, so days rise strictly. `w_query`: a projection of the normalized patch features. `w_key`: a projection of the normalized patch features.
All inputs are finite; a program needn't handle non-finite values. No bound on the sum of `valid` on one device may be relied on, other than what follows from the above.
Results may differ from a plain program's by a relative error of at most 0.008.
Values may be sent and summed in bfloat16 or wider, within the bound.
No kernel may reach another device: no remote copies, remote signals or barrier semaphores. Data moves between devices by JAX's collectives and lax.ppermute only.
A program may use at most 192 MiB of HBM per device.

v0:
```python
import math

import jax
import jax.numpy as jnp
from jax import lax
from jax.sharding import PartitionSpec as P

PATCH = 16


def extended(block, sides, width):
    for axis, dim in sides:
        count = lax.axis_size(axis)
        forward = [(i, i + 1) for i in range(count - 1)]
        backward = [(target, source) for source, target in forward]
        low = lax.ppermute(
            lax.slice_in_dim(block, block.shape[dim] - width, None, axis=dim), axis, forward
        )
        high = lax.ppermute(lax.slice_in_dim(block, 0, width, axis=dim), axis, backward)
        block = jnp.concatenate([low, block, high], axis=dim)
    return block


def from_behind(block, axis, distance):
    devices = range(lax.axis_size(axis))
    route = [(i - distance, i) for i in devices if i - distance in devices]
    return lax.ppermute(block, axis, route)


def layer_norm(values):
    center = jnp.mean(values, axis=-1, keepdims=True)
    centred = values - center
    spread = jnp.mean(centred * centred, axis=-1, keepdims=True)
    return centred * lax.rsqrt(spread + 1e-06)


def depthwise(padded, kernel, height, width):
    total = jnp.zeros(padded.shape[:-3] + (height, width, padded.shape[-1]), jnp.float32)
    for offset_y in range(7):
        for offset_x in range(7):
            window = padded[..., offset_y : offset_y + height, offset_x : offset_x + width, :]
            total = total + window.astype(jnp.float32) * kernel[offset_y, offset_x]
    return total


def gate_conv(padded, weights, height, width):
    channels = padded.shape[-1]
    total = None
    for offset_y in range(3):
        for offset_x in range(3):
            window = padded[
                ..., offset_y : offset_y + height, offset_x : offset_x + width, :
            ].reshape(-1, channels)
            term = jnp.dot(window, weights[offset_y, offset_x], preferred_element_type=jnp.float32)
            total = term if total is None else total + term
    return total


def cell_inputs(preact, keep_mask, rates):
    count = preact.shape[-1] // 4
    split = preact.reshape(preact.shape[:-1] + (count, 4))
    gate_in = split[..., 0]
    gate_keep = split[..., 1]
    gate_new = split[..., 2]
    gate_out = split[..., 3]
    mask = keep_mask[..., None]
    decay = jnp.where(mask, jnp.exp(-rates * jax.nn.softplus(gate_keep)), 1.0)
    inflow = jnp.where(mask, jax.nn.sigmoid(gate_in) * jnp.tanh(gate_new), 0.0)
    return (decay, inflow, gate_out)


def convnext(
    rimmed,
    centre,
    out_rows,
    dw_kernel,
    dw_bias,
    norm_gain,
    norm_shift,
    w_expand,
    b_expand,
    w_reduce,
    layer_scale,
):
    width = rimmed.shape[2]
    channels = rimmed.shape[3]
    padded = jnp.pad(rimmed, ((0, 0), (0, 0), (3, 3), (0, 0)))
    spread = depthwise(padded, dw_kernel, out_rows, width) + dw_bias
    normed = (layer_norm(spread) * norm_gain + norm_shift).astype(jnp.bfloat16)
    expanded = jax.nn.gelu(
        jnp.dot(normed.reshape(-1, channels), w_expand, preferred_element_type=jnp.float32)
        + b_expand,
        approximate=True,
    ).astype(jnp.bfloat16)
    reduced = jnp.dot(expanded, w_reduce, preferred_element_type=jnp.float32)
    return (centre.astype(jnp.float32) + layer_scale * reduced.reshape(centre.shape)).astype(
        jnp.bfloat16
    )


def body(
    frames,
    valid,
    days,
    dw_kernel,
    dw_bias,
    norm_gain,
    norm_shift,
    w_expand,
    b_expand,
    w_reduce,
    layer_scale,
    w_gates,
    b_gates,
    forget_rate,
    attn_gain,
    w_query,
    w_key,
    w_value,
    w_out,
    head_slope,
):
    epochs_dev, height, width, channels = frames.shape
    rimmed = extended(frames, (("tile", 1),), 3)
    features = convnext(
        rimmed,
        frames,
        height,
        dw_kernel,
        dw_bias,
        norm_gain,
        norm_shift,
        w_expand,
        b_expand,
        w_reduce,
        layer_scale,
    )
    rim_single = extended(features, (("tile", 1),), 1)
    feature_pad = jnp.pad(rim_single, ((0, 0), (0, 0), (1, 1), (0, 0)))
    columns = w_gates.shape[3]
    preact = (gate_conv(feature_pad, w_gates, height, width) + b_gates).reshape(
        epochs_dev, height, width, columns
    )
    decay, inflow, gate_out = cell_inputs(preact, valid > 0, forget_rate)
    block_keep = jnp.prod(decay, axis=0)
    block_cell = jnp.zeros(decay.shape[1:], jnp.float32)
    for step in range(epochs_dev):
        block_cell = decay[step] * block_cell + inflow[step]

    def relay_turn(turn, arriving):
        return from_behind(block_keep * arriving + block_cell, "epoch", 1)

    incoming = lax.fori_loop(0, lax.axis_size("epoch") - 1, relay_turn, jnp.zeros_like(block_cell))
    cell = incoming
    results = []
    for step in range(epochs_dev):
        cell = decay[step] * cell + inflow[step]
        results.append((jax.nn.sigmoid(gate_out[step]) * jnp.tanh(cell)).astype(jnp.bfloat16))
    memory = jnp.stack(results)
    rows_patch = height // PATCH
    cols_patch = width // PATCH
    patches = rows_patch * cols_patch
    pooled = (
        memory.astype(jnp.float32)
        .reshape(epochs_dev, rows_patch, PATCH, cols_patch, PATCH, channels)
        .mean(axis=(2, 4))
    )
    tokens = (layer_norm(pooled.reshape(-1, channels)) * attn_gain).astype(jnp.bfloat16)
    heads = head_slope.shape[0]
    head_dim = channels // heads

    def project(weight):
        return (
            jnp.dot(tokens, weight, preferred_element_type=jnp.float32)
            .astype(jnp.bfloat16)
            .reshape(epochs_dev, patches, heads, head_dim)
        )

    queries = project(w_query)
    keys_own = project(w_key)
    values_own = project(w_value)
    months = days.astype(jnp.float32) / 30.0
    query_index = lax.axis_index("epoch") * epochs_dev + jnp.arange(epochs_dev, dtype=jnp.int32)
    query_months = lax.dynamic_slice_in_dim(
        months, lax.axis_index("epoch") * epochs_dev, epochs_dev
    )
    queries_wide = queries.astype(jnp.float32)
    all_keys, all_values = (
        lax.all_gather(keys_own, "epoch", axis=0, tiled=True),
        lax.all_gather(values_own, "epoch", axis=0, tiled=True),
    )
    key_count = all_keys.shape[0]
    key_index = jnp.arange(key_count, dtype=jnp.int32)
    raw = jnp.einsum(
        "tphd,sphd->hpts",
        queries_wide,
        all_keys.astype(jnp.float32),
        precision=lax.Precision.HIGHEST,
    ) / math.sqrt(head_dim)
    bias = (
        -head_slope[:, None, None, None]
        * (query_months[:, None] - months[None, :])[None, None, :, :]
    )
    allowed = query_index[:, None] >= key_index[None, :]
    scores = jnp.where(allowed[None, None], raw + bias, -1e30)
    top = jnp.max(scores, axis=-1, keepdims=True)
    expo = jnp.exp(scores - top)
    weights = expo / jnp.sum(expo, axis=-1, keepdims=True)
    mixed = jnp.einsum(
        "hpts,sphd->hptd", weights, all_values.astype(jnp.float32), precision=lax.Precision.HIGHEST
    )
    mixed_tokens = jnp.transpose(mixed, (2, 1, 0, 3)).reshape(-1, channels).astype(jnp.bfloat16)
    change = jnp.dot(mixed_tokens, w_out, preferred_element_type=jnp.float32).astype(jnp.bfloat16)
    return (memory, change.reshape(epochs_dev, rows_patch, cols_patch, channels))


def solution(mesh):
    placed = (
        P("epoch", ("groups", "tile"), None, None),
        P("epoch", ("groups", "tile"), None),
        P("groups"),
        P(),
        P(),
        P(),
        P(),
        P(),
        P(),
        P(),
        P(),
        P(),
        P(),
        P(),
        P(),
        P(),
        P(),
        P(),
        P(),
        P(),
    )
    return jax.shard_map(
        body,
        mesh=mesh,
        in_specs=placed,
        out_specs=(
            P("epoch", ("groups", "tile"), None, None),
            P("epoch", ("groups", "tile"), None, None),
        ),
        check_vma=False,
    )
```

profile of v0, /device:TPU:0, one launch (start us, length us, event | category | flops | bytes accessed | tf_op | source)
XLA Modules:
  0.0 185.1 jit_solution(16929431659440542832)
XLA Ops:
  1.7 2.4 %collective-permute-start.1 = (bf16[2,3,16,384]{3,2,1,0:T(8,128)(2,1)S(1)}, bf16[2,3,16,384]{3,2,1,0:T(8,128)(2,1)S(1)}, u32[]{:S(2)}, u32[]{:S(2)}) collective-permute-start(bf16[2,3,16,384]{3,2,1,0:T(8,128)(2,1)S(1)} %get-tuple-element.123), channel_id=1, source_target_pairs={{0,1},{1,2},{2,3},{4,5},{5,6},{6,7},{8,9},{9,10},{10,11},{12,13},{... | collective-permute-start | bytes 221192 | tf_op jit(solution)/shard_map/ppermute | solution.py:16
  4.1 1.3 collective-permute-start.2
  5.4 1.3 slice_reduce_fusion.48
  11.6 1.4 fusion.41
  13.1 5.9 %fusion.103 = (f32[2,16,16]{2,1,0:T(8,128)S(1)}, f32[2,16,16,384]{3,2,1,0:T(8,128)S(1)}) fusion(f32[384]{0:T(512)S(1)} %copy-done.6, f32[384]{0:T(512)S(1)} %get-tuple-element.90, bf16[2,22,22,384]{3,2,1,0:T(8,128)(2,1)S(1)} %fusion.41, f32[384]{0:T(512)S(1)} %get-tuple-element.91, f32[384]{0:T(512)S(1)} %get-tuple-element.44, ...), kind=kLoop, calls=%fused_computation.210 | loop fusion | flops 29097472 | bytes 20132864 | tf_op jit(solution)/shard_map/reduce_sum | solution.py:31
  19.6 3.2 %fusion.32 = f32[512,384]{1,0:T(8,128)S(1)} fusion(bf16[1536,384]{1,0:T(8,128)(2,1)S(1)} %copy-done, bf16[512,384]{1,0:T(8,128)(2,1)S(1)} %bitcast.188, bf16[384,1536]{1,0:T(8,128)(2,1)} %param.29, f32[1536]{0:T(1024)S(1)} %copy-done.12), kind=kOutput, calls=%fused_computation.49 | convolution fusion | flops 1215823872 | bytes 3545088 | tf_op jit(solution)/shard_map/dot_general | solution.py:95
  23.0 5.4 %collective-permute-start.3 = (bf16[2,1,16,384]{3,2,1,0:T(8,128)(2,1)S(1)}, bf16[2,1,16,384]{3,2,1,0:T(8,128)(2,1)S(1)}, u32[]{:S(2)}, u32[]{:S(2)}) collective-permute-start(bf16[2,1,16,384]{3,2,1,0:T(8,128)(2,1)S(1)} %get-tuple-element.119), channel_id=1, source_target_pairs={{0,1},{1,2},{2,3},{4,5},{5,6},{6,7},{8,9},{9,10},{10,11},{12,13},{... | collective-permute-start | bytes 73736 | tf_op jit(solution)/shard_map/ppermute | solution.py:16
  28.4 1.3 collective-permute-start.4
  29.8 2.9 %collective-permute-done.4 = bf16[2,1,16,384]{3,2,1,0:T(8,128)(2,1)S(1)} collective-permute-done((bf16[2,1,16,384]{3,2,1,0:T(8,128)(2,1)S(1)}, bf16[2,1,16,384]{3,2,1,0:T(8,128)(2,1)S(1)}, u32[]{:S(2)}, u32[]{:S(2)}) %collective-permute-start.4) | collective-permute-done | bytes 24608 | tf_op jit(solution)/shard_map/ppermute | solution.py:19
  33.3 2.4 %fusion.21 = f32[512,1536]{1,0:T(8,128)S(1)} fusion(bf16[512,384]{1,0:T(8,128)(2,1)S(1)} %bitcast.176, bf16[3,3,384,1536]{3,2,1,0:T(8,128)(2,1)} %param.33), kind=kOutput, calls=%fused_computation.38 | convolution fusion | flops 603979776 | bytes 4718592 | tf_op jit(solution)/shard_map/dot_general | solution.py:54
  35.7 2.4 %fusion.12 = f32[512,1536]{1,0:T(8,128)S(1)} fusion(bf16[512,384]{1,0:T(8,128)(2,1)S(1)} %bitcast.175, bf16[3,3,384,1536]{3,2,1,0:T(8,128)(2,1)} %param.33), kind=kOutput, calls=%fused_computation.29 | convolution fusion | flops 603979776 | bytes 4718592 | tf_op jit(solution)/shard_map/dot_general | solution.py:54
  44.2 2.7 %fusion.1 = f32[512,1536]{1,0:T(8,128)} fusion(f32[512,1536]{1,0:T(8,128)S(1)} %fusion.12, f32[512,1536]{1,0:T(8,128)S(1)} %convolution_add_fusion.1, bf16[512,384]{1,0:T(8,128)(2,1)S(1)} %bitcast.181, f32[1536]{0:T(1024)S(1)} %copy-done.5, bf16[3,3,384,1536]{3,2,1,0:T(8,128)(2,1)S(1)} %bitcast.173), kind=kOutput, calls=%fused_computation.4 | convolution fusion | flops 606339072 | bytes 11018240 | tf_op jit(solution)/shard_map/dot_general | solution.py:54
  46.9 3.6 %copy.87 = f32[512,1536]{0,1:T(8,128)} copy(f32[512,1536]{1,0:T(8,128)} %fusion.1) | data formatting | bytes 6291456 | tf_op jit(solution)/shard_map/add | solution.py:141
  50.5 15.3 %reshape_reshape.3 = f32[2,16,16,384,4]{2,1,0,4,3:T(8,128)} reshape(f32[512,1536]{0,1:T(8,128)} %copy.87) | data formatting | bytes 6291456 | tf_op jit(solution)/shard_map/reshape;reshape | solution.py:61
  65.8 13.8 %fusion.106 = (f32[2,16,16,384,1]{2,1,0,4,3:T(8,128)}, f32[2,16,16,384,1]{2,1,0,4,3:T(8,128)}, f32[2,16,16,384,1]{2,1,0,4,3:T(8,128)}) fusion(f32[2,16,16,384,4]{2,1,0,4,3:T(8,128)} %reshape_reshape.3), kind=kLoop, calls=%fused_computation.212 | loop fusion | bytes 4718592 | tf_op jit(solution)/shard_map/slice | solution.py:62
  79.6 5.9 %fusion.105 = (f32[1,16,16,384,1]{2,1,0,4,3:T(8,128)}, f32[1,16,16,384,1]{2,1,0,4,3:T(8,128)}) fusion(f32[2,16,16,384,4]{2,1,0,4,3:T(8,128)} %reshape_reshape.3), kind=kLoop, calls=%fused_computation.211 | loop fusion | bytes 1572864 | tf_op jit(solution)/shard_map/slice | solution.py:158
  85.4 6.1 %copy.109 = f32[2,16,16,384,1]{3,2,1,0,4:T(8,128)} copy(f32[2,16,16,384,1]{2,1,0,4,3:T(8,128)} %get-tuple-element.107) | data formatting | bytes 1572864
  91.6 6.1 %copy.110 = f32[2,16,16,384,1]{3,2,1,0,4:T(8,128)} copy(f32[2,16,16,384,1]{2,1,0,4,3:T(8,128)} %get-tuple-element.106) | data formatting | bytes 1572864
  97.7 6.1 %copy.111 = f32[2,16,16,384,1]{3,2,1,0,4:T(8,128)} copy(f32[2,16,16,384,1]{2,1,0,4,3:T(8,128)} %get-tuple-element.108) | data formatting | bytes 1572864
  103.8 2.3 %copy.108 = f32[1,16,16,384,1]{3,2,1,4,0:T(8,128)S(1)} copy(f32[1,16,16,384,1]{2,1,0,4,3:T(8,128)} %get-tuple-element.104) | data formatting | bytes 786432
  106.1 3.0 %copy.112 = f32[1,16,16,384,1]{3,2,4,1,0:T(8,128)} copy(f32[1,16,16,384,1]{2,1,0,4,3:T(8,128)} %get-tuple-element.105) | data formatting | bytes 786432
  109.2 2.4 %fusion.101 = (f32[16,16,384]{2,1,0:T(8,128)S(1)}, f32[2,16,16,384]{3,2,1,0:T(8,128)S(1)}, f32[2,16,16,384]{3,2,1,0:T(8,128)S(1)}) fusion(f32[2,16,16,384,1]{3,2,1,0,4:T(8,128)} %copy.109, f32[384]{0:T(512)S(1)} %neg.24, pred[2,16,16]{2,1,0:T(8,128)(4,1)S(1)} %broadcast_compare_fusion, f32[2,16,16,384,1]{3,2,1,0,4:T(8,128)} %copy.111, ...), kind=kLoop, calls=%fused_computation.209 | loop fusion | flops 2654208 | bytes 4327424 | tf_op jit(solution)/shard_map/reduce_prod | solution.py:145
  112.4 38.1 %while.10 = (s32[]{:T(128)}, f32[16,16,384]{2,1,0:T(8,128)S(1)}, f32[16,16,384]{2,1,0:T(8,128)S(1)}, f32[16,16,384]{2,1,0:T(8,128)S(1)}, s32[]{:T(128)}) while((s32[]{:T(128)}, f32[16,16,384]{2,1,0:T(8,128)S(1)}, f32[16,16,384]{2,1,0:T(8,128)S(1)}, f32[16,16,384]{2,1,0:T(8,128)S(1)}, s32[]{:T(128)}) %tuple.90), condition=%wide.region_4.5_spmd, body=%wide.region_3.4_spmd.sunk | while | flops 196610 | bytes 3145829 | solution.py:153
  112.5 3.5 %collective-permute-start = (f32[16,16,384]{2,1,0:T(8,128)S(1)}, f32[16,16,384]{2,1,0:T(8,128)S(1)}, u32[]{:S(2)}, u32[]{:S(2)}) collective-permute-start(f32[16,16,384]{2,1,0:T(8,128)S(1)} %multiply_add_fusion.4), channel_id=1, source_target_pairs={{0,4},{4,8},{8,12},{1,5},{5,9},{9,13},{2,6},{6,10},{10,14},{3,7},{... | collective-permute-start | bytes 1179656 | tf_op jit(solution)/shard_map/while/body/eval_jaxpr/ppermute | solution.py:27
  116.0 7.8 %collective-permute-done = f32[16,16,384]{2,1,0:T(8,128)S(1)} collective-permute-done((f32[16,16,384]{2,1,0:T(8,128)S(1)}, f32[16,16,384]{2,1,0:T(8,128)S(1)}, u32[]{:S(2)}, u32[]{:S(2)}) %collective-permute-start) | collective-permute-done | bytes 393248 | tf_op jit(solution)/shard_map/while/body/eval_jaxpr/ppermute | solution.py:27
  123.9 4.4 %collective-permute-start = (f32[16,16,384]{2,1,0:T(8,128)S(1)}, f32[16,16,384]{2,1,0:T(8,128)S(1)}, u32[]{:S(2)}, u32[]{:S(2)}) collective-permute-start(f32[16,16,384]{2,1,0:T(8,128)S(1)} %multiply_add_fusion.4), channel_id=1, source_target_pairs={{0,4},{4,8},{8,12},{1,5},{5,9},{9,13},{2,6},{6,10},{10,14},{3,7},{... | collective-permute-start | bytes 1179656 | tf_op jit(solution)/shard_map/while/body/eval_jaxpr/ppermute | solution.py:27
  128.3 9.0 %collective-permute-done = f32[16,16,384]{2,1,0:T(8,128)S(1)} collective-permute-done((f32[16,16,384]{2,1,0:T(8,128)S(1)}, f32[16,16,384]{2,1,0:T(8,128)S(1)}, u32[]{:S(2)}, u32[]{:S(2)}) %collective-permute-start) | collective-permute-done | bytes 393248 | tf_op jit(solution)/shard_map/while/body/eval_jaxpr/ppermute | solution.py:27
  137.4 4.4 %collective-permute-start = (f32[16,16,384]{2,1,0:T(8,128)S(1)}, f32[16,16,384]{2,1,0:T(8,128)S(1)}, u32[]{:S(2)}, u32[]{:S(2)}) collective-permute-start(f32[16,16,384]{2,1,0:T(8,128)S(1)} %multiply_add_fusion.4), channel_id=1, source_target_pairs={{0,4},{4,8},{8,12},{1,5},{5,9},{9,13},{2,6},{6,10},{10,14},{3,7},{... | collective-permute-start | bytes 1179656 | tf_op jit(solution)/shard_map/while/body/eval_jaxpr/ppermute | solution.py:27
  141.8 8.8 %collective-permute-done = f32[16,16,384]{2,1,0:T(8,128)S(1)} collective-permute-done((f32[16,16,384]{2,1,0:T(8,128)S(1)}, f32[16,16,384]{2,1,0:T(8,128)S(1)}, u32[]{:S(2)}, u32[]{:S(2)}) %collective-permute-start) | collective-permute-done | bytes 393248 | tf_op jit(solution)/shard_map/while/body/eval_jaxpr/ppermute | solution.py:27
  150.6 1.7 fusion.86
  154.2 14.3 %all_gather.6 = bf16[8,1,8,48]{3,2,1,0:T(8,128)(2,1)S(1)} all-gather(bf16[2,1,8,48]{3,2,1,0:T(8,128)(2,1)S(1)} %bitcast.189), channel_id=1, replica_groups=mesh['groups'=2,'epoch'=4,'tile'=4] {'epoch'}, dimensions={0}, use_global_device_ids=true | all-gather | bytes 7680 | tf_op jit(solution)/shard_map/all_gather | solution.py:189
  169.7 13.1 %all_gather.7 = bf16[8,1,8,48]{3,2,1,0:T(8,128)(2,1)S(1)} all-gather(bf16[2,1,8,48]{3,2,1,0:T(8,128)(2,1)S(1)} %bitcast.190), channel_id=1, replica_groups=mesh['groups'=2,'epoch'=4,'tile'=4] {'epoch'}, dimensions={0}, use_global_device_ids=true | all-gather | bytes 7680 | tf_op jit(solution)/shard_map/all_gather | solution.py:190
  (92 shorter events, 19.8 us)
Async XLA Ops:
  0.6 18.9 %copy-start = (bf16[1536,384]{1,0:T(8,128)(2,1)S(1)}, bf16[1536,384]{1,0:T(8,128)(2,1)}, u32[]{:S(2)}) copy-start(bf16[1536,384]{1,0:T(8,128)(2,1)} %param.31) | copy-start | bytes 3538948
  0.6 12.4 %copy-start.2 = (bf16[2,16,16,384]{3,2,1,0:T(8,128)(2,1)S(1)}, bf16[2,16,16,384]{3,2,1,0:T(8,128)(2,1)}, u32[]{:S(2)}) copy-start(bf16[2,16,16,384]{3,2,1,0:T(8,128)(2,1)} %param.22) | copy-start | bytes 1179652
  0.7 12.4 %copy-start.6 = (f32[384]{0:T(512)S(1)}, f32[384]{0:T(512)}, u32[]{:S(2)}) copy-start(f32[384]{0:T(512)} %param.26) | copy-start | bytes 4612
  1.7 8.8 %collective-permute-start.1 = (bf16[2,3,16,384]{3,2,1,0:T(8,128)(2,1)S(1)}, bf16[2,3,16,384]{3,2,1,0:T(8,128)(2,1)S(1)}, u32[]{:S(2)}, u32[]{:S(2)}) collective-permute-start(bf16[2,3,16,384]{3,2,1,0:T(8,128)(2,1)S(1)} %get-tuple-element.123), channel_id=1, source_target_pairs={{0,1},{1,2},{2,3},{4,5},{5,6},{6,7},{8,9},{9,10},{10,11},{12,13},{... | collective-permute-start | bytes 221192 | tf_op jit(solution)/shard_map/ppermute | solution.py:16
  4.1 7.5 %collective-permute-start.2 = (bf16[2,3,16,384]{3,2,1,0:T(8,128)(2,1)S(1)}, bf16[2,3,16,384]{3,2,1,0:T(8,128)(2,1)S(1)}, u32[]{:S(2)}, u32[]{:S(2)}) collective-permute-start(bf16[2,3,16,384]{3,2,1,0:T(8,128)(2,1)S(1)} %get-tuple-element.124), channel_id=1, source_target_pairs={{1,0},{2,1},{3,2},{5,4},{6,5},{7,6},{9,8},{10,9},{11,10},{13,12},{... | collective-permute-start | bytes 221192 | tf_op jit(solution)/shard_map/ppermute | solution.py:19
  13.0 6.3 %copy-start.7 = (f32[384]{0:T(512)S(1)}, f32[384]{0:T(512)}, u32[]{:S(2)}) copy-start(f32[384]{0:T(512)} %param.28) | copy-start | bytes 4612
  13.1 6.3 %copy-start.8 = (f32[384]{0:T(512)S(1)}, f32[384]{0:T(512)}, u32[]{:S(2)}) copy-start(f32[384]{0:T(512)} %param.27) | copy-start | bytes 4612
  13.1 6.5 %copy-start.12 = (f32[1536]{0:T(1024)S(1)}, f32[1536]{0:T(1024)}, u32[]{:S(2)}) copy-start(f32[1536]{0:T(1024)} %param.30) | copy-start | bytes 18436
  19.6 3.3 %copy-start.9 = (f32[384]{0:T(512)S(1)}, f32[384]{0:T(512)}, u32[]{:S(2)}) copy-start(f32[384]{0:T(512)} %param.32) | copy-start | bytes 4612
  19.6 10.2 %copy-start.10 = (f32[384]{0:T(512)S(1)}, f32[384]{0:T(512)}, u32[]{:S(2)}) copy-start(f32[384]{0:T(512)} %param.35) | copy-start | bytes 4612
  19.6 10.2 %copy-start.14 = (f32[8]{0:T(128)S(1)}, f32[8]{0:T(128)}, u32[]{:S(2)}) copy-start(f32[8]{0:T(128)} %param.41) | copy-start | bytes 100
  22.8 15.3 %slice-start = ((s8[10616832]{0:T(1024)(128)(4,1)}), s8[4194304]{0:T(1024)(128)(4,1)S(1)}, s32[]{:S(2)}) async-start(s8[10616832]{0:T(1024)(128)(4,1)} %bitcast.172), calls=%async_computation | async-start | bytes 8388608
  23.0 6.8 %collective-permute-start.3 = (bf16[2,1,16,384]{3,2,1,0:T(8,128)(2,1)S(1)}, bf16[2,1,16,384]{3,2,1,0:T(8,128)(2,1)S(1)}, u32[]{:S(2)}, u32[]{:S(2)}) collective-permute-start(bf16[2,1,16,384]{3,2,1,0:T(8,128)(2,1)S(1)} %get-tuple-element.119), channel_id=1, source_target_pairs={{0,1},{1,2},{2,3},{4,5},{5,6},{6,7},{8,9},{9,10},{10,11},{12,13},{... | collective-permute-start | bytes 73736 | tf_op jit(solution)/shard_map/ppermute | solution.py:16
  28.4 4.3 %collective-permute-start.4 = (bf16[2,1,16,384]{3,2,1,0:T(8,128)(2,1)S(1)}, bf16[2,1,16,384]{3,2,1,0:T(8,128)(2,1)S(1)}, u32[]{:S(2)}, u32[]{:S(2)}) collective-permute-start(bf16[2,1,16,384]{3,2,1,0:T(8,128)(2,1)S(1)} %get-tuple-element.120), channel_id=1, source_target_pairs={{1,0},{2,1},{3,2},{5,4},{6,5},{7,6},{9,8},{10,9},{11,10},{13,12},{... | collective-permute-start | bytes 73736 | tf_op jit(solution)/shard_map/ppermute | solution.py:19
  33.0 5.2 %slice-start.1 = ((s8[10616832]{0:T(1024)(128)(4,1)}), s8[4194304]{0:T(1024)(128)(4,1)S(1)}, s32[]{:S(2)}) async-start(s8[10616832]{0:T(1024)(128)(4,1)} %bitcast.172), calls=%async_computation.1 | async-start | bytes 8388608
  35.7 2.5 %slice-start.2 = ((s8[10616832]{0:T(1024)(128)(4,1)}), s8[2228224]{0:T(1024)(128)(4,1)S(1)}, s32[]{:S(2)}) async-start(s8[10616832]{0:T(1024)(128)(4,1)} %bitcast.172), calls=%async_computation.2 | async-start | bytes 4456448
  43.2 1.0 copy-start.5
  111.5 0.9 copy-start.3
  112.5 11.3 %collective-permute-start = (f32[16,16,384]{2,1,0:T(8,128)S(1)}, f32[16,16,384]{2,1,0:T(8,128)S(1)}, u32[]{:S(2)}, u32[]{:S(2)}) collective-permute-start(f32[16,16,384]{2,1,0:T(8,128)S(1)} %multiply_add_fusion.4), channel_id=1, source_target_pairs={{0,4},{4,8},{8,12},{1,5},{5,9},{9,13},{2,6},{6,10},{10,14},{3,7},{... | collective-permute-start | bytes 1179656 | tf_op jit(solution)/shard_map/while/body/eval_jaxpr/ppermute | solution.py:27
  123.9 13.4 %collective-permute-start = (f32[16,16,384]{2,1,0:T(8,128)S(1)}, f32[16,16,384]{2,1,0:T(8,128)S(1)}, u32[]{:S(2)}, u32[]{:S(2)}) collective-permute-start(f32[16,16,384]{2,1,0:T(8,128)S(1)} %multiply_add_fusion.4), channel_id=1, source_target_pairs={{0,4},{4,8},{8,12},{1,5},{5,9},{9,13},{2,6},{6,10},{10,14},{3,7},{... | collective-permute-start | bytes 1179656 | tf_op jit(solution)/shard_map/while/body/eval_jaxpr/ppermute | solution.py:27
  137.4 13.2 %collective-permute-start = (f32[16,16,384]{2,1,0:T(8,128)S(1)}, f32[16,16,384]{2,1,0:T(8,128)S(1)}, u32[]{:S(2)}, u32[]{:S(2)}) collective-permute-start(f32[16,16,384]{2,1,0:T(8,128)S(1)} %multiply_add_fusion.4), channel_id=1, source_target_pairs={{0,4},{4,8},{8,12},{1,5},{5,9},{9,13},{2,6},{6,10},{10,14},{3,7},{... | collective-permute-start | bytes 1179656 | tf_op jit(solution)/shard_map/while/body/eval_jaxpr/ppermute | solution.py:27
  150.6 2.1 %copy-start.11 = (bf16[384,384]{1,0:T(8,128)(2,1)S(1)}, bf16[384,384]{1,0:T(8,128)(2,1)}, u32[]{:S(2)}) copy-start(bf16[384,384]{1,0:T(8,128)(2,1)} %param.37) | copy-start | bytes 884740
  150.6 2.1 %copy-start.13 = (f32[384]{0:T(512)S(1)}, f32[384]{0:T(512)}, u32[]{:S(2)}) copy-start(f32[384]{0:T(512)} %param.36) | copy-start | bytes 4612
  150.6 33.0 %copy-start.4 = (bf16[384,384]{1,0:T(8,128)(2,1)S(1)}, bf16[384,384]{1,0:T(8,128)(2,1)}, u32[]{:S(2)}) copy-start(bf16[384,384]{1,0:T(8,128)(2,1)} %param.40) | copy-start | bytes 884740
  150.6 34.6 %copy-start.1 = (bf16[1536,384]{1,0:T(8,128)(2,1)S(1)}, bf16[1536,384]{1,0:T(8,128)(2,1)}, u32[]{:S(2)}) copy-start(bf16[1536,384]{1,0:T(8,128)(2,1)} %param.31) | copy-start | bytes 3538948
where the time goes:
time: 186 us; the launch traced here: 185 us
  local copies, waits for them, and re-layouts  69.5 us (37%)
  waiting for transfers between devices  28.5 us (15%)
  blocking collectives  27.4 us (15%)
  starting transfers between devices  22.7 us (12%)
  matrix products  20.3 us (11%)
  other arithmetic  15.5 us (8%)
    ppermute x3, waiting for transfers between devices, from_behind(): return lax.ppermute(block, axis, route)  25.6 us
    unnamed x42, local copies, waits for them, and re-layouts  24.6 us
    another operation x1, local copies, waits for them, and re-layouts, cell_inputs(): split = preact.reshape(preact.shape[:-1] + (count, 4))  15.3 us
    all_gather x1, blocking collectives, body(): lax.all_gather(keys_own, 'epoch', axis=0, tiled=True)  14.3 us
    slice x1, local copies, waits for them, and re-layouts, cell_inputs(): gate_in = split[..., 0]  13.8 us
    dot_general x9, matrix products, gate_conv(): jnp.dot(window, weights[offset_y, offset_x], preferred_element_type=jnp.f...  13.4 us
    all_gather x1, blocking collectives, body(): lax.all_gather(values_own, 'epoch', axis=0, tiled=True)  13.1 us
    ppermute x3, starting transfers between devices, from_behind(): return lax.ppermute(block, axis, route)  12.3 us
  transfers between devices with their start and end apart: 7, of which 4 were waited for; matrix products, arithmetic and copies ran while one was open for 3% of the time, Pallas kernels for 0%

commit v1 on v0

v1 whole, which is shorter than its diff:
```python
import functools
import math

import jax
import jax.numpy as jnp
from jax import lax
from jax.experimental import pallas as pl
from jax.experimental.pallas import tpu as pltpu
from jax.sharding import PartitionSpec as P

PATCH = 16
REACH = 4
LANES = 128
F32 = jnp.float32
BF16 = jnp.bfloat16


def sigmoid(x):
    return 0.5 * jnp.tanh(0.5 * x) + 0.5


def softplus(x):
    return jnp.maximum(x, 0.0) + jnp.log(1.0 + jnp.exp(-jnp.abs(x)))


def gelu(x):
    inner = x * (0.7978845608028654 + (0.7978845608028654 * 0.044715) * (x * x))
    half = 0.5 * x
    return half + half * jnp.tanh(inner)


def block_kernel(
    tiles,
    frames,
    recv_pair,
    recv_next,
    valid,
    dw_kernel,
    dw_bias,
    norm_gain,
    norm_shift,
    b_expand,
    layer_scale,
    b_gates,
    forget_rate,
    w_expand_hbm,
    w_reduce_hbm,
    w_gates_hbm,
    send,
    decay0,
    inflow0,
    keep,
    block,
    open0,
    open1,
    padded,
    spread,
    taps,
    w_expand,
    w_reduce,
    w_gates,
    sems,
):
    epochs, height, width, channels = frames.shape
    groups = channels // LANES
    hidden = w_expand.shape[1]
    rows = height + 2
    pixels = height * width
    wide = 4 * LANES

    copies = [
        pltpu.make_async_copy(w_expand_hbm, w_expand, sems.at[0]),
        pltpu.make_async_copy(w_reduce_hbm, w_reduce, sems.at[1]),
    ]
    gate_copies = [
        pltpu.make_async_copy(
            w_gates_hbm.at[:, pl.ds(j * wide, wide)],
            w_gates.at[:, pl.ds(j * wide, wide)],
            sems.at[2 + j],
        )
        for j in range(groups)
    ]
    for copy in copies + gate_copies:
        copy.start()

    me = lax.axis_index("tile")
    odd = lax.rem(me, 2)
    pair_row = (1 - odd) * (height + REACH)
    next_row = odd * (height + REACH)

    for c in range(groups):
        lanes = pl.ds(c * LANES, LANES)
        for e in range(epochs):
            total_rows = height + 2 * REACH
            padded[c, e, :, 0:8, :] = jnp.zeros((total_rows, 8, LANES), F32)
            padded[c, e, :, 8 + width : 16 + width, :] = jnp.zeros((total_rows, 8, LANES), F32)
            padded[c, e, REACH : REACH + height, 8 : 8 + width, :] = frames[e, :, :, lanes].astype(F32)
            padded[c, e, pl.ds(pair_row, REACH), 8 : 8 + width, :] = recv_pair[e, :, :, lanes].astype(F32)
            padded[c, e, pl.ds(next_row, REACH), 8 : 8 + width, :] = recv_next[e, :, :, lanes].astype(F32)

    step_rows = rows // 2

    def depthwise(index, carry):
        c = index // (2 * epochs)
        rest = index - c * (2 * epochs)
        e = rest // 2
        part = rest - e * 2
        lanes = pl.ds(pl.multiple_of(c * LANES, LANES), LANES)
        start = part * step_rows
        total = [None] * step_rows
        for ox in range(7):
            factors = [dw_kernel[oy, pl.ds(ox, 1), lanes] for oy in range(7)]
            for r in range(step_rows + 6):
                window = padded[c, e, start + r, pl.ds(5 + ox, width), :]
                for oy in range(7):
                    y = r - oy
                    if 0 <= y < step_rows:
                        term = window * factors[oy]
                        total[y] = term if total[y] is None else total[y] + term
        for y in range(step_rows):
            at = pl.multiple_of((e * rows + start + y) * width, width)
            spread[pl.ds(at, width), lanes] = total[y]
        return carry

    lax.fori_loop(0, groups * epochs * 2, depthwise, 0)

    for copy in copies:
        copy.wait()

    count = rows * width
    column = lax.broadcasted_iota(jnp.int32, (count, LANES), 0)
    across = lax.rem(column, width)
    line = column // width
    first = jnp.where(me == 0, 1, 0)
    last = jnp.where(me == tiles - 1, rows - 2, rows - 1)
    inside = jnp.where((line >= first) & (line <= last), 1.0, 0.0)
    for e in range(epochs):
        values = spread[e * count : (e + 1) * count, :] + dw_bias[...]
        center = jnp.mean(values, axis=-1, keepdims=True)
        centred = values - center
        variance = jnp.mean(centred * centred, axis=-1, keepdims=True)
        normed = (centred * lax.rsqrt(variance + 1e-06) * norm_gain[...] + norm_shift[...]).astype(BF16)
        reduced = None
        for k in range(hidden // 512):
            cols = slice(k * 512, (k + 1) * 512)
            grown = jnp.dot(normed, w_expand[:, cols], preferred_element_type=F32) + b_expand[:, cols]
            part = jnp.dot(gelu(grown).astype(BF16), w_reduce[cols, :], preferred_element_type=F32)
            reduced = part if reduced is None else reduced + part
        for c in range(groups):
            lanes = slice(c * LANES, (c + 1) * LANES)
            centre = padded[c, e, REACH - 1 : REACH + height + 1, 8 : 8 + width, :].reshape(count, LANES)
            feature = centre + layer_scale[:, lanes] * reduced[:, lanes]
            feature = (feature * inside).astype(BF16).astype(F32)
            before = jnp.where(across == 0, 0.0, pltpu.roll(feature, 1, 0))
            after = jnp.where(across == width - 1, 0.0, pltpu.roll(feature, count - 1, 0))
            for ox, shifted in enumerate((before, feature, after)):
                packed = shifted.astype(BF16)
                for oy in range(3):
                    at = (oy * 3 + ox) * channels + c * LANES
                    taps[e * pixels : (e + 1) * pixels, at : at + LANES] = packed[
                        oy * width : oy * width + pixels
                    ]

    source = lax.broadcasted_iota(jnp.int32, (wide, wide), 0)
    target = lax.broadcasted_iota(jnp.int32, (wide, wide), 1)
    order = jnp.where(
        source == 4 * lax.rem(target, LANES) + target // LANES, 1.0, 0.0
    ).astype(BF16)
    good = valid[...] > 0
    for j in range(groups):
        gate_copies[j].wait()
        cols = slice(j * wide, (j + 1) * wide)
        lanes = slice(j * LANES, (j + 1) * LANES)
        preact = jnp.dot(taps[...], w_gates[:, cols], preferred_element_type=F32) + b_gates[:, cols]
        high = preact.astype(BF16)
        low = (preact - high.astype(F32)).astype(BF16)
        gates = jnp.dot(high, order, preferred_element_type=F32) + jnp.dot(
            low, order, preferred_element_type=F32
        )
        gate_in = gates[:, :LANES]
        gate_keep = gates[:, LANES : 2 * LANES]
        gate_new = gates[:, 2 * LANES : 3 * LANES]
        gate_out = gates[:, 3 * LANES :]
        decay = jnp.where(good, jnp.exp(-forget_rate[:, lanes] * softplus(gate_keep)), 1.0)
        inflow = jnp.where(good, sigmoid(gate_in) * jnp.tanh(gate_new), 0.0)
        opened = sigmoid(gate_out)
        d0, d1 = decay[:pixels], decay[pixels:]
        i0, i1 = inflow[:pixels], inflow[pixels:]
        decay0[:, lanes] = d0
        inflow0[:, lanes] = i0
        keep[:, lanes] = d0 * d1
        total = d1 * i0 + i1
        block[:, lanes] = total
        send[:, lanes] = total.astype(BF16)
        open0[:, lanes] = opened[:pixels]
        open1[:, lanes] = opened[pixels:]


def run_block(tiles, frames, recv_pair, recv_next, valid, rows, weights):
    epochs, height, width, channels = frames.shape
    w_expand, w_reduce, w_gates = weights
    pixels = height * width
    count = height + 2
    plane = jax.ShapeDtypeStruct((pixels, channels), F32)
    vmem = pl.BlockSpec(memory_space=pltpu.VMEM)
    anywhere = pl.BlockSpec(memory_space=pl.ANY)
    flops = 2 * (epochs * count * width * 2 * w_expand.size + epochs * pixels * w_gates.size)
    return pl.pallas_call(
        functools.partial(block_kernel, tiles),
        name="block",
        out_shape=[jax.ShapeDtypeStruct((pixels, channels), BF16)] + [plane] * 6,
        in_specs=[vmem] * (4 + len(rows)) + [anywhere] * 3,
        out_specs=[vmem] * 7,
        scratch_shapes=[
            pltpu.VMEM((channels // LANES, epochs, height + 2 * REACH, width + 16, LANES), F32),
            pltpu.VMEM((epochs * count * width, channels), F32),
            pltpu.VMEM((epochs * pixels, 9 * channels), BF16),
            pltpu.VMEM(w_expand.shape, BF16),
            pltpu.VMEM(w_reduce.shape, BF16),
            pltpu.VMEM(w_gates.shape, BF16),
            pltpu.SemaphoreType.DMA((2 + channels // LANES,)),
        ],
        compiler_params=pltpu.CompilerParams(vmem_limit_bytes=48 * 2**20),
        cost_estimate=pl.CostEstimate(flops=flops, bytes_accessed=2 * w_gates.size, transcendentals=0),
    )(frames, recv_pair, recv_next, valid, *rows, w_expand, w_reduce, w_gates)


def patch_tokens(first, second, gain):
    pooled = jnp.concatenate(
        [jnp.mean(first, axis=0, keepdims=True), jnp.mean(second, axis=0, keepdims=True)], axis=0
    )
    center = jnp.mean(pooled, axis=-1, keepdims=True)
    centred = pooled - center
    variance = jnp.mean(centred * centred, axis=-1, keepdims=True)
    return (centred * lax.rsqrt(variance + 1e-06) * gain).astype(BF16).astype(F32)


def memory_of(incoming, decay0, inflow0, keep, block, open0, open1):
    cell0 = decay0[...] * incoming + inflow0[...]
    cell1 = keep[...] * incoming + block[...]
    first = (open0[...] * jnp.tanh(cell0)).astype(BF16)
    second = (open1[...] * jnp.tanh(cell1)).astype(BF16)
    return first, second


def put_tokens(known, own, at):
    line = lax.broadcasted_iota(jnp.int32, known.shape, 0)
    return jnp.where(line == at, own[0:1], jnp.where(line == at + 1, own[1:2], known))


def token_kernel(stage, received, incoming, decay0, inflow0, keep, block, open0, open1, gain, known, out):
    if received:
        state = incoming[...].astype(F32)
    else:
        state = jnp.zeros(incoming.shape, F32)
    first, second = memory_of(state, decay0, inflow0, keep, block, open0, open1)
    own = patch_tokens(first.astype(F32), second.astype(F32), gain[...])
    out[...] = put_tokens(known[...].astype(F32), own, 2 * stage).astype(BF16)


def final_kernel(
    incoming,
    decay0,
    inflow0,
    keep,
    block,
    open0,
    open1,
    gain,
    known,
    days,
    slope,
    w_query,
    w_key,
    w_value,
    w_out,
    memory,
    change,
):
    pixels, channels = incoming.shape
    first, second = memory_of(incoming[...].astype(F32), decay0, inflow0, keep, block, open0, open1)
    memory[0] = first
    memory[1] = second
    own = patch_tokens(first.astype(F32), second.astype(F32), gain[...])
    stage = lax.axis_index("epoch")
    tokens = put_tokens(known[...].astype(F32), own, 2 * stage).astype(BF16)
    total = tokens.shape[0]
    heads = slope.shape[1]
    depth = channels // heads

    def project(weight):
        out = jnp.dot(tokens, weight[...], preferred_element_type=F32)
        return out.astype(BF16).astype(F32)

    queries = project(w_query)
    keys = project(w_key)
    values = project(w_value)
    line = lax.broadcasted_iota(jnp.int32, (total, channels), 0)
    member = lax.broadcasted_iota(jnp.int32, (channels, heads), 0) // depth
    head_of = jnp.where(member == lax.broadcasted_iota(jnp.int32, (channels, heads), 1), 1.0, 0.0)
    member_t = lax.broadcasted_iota(jnp.int32, (heads, channels), 1) // depth
    channel_of = jnp.where(
        member_t == lax.broadcasted_iota(jnp.int32, (heads, channels), 0), 1.0, 0.0
    )
    key_index = lax.broadcasted_iota(jnp.int32, (total, heads), 0)
    months = days[...].astype(F32) / 30.0
    results = []
    for step in range(2):
        mine = 2 * stage + step
        query = jnp.sum(jnp.where(line == mine, queries, 0.0), axis=0, keepdims=True)
        raw = jnp.dot(query * keys, head_of, preferred_element_type=F32, precision=lax.Precision.HIGHEST)
        now = jnp.sum(jnp.where(key_index == mine, months, 0.0), axis=0, keepdims=True)
        scores = raw / math.sqrt(depth) - slope[...] * (now - months)
        scores = jnp.where(key_index <= mine, scores, -1e30)
        expo = jnp.exp(scores - jnp.max(scores, axis=0, keepdims=True))
        weights = expo / jnp.sum(expo, axis=0, keepdims=True)
        spread = jnp.dot(weights, channel_of, preferred_element_type=F32, precision=lax.Precision.HIGHEST)
        results.append(jnp.sum(spread * values, axis=0, keepdims=True))
    mixed = jnp.concatenate(results, axis=0).astype(BF16)
    change[...] = jnp.dot(mixed, w_out[...], preferred_element_type=F32).astype(BF16)


def pairs(count, start):
    links = []
    for i in range(start, count - 1, 2):
        links += [(i, i + 1), (i + 1, i)]
    return links


def body(
    frames,
    valid,
    days,
    dw_kernel,
    dw_bias,
    norm_gain,
    norm_shift,
    w_expand,
    b_expand,
    w_reduce,
    layer_scale,
    w_gates,
    b_gates,
    forget_rate,
    attn_gain,
    w_query,
    w_key,
    w_value,
    w_out,
    head_slope,
):
    epochs, height, width, channels = frames.shape
    pixels = height * width
    tiles = lax.axis_size("tile")
    stages = lax.axis_size("epoch")
    total = epochs * stages
    even = lax.rem(lax.axis_index("tile"), 2) == 0
    top = frames[:, :REACH]
    bottom = frames[:, height - REACH :]
    recv_pair = lax.ppermute(jnp.where(even, bottom, top), "tile", pairs(tiles, 0))
    recv_next = lax.ppermute(jnp.where(even, top, bottom), "tile", pairs(tiles, 1))

    def row(vector):
        return vector.reshape(1, -1)

    valid_wide = jnp.broadcast_to(valid.reshape(epochs * pixels, 1), (epochs * pixels, LANES))
    send, *state = run_block(
        tiles,
        frames,
        recv_pair,
        recv_next,
        valid_wide,
        [
            dw_kernel,
            row(dw_bias),
            row(norm_gain),
            row(norm_shift),
            row(b_expand),
            row(layer_scale),
            row(b_gates),
            row(forget_rate),
        ],
        (w_expand, w_reduce, w_gates.reshape(9 * channels, -1)),
    )
    keep, block = state[2], state[3]
    gain = row(attn_gain)
    vmem = pl.BlockSpec(memory_space=pltpu.VMEM)

    def tokens(stage, received, incoming, known):
        return pl.pallas_call(
            functools.partial(token_kernel, stage, received),
            name="tokens",
            out_shape=jax.ShapeDtypeStruct((total, channels), BF16),
            in_specs=[vmem] * 9,
            out_specs=vmem,
            compiler_params=pltpu.CompilerParams(vmem_limit_bytes=16 * 2**20),
        )(incoming, *state, gain, known)

    incoming = jnp.zeros((pixels, channels), BF16)
    known = jnp.zeros((total, channels), BF16)
    if stages <= 8:
        for stage in range(stages - 1):
            link = [(stage, stage + 1)]
            if stage > 0:
                send = (keep * incoming.astype(F32) + block).astype(BF16)
            arrived = lax.ppermute(send, "epoch", link)
            told = lax.ppermute(
                tokens(stage, stage > 0, incoming if stage > 0 else send, known), "epoch", link
            )
            incoming = incoming + arrived
            known = known + told
    else:
        chain = [(i, i + 1) for i in range(stages - 1)]

        def turn(_, arriving):
            out = (keep * arriving.astype(F32) + block).astype(BF16)
            return lax.ppermute(out, "epoch", chain)

        incoming = lax.fori_loop(0, stages - 1, turn, incoming)
        own = tokens(0, True, incoming, known)[:epochs]
        known = lax.all_gather(own, "epoch", axis=0, tiled=True)

    memory, change = pl.pallas_call(
        final_kernel,
        name="final",
        out_shape=[
            jax.ShapeDtypeStruct((epochs, pixels, channels), BF16),
            jax.ShapeDtypeStruct((epochs, channels), BF16),
        ],
        in_specs=[vmem] * 15,
        out_specs=[vmem] * 2,
        compiler_params=pltpu.CompilerParams(vmem_limit_bytes=24 * 2**20),
    )(
        incoming,
        *state,
        gain,
        known,
        days.reshape(-1, 1),
        row(head_slope),
        w_query,
        w_key,
        w_value,
        w_out,
    )
    return (
        memory.reshape(epochs, height, width, channels),
        change.reshape(epochs, 1, 1, channels),
    )


def solution(mesh):
    placed = (
        P("epoch", ("groups", "tile"), None, None),
        P("epoch", ("groups", "tile"), None),
        P("groups"),
    ) + (P(),) * 17
    return jax.shard_map(
        body,
        mesh=mesh,
        in_specs=placed,
        out_specs=(
            P("epoch", ("groups", "tile"), None, None),
            P("epoch", ("groups", "tile"), None, None),
        ),
        check_vma=False,
    )
```

time: 186 us -> 62.5 us (0.34)
  the two profiles are of different devices: /device:TPU:0 before, /device:TPU:30 now
where the time goes in v1:
time: 62.5 us; the launch traced here: 61.7 us
  waiting for transfers between devices  20.1 us (32%)
  Pallas kernels  18.9 us (30%)
  local copies, waits for them, and re-layouts  11.2 us (18%)
  starting transfers between devices  7.82 us (13%)
  other arithmetic  2.78 us (4%)
  between operations  0.91 us (1%)
    ppermute x3, waiting for transfers between devices, body(): lax.ppermute(tokens(stage, stage > 0, incoming if stage > 0 else send, kn...  20.1 us
    pallas_call x1, Pallas kernels, run_block(): pl.pallas_call(functools.partial(block_kernel, tiles), name='block', out_...  15.4 us
    unnamed x22, local copies, waits for them, and re-layouts  5.42 us
    reshape x8, local copies, waits for them, and re-layouts, row(): return vector.reshape(1, -1)  4.82 us
    ppermute x3, starting transfers between devices, body(): arrived = lax.ppermute(send, 'epoch', link)  2.63 us
    ppermute x3, starting transfers between devices, body(): lax.ppermute(tokens(stage, stage > 0, incoming if stage > 0 else send, kn...  2.59 us
    ppermute x1, starting transfers between devices, body(): lax.ppermute(jnp.where(even, top, bottom), 'tile', pairs(tiles, 1))  2.53 us
    pallas_call x1, Pallas kernels, body(): pl.pallas_call(final_kernel, name='final', out_shape=[jax.ShapeDtypeStruc...  2.15 us
  transfers between devices with their start and end apart: 8, of which 1 were waited for; matrix products, arithmetic and copies ran while one was open for 9% of the time, Pallas kernels for 2%

profile of v1, /device:TPU:30, one launch (start us, length us, event | category | flops | bytes accessed | tf_op | source)
XLA Modules:
  0.0 61.7 jit_solution(5041995020302582868)
XLA Ops:
  0.6 1.0 %broadcast_select_fusion = (bf16[2,4,16,384]{3,2,1,0:T(8,128)(2,1)S(1)}, bf16[2,4,16,384]{3,2,1,0:T(8,128)(2,1)S(1)}) fusion(pred[]{:T(512)S(6)} %eq.3, bf16[2,16,16,384]{3,2,1,0:T(8,128)(2,1)} %frames.1), kind=kLoop, calls=%fused_computation.2 | loop fusion | flops 98304 | bytes 393217 | tf_op jit(solution)/shard_map/jit(_where)/select_n | solution.py:361
  1.6 0.1 collective-permute-start
  1.7 2.5 %collective-permute-start.1 = (bf16[2,4,16,384]{3,2,1,0:T(8,128)(2,1)S(1)}, bf16[2,4,16,384]{3,2,1,0:T(8,128)(2,1)S(1)}, u32[]{:S(2)}, u32[]{:S(2)}) collective-permute-start(bf16[2,4,16,384]{3,2,1,0:T(8,128)(2,1)S(1)} %get-tuple-element.22), channel_id=1, source_target_pairs={{1,2},{2,1},{5,6},{6,5},{9,10},{10,9},{13,14},{14,13},{17,18},{18,... | collective-permute-start | bytes 294920 | tf_op jit(solution)/shard_map/ppermute | solution.py:361
  4.2 0.8 %broadcast_in_dim.10 = s32[512]{0:T(512)S(1)} reshape(s32[2,16,16]{2,1,0:T(8,128)} %param.21) | data formatting | bytes 4096 | tf_op jit(solution)/shard_map/broadcast_in_dim | solution.py:366
  5.0 0.7 %reshape.48.b_expand = f32[1,1536]{1,0:T(1,128)S(1)} reshape(f32[1536]{0:T(1024)} %param.28) | data formatting | bytes 12288 | tf_op jit(solution)/shard_map/reshape | solution.py:364
  5.7 0.7 %reshape.50.b_gates = f32[1,1536]{1,0:T(1,128)S(1)} reshape(f32[1536]{0:T(1024)} %param.32) | data formatting | bytes 12288 | tf_op jit(solution)/shard_map/reshape | solution.py:364
  6.4 0.7 %reshape.45.dw_bias = f32[1,384]{1,0:T(1,128)S(1)} reshape(f32[384]{0:T(512)} %param.24) | data formatting | bytes 3072 | tf_op jit(solution)/shard_map/reshape | solution.py:364
  7.1 0.7 %reshape.46.norm_gain = f32[1,384]{1,0:T(1,128)S(1)} reshape(f32[384]{0:T(512)} %param.25) | data formatting | bytes 3072 | tf_op jit(solution)/shard_map/reshape | solution.py:364
  7.8 0.7 %reshape.47.norm_shift = f32[1,384]{1,0:T(1,128)S(1)} reshape(f32[384]{0:T(512)} %param.26) | data formatting | bytes 3072 | tf_op jit(solution)/shard_map/reshape | solution.py:364
  8.5 0.7 %reshape.49.layer_scale = f32[1,384]{1,0:T(1,128)S(1)} reshape(f32[384]{0:T(512)} %param.30) | data formatting | bytes 3072 | tf_op jit(solution)/shard_map/reshape | solution.py:364
  9.2 0.7 %reshape.51.forget_rate = f32[1,384]{1,0:T(1,128)S(1)} reshape(f32[384]{0:T(512)} %param.33) | data formatting | bytes 3072 | tf_op jit(solution)/shard_map/reshape | solution.py:364
  9.9 0.1 broadcast_in_dim.11.valid
  10.0 1.0 %copy-done.4 = bf16[2,16,16,384]{3,2,1,0:T(8,128)(2,1)S(1)} copy-done((bf16[2,16,16,384]{3,2,1,0:T(8,128)(2,1)S(1)}, bf16[2,16,16,384]{3,2,1,0:T(8,128)(2,1)}, u32[]{:S(2)}) %copy-start.4) | copy-done | bytes 393240
  11.0 1.3 %copy-done.6 = bf16[384,1536]{1,0:T(8,128)(2,1)S(1)} copy-done((bf16[384,1536]{1,0:T(8,128)(2,1)S(1)}, bf16[384,1536]{1,0:T(8,128)(2,1)}, u32[]{:S(2)}) %copy-start.6) | copy-done | bytes 1179672
  12.3 1.3 %copy-done.7 = bf16[1536,384]{1,0:T(8,128)(2,1)S(1)} copy-done((bf16[1536,384]{1,0:T(8,128)(2,1)S(1)}, bf16[1536,384]{1,0:T(8,128)(2,1)}, u32[]{:S(2)}) %copy-start.7) | copy-done | bytes 1179672
  13.5 0.9 %copy-done.8 = f32[7,7,384]{2,1,0:T(8,128)S(1)} copy-done((f32[7,7,384]{2,1,0:T(8,128)S(1)}, f32[7,7,384]{2,1,0:T(8,128)}, u32[]{:S(2)}) %copy-start.8) | copy-done | bytes 75288
  14.4 15.4 %block.1 = (bf16[256,384]{1,0:T(8,128)(2,1)S(1)}, f32[256,384]{1,0:T(8,128)S(1)}, f32[256,384]{1,0:T(8,128)S(1)}, f32[256,384]{1,0:T(8,128)S(1)}, f32[256,384]{1...) custom-call(bf16[2,16,16,384]{3,2,1,0:T(8,128)(2,1)S(1)} %copy-done.4, ...), custom_call_target="tpu_custom_call" | custom-call | flops 6794772480 | bytes 10616832 | tf_op jit(solution)/shard_map/block/pallas_call | solution.py:208
  29.8 0.7 %collective-permute-start.2 = (bf16[256,384]{1,0:T(8,128)(2,1)S(1)}, bf16[256,384]{1,0:T(8,128)(2,1)S(1)}, u32[]{:S(2)}, u32[]{:S(2)}) collective-permute-start(bf16[256,384]{1,0:T(8,128)(2,1)S(1)} %get-tuple-element.11.incoming), channel_id=1, source_target_pairs={{0,4},{1,5},{2,6},{3,7},{16,20},{17,21},{18,22},{19,23}} | collective-permute-start | bytes 589832 | tf_op jit(solution)/shard_map/ppermute | solution.py:406
  30.6 0.7 %collective-permute-start.3 = (bf16[256,384]{1,0:T(8,128)(2,1)S(1)}, bf16[256,384]{1,0:T(8,128)(2,1)S(1)}, u32[]{:S(2)}, u32[]{:S(2)}) collective-permute-start(bf16[256,384]{1,0:T(8,128)(2,1)S(1)} %add_convert_fusion.1), channel_id=1, source_target_pairs={{4,8},{5,9},{6,10},{7,11},{20,24},{21,25},{22,26},{23,27}} | collective-permute-start | bytes 589832 | tf_op jit(solution)/shard_map/ppermute | solution.py:406
  31.3 0.8 %add_convert_fusion = (bf16[256,384]{1,0:T(8,128)(2,1)}, bf16[256,384]{1,0:T(8,128)(2,1)S(1)}) fusion(f32[256,384]{1,0:T(8,128)S(1)} %get-tuple-element.13.block, f32[256,384]{1,0:T(8,128)S(1)} %get-tuple-element.12.keep, bf16[256,384]{1,0:T(8,128)(2,1)S(1)} %collective-permute-done.2.incoming, bf16[256,384]{1,0:T(8,128)(2,1)S(1)} %collective-permute-done.3), kind=kLoop, calls=%fused_computation | loop fusion | flops 491520 | bytes 1572864 | tf_op jit(solution)/shard_map/convert_element_type | solution.py:405
  32.0 1.3 %collective-permute-start.4 = (bf16[256,384]{1,0:T(8,128)(2,1)}, bf16[256,384]{1,0:T(8,128)(2,1)}, u32[]{:S(2)}, u32[]{:S(2)}) collective-permute-start(bf16[256,384]{1,0:T(8,128)(2,1)} %get-tuple-element.20), channel_id=1, source_target_pairs={{8,12},{9,13},{10,14},{11,15},{24,28},{25,29},{26,30},{27,31}} | collective-permute-start | bytes 589832 | tf_op jit(solution)/shard_map/ppermute | solution.py:406
  33.3 0.4 tokens.3
  33.8 0.7 %collective-permute-start.5 = (bf16[8,384]{1,0:T(8,128)(2,1)S(1)}, bf16[8,384]{1,0:T(8,128)(2,1)S(1)}, u32[]{:S(2)}, u32[]{:S(2)}) collective-permute-start(bf16[8,384]{1,0:T(8,128)(2,1)S(1)} %tokens.3), channel_id=1, source_target_pairs={{0,4},{1,5},{2,6},{3,7},{16,20},{17,21},{18,22},{19,23}} | collective-permute-start | bytes 18440 | tf_op jit(solution)/shard_map/ppermute | solution.py:407
  34.5 0.5 tokens.4
  34.9 0.7 %collective-permute-start.6 = (bf16[8,384]{1,0:T(8,128)(2,1)S(1)}, bf16[8,384]{1,0:T(8,128)(2,1)S(1)}, u32[]{:S(2)}, u32[]{:S(2)}) collective-permute-start(bf16[8,384]{1,0:T(8,128)(2,1)S(1)} %tokens.4), channel_id=1, source_target_pairs={{4,8},{5,9},{6,10},{7,11},{20,24},{21,25},{22,26},{23,27}} | collective-permute-start | bytes 18440 | tf_op jit(solution)/shard_map/ppermute | solution.py:407
  35.7 0.5 tokens.5
  36.1 1.3 %collective-permute-start.7 = (bf16[8,384]{1,0:T(8,128)(2,1)S(1)}, bf16[8,384]{1,0:T(8,128)(2,1)S(1)}, u32[]{:S(2)}, u32[]{:S(2)}) collective-permute-start(bf16[8,384]{1,0:T(8,128)(2,1)S(1)} %tokens.5), channel_id=1, source_target_pairs={{8,12},{9,13},{10,14},{11,15},{24,28},{25,29},{26,30},{27,31}} | collective-permute-start | bytes 18440 | tf_op jit(solution)/shard_map/ppermute | solution.py:407
  37.4 0.1 copy.22.days
  37.5 20.1 %collective-permute-done.7 = bf16[8,384]{1,0:T(8,128)(2,1)S(1)} collective-permute-done((bf16[8,384]{1,0:T(8,128)(2,1)S(1)}, bf16[8,384]{1,0:T(8,128)(2,1)S(1)}, u32[]{:S(2)}, u32[]{:S(2)}) %collective-permute-start.7) | collective-permute-done | bytes 6176 | tf_op jit(solution)/shard_map/ppermute | solution.py:407
  57.6 1.0 %add.21.incoming = bf16[256,384]{1,0:T(8,128)(2,1)S(1)} add(bf16[256,384]{1,0:T(8,128)(2,1)S(1)} %get-tuple-element.21.incoming, bf16[256,384]{1,0:T(8,128)(2,1)} %collective-permute-done.4) | non-fusion elementwise | flops 98304 | bytes 589824 | tf_op jit(solution)/shard_map/add | solution.py:410
  58.6 1.0 %copy-done.3 = bf16[384,384]{1,0:T(8,128)(2,1)S(1)} copy-done((bf16[384,384]{1,0:T(8,128)(2,1)S(1)}, bf16[384,384]{1,0:T(8,128)(2,1)}, u32[]{:S(2)}) %copy-start.3) | copy-done | bytes 294936
  59.6 2.2 %final.1 = (bf16[2,256,384]{2,1,0:T(8,128)(2,1)}, bf16[2,384]{1,0:T(2,128)(2,1)}) custom-call(bf16[256,384]{1,0:T(8,128)(2,1)S(1)} %add.21.incoming, f32[256,384]{1,0:T(8,128)S(1)} %get-tuple-element.14.decay0, f32[256,384]{1,0:T(8,128)S(1)} %get-tuple-element.15.inflow0, f32[256,384]{1,0:T(8,128)S(1)} %get-tuple-element.12.keep, ...), custom_call_target="tpu_custom_call" | custom-call | tf_op jit(solution)/shard_map/final/pallas_call | solution.py:423
  (29 shorter events, 0.1 us)
Async XLA Ops:
  1.6 8.2 %collective-permute-start = (bf16[2,4,16,384]{3,2,1,0:T(8,128)(2,1)S(1)}, bf16[2,4,16,384]{3,2,1,0:T(8,128)(2,1)S(1)}, u32[]{:S(2)}, u32[]{:S(2)}) collective-permute-start(bf16[2,4,16,384]{3,2,1,0:T(8,128)(2,1)S(1)} %get-tuple-element.23), channel_id=1, source_target_pairs={{0,1},{1,0},{2,3},{3,2},{4,5},{5,4},{6,7},{7,6},{8,9},{9,8},{10,11... | collective-permute-start | bytes 294920 | tf_op jit(solution)/shard_map/ppermute | solution.py:360
  1.7 8.2 %collective-permute-start.1 = (bf16[2,4,16,384]{3,2,1,0:T(8,128)(2,1)S(1)}, bf16[2,4,16,384]{3,2,1,0:T(8,128)(2,1)S(1)}, u32[]{:S(2)}, u32[]{:S(2)}) collective-permute-start(bf16[2,4,16,384]{3,2,1,0:T(8,128)(2,1)S(1)} %get-tuple-element.22), channel_id=1, source_target_pairs={{1,2},{2,1},{5,6},{6,5},{9,10},{10,9},{13,14},{14,13},{17,18},{18,... | collective-permute-start | bytes 294920 | tf_op jit(solution)/shard_map/ppermute | solution.py:361
  10.0 1.0 %copy-start.4 = (bf16[2,16,16,384]{3,2,1,0:T(8,128)(2,1)S(1)}, bf16[2,16,16,384]{3,2,1,0:T(8,128)(2,1)}, u32[]{:S(2)}) copy-start(bf16[2,16,16,384]{3,2,1,0:T(8,128)(2,1)} %frames.1) | copy-start | bytes 1179652
  11.0 1.3 %copy-start.6 = (bf16[384,1536]{1,0:T(8,128)(2,1)S(1)}, bf16[384,1536]{1,0:T(8,128)(2,1)}, u32[]{:S(2)}) copy-start(bf16[384,1536]{1,0:T(8,128)(2,1)} %w_expand_hbm.1) | copy-start | bytes 3538948
  12.3 1.3 %copy-start.7 = (bf16[1536,384]{1,0:T(8,128)(2,1)S(1)}, bf16[1536,384]{1,0:T(8,128)(2,1)}, u32[]{:S(2)}) copy-start(bf16[1536,384]{1,0:T(8,128)(2,1)} %w_reduce_hbm.1) | copy-start | bytes 3538948
  13.5 0.9 %copy-start.8 = (f32[7,7,384]{2,1,0:T(8,128)S(1)}, f32[7,7,384]{2,1,0:T(8,128)}, u32[]{:S(2)}) copy-start(f32[7,7,384]{2,1,0:T(8,128)} %dw_kernel.1) | copy-start | bytes 225796
  29.8 0.7 %collective-permute-start.2 = (bf16[256,384]{1,0:T(8,128)(2,1)S(1)}, bf16[256,384]{1,0:T(8,128)(2,1)S(1)}, u32[]{:S(2)}, u32[]{:S(2)}) collective-permute-start(bf16[256,384]{1,0:T(8,128)(2,1)S(1)} %get-tuple-element.11.incoming), channel_id=1, source_target_pairs={{0,4},{1,5},{2,6},{3,7},{16,20},{17,21},{18,22},{19,23}} | collective-permute-start | bytes 589832 | tf_op jit(solution)/shard_map/ppermute | solution.py:406
  30.5 2.8 %copy-start.9 = (f32[384]{0:T(512)S(1)}, f32[384]{0:T(512)}, u32[]{:S(2)}) copy-start(f32[384]{0:T(512)} %param.34) | copy-start | bytes 4612
  30.6 0.7 %collective-permute-start.3 = (bf16[256,384]{1,0:T(8,128)(2,1)S(1)}, bf16[256,384]{1,0:T(8,128)(2,1)S(1)}, u32[]{:S(2)}, u32[]{:S(2)}) collective-permute-start(bf16[256,384]{1,0:T(8,128)(2,1)S(1)} %add_convert_fusion.1), channel_id=1, source_target_pairs={{4,8},{5,9},{6,10},{7,11},{20,24},{21,25},{22,26},{23,27}} | collective-permute-start | bytes 589832 | tf_op jit(solution)/shard_map/ppermute | solution.py:406
  32.0 25.6 %collective-permute-start.4 = (bf16[256,384]{1,0:T(8,128)(2,1)}, bf16[256,384]{1,0:T(8,128)(2,1)}, u32[]{:S(2)}, u32[]{:S(2)}) collective-permute-start(bf16[256,384]{1,0:T(8,128)(2,1)} %get-tuple-element.20), channel_id=1, source_target_pairs={{8,12},{9,13},{10,14},{11,15},{24,28},{25,29},{26,30},{27,31}} | collective-permute-start | bytes 589832 | tf_op jit(solution)/shard_map/ppermute | solution.py:406
  33.8 0.7 %collective-permute-start.5 = (bf16[8,384]{1,0:T(8,128)(2,1)S(1)}, bf16[8,384]{1,0:T(8,128)(2,1)S(1)}, u32[]{:S(2)}, u32[]{:S(2)}) collective-permute-start(bf16[8,384]{1,0:T(8,128)(2,1)S(1)} %tokens.3), channel_id=1, source_target_pairs={{0,4},{1,5},{2,6},{3,7},{16,20},{17,21},{18,22},{19,23}} | collective-permute-start | bytes 18440 | tf_op jit(solution)/shard_map/ppermute | solution.py:407
  34.9 0.7 %collective-permute-start.6 = (bf16[8,384]{1,0:T(8,128)(2,1)S(1)}, bf16[8,384]{1,0:T(8,128)(2,1)S(1)}, u32[]{:S(2)}, u32[]{:S(2)}) collective-permute-start(bf16[8,384]{1,0:T(8,128)(2,1)S(1)} %tokens.4), channel_id=1, source_target_pairs={{4,8},{5,9},{6,10},{7,11},{20,24},{21,25},{22,26},{23,27}} | collective-permute-start | bytes 18440 | tf_op jit(solution)/shard_map/ppermute | solution.py:407
  35.6 1.8 %copy-start.10 = (s32[8]{0:T(128)S(1)}, s32[8]{0:T(128)}, u32[]{:S(2)}) copy-start(s32[8]{0:T(128)} %param.22) | copy-start | bytes 100
  35.6 23.0 %copy-start = (bf16[384,384]{1,0:T(8,128)(2,1)S(1)}, bf16[384,384]{1,0:T(8,128)(2,1)}, u32[]{:S(2)}) copy-start(bf16[384,384]{1,0:T(8,128)(2,1)} %w_query.1) | copy-start | bytes 884740
  35.6 23.0 %copy-start.1 = (bf16[384,384]{1,0:T(8,128)(2,1)S(1)}, bf16[384,384]{1,0:T(8,128)(2,1)}, u32[]{:S(2)}) copy-start(bf16[384,384]{1,0:T(8,128)(2,1)} %w_key.1) | copy-start | bytes 884740
  35.6 23.0 %copy-start.2 = (bf16[384,384]{1,0:T(8,128)(2,1)S(1)}, bf16[384,384]{1,0:T(8,128)(2,1)}, u32[]{:S(2)}) copy-start(bf16[384,384]{1,0:T(8,128)(2,1)} %w_value.1) | copy-start | bytes 884740
  35.7 23.0 %copy-start.5 = (f32[8]{0:T(128)S(1)}, f32[8]{0:T(128)}, u32[]{:S(2)}) copy-start(f32[8]{0:T(128)} %param.39) | copy-start | bytes 100
  36.1 21.5 %collective-permute-start.7 = (bf16[8,384]{1,0:T(8,128)(2,1)S(1)}, bf16[8,384]{1,0:T(8,128)(2,1)S(1)}, u32[]{:S(2)}, u32[]{:S(2)}) collective-permute-start(bf16[8,384]{1,0:T(8,128)(2,1)S(1)} %tokens.5), channel_id=1, source_target_pairs={{8,12},{9,13},{10,14},{11,15},{24,28},{25,29},{26,30},{27,31}} | collective-permute-start | bytes 18440 | tf_op jit(solution)/shard_map/ppermute | solution.py:407
  58.6 1.0 %copy-start.3 = (bf16[384,384]{1,0:T(8,128)(2,1)S(1)}, bf16[384,384]{1,0:T(8,128)(2,1)}, u32[]{:S(2)}) copy-start(bf16[384,384]{1,0:T(8,128)(2,1)} %w_out.1) | copy-start | bytes 884740

commit v2 on v1

v2 whole, which is shorter than its diff:
```python
import functools
import math

import jax
import jax.numpy as jnp
from jax import lax
from jax.experimental import pallas as pl
from jax.experimental.pallas import tpu as pltpu
from jax.sharding import PartitionSpec as P

PATCH = 16
REACH = 4
LANES = 128
F32 = jnp.float32
BF16 = jnp.bfloat16


def sigmoid(x):
    return 0.5 * jnp.tanh(0.5 * x) + 0.5


def softplus(x):
    return jnp.maximum(x, 0.0) + jnp.log(1.0 + jnp.exp(-jnp.abs(x)))


def gelu(x):
    inner = x * (0.7978845608028654 + (0.7978845608028654 * 0.044715) * (x * x))
    half = 0.5 * x
    return half + half * jnp.tanh(inner)


def stage_kernel(
    frames_hbm,
    valid_hbm,
    days_hbm,
    dw_hbm,
    dw_bias_hbm,
    norm_gain_hbm,
    norm_shift_hbm,
    b_expand_hbm,
    layer_scale_hbm,
    b_gates_hbm,
    forget_rate_hbm,
    attn_gain_hbm,
    head_slope_hbm,
    w_expand_hbm,
    w_reduce_hbm,
    w_query_hbm,
    w_key_hbm,
    w_value_hbm,
    w_out_hbm,
    spread,
    mask,
    short_rows,
    long_rows,
    months,
    slope,
    frames,
    dw_kernel,
    w_expand,
    w_reduce,
    w_qkv,
    w_out,
    padded,
    valid,
    days,
    slope_line,
    short_lines,
    long_lines,
    sems,
):
    epochs, height, width, channels = frames.shape
    groups = channels // LANES
    rows = height + 2
    pixels = height * width
    moves = [
        (frames_hbm, frames),
        (dw_hbm, dw_kernel),
        (valid_hbm, valid),
        (days_hbm, days),
        (head_slope_hbm, slope_line),
        (b_expand_hbm, long_lines[0]),
        (b_gates_hbm, long_lines[1]),
        (dw_bias_hbm, short_lines[0]),
        (norm_gain_hbm, short_lines[1]),
        (norm_shift_hbm, short_lines[2]),
        (layer_scale_hbm, short_lines[3]),
        (forget_rate_hbm, short_lines[4]),
        (attn_gain_hbm, short_lines[5]),
        (w_expand_hbm, w_expand),
        (w_reduce_hbm, w_reduce),
        (w_query_hbm, w_qkv.at[:, pl.ds(0, channels)]),
        (w_key_hbm, w_qkv.at[:, pl.ds(channels, channels)]),
        (w_value_hbm, w_qkv.at[:, pl.ds(2 * channels, channels)]),
        (w_out_hbm, w_out),
    ]
    copies = [pltpu.make_async_copy(a, b, sems.at[i]) for i, (a, b) in enumerate(moves)]
    for copy in copies:
        copy.start()

    for c in range(groups):
        for e in range(epochs):
            padded[c, e, :, 0:8, :] = jnp.zeros((height, 8, LANES), F32)
            padded[c, e, :, 8 + width : 16 + width, :] = jnp.zeros((height, 8, LANES), F32)
    copies[0].wait()
    for c in range(groups):
        for e in range(epochs):
            lanes = slice(c * LANES, (c + 1) * LANES)
            padded[c, e, :, 8 : 8 + width, :] = frames[e, :, :, lanes].astype(F32)
    copies[1].wait()

    half = rows // 2

    def depthwise(index, carry):
        c = index // epochs
        e = index - c * epochs
        lanes = pl.ds(pl.multiple_of(c * LANES, LANES), LANES)
        for part in range(2):
            total = [None] * half
            for ox in range(7):
                factors = [dw_kernel[oy, pl.ds(ox, 1), lanes] for oy in range(7)]
                for r in range(height):
                    at = [(y, r + REACH - (part * half + y)) for y in range(half)]
                    at = [(y, oy) for y, oy in at if 0 <= oy < 7]
                    if not at:
                        continue
                    window = padded[c, e, r, pl.ds(5 + ox, width), :]
                    for y, oy in at:
                        term = window * factors[oy]
                        total[y] = term if total[y] is None else total[y] + term
            for y in range(half):
                line = (part * half + y) * width
                spread[e, pl.ds(line, width), lanes] = total[y]
        return carry

    lax.fori_loop(0, groups * epochs, depthwise, 0)

    for copy in copies[2:]:
        copy.wait()
    for k in range(6):
        short_rows[k : k + 1, :] = short_lines[k][...].reshape(1, -1)
    for k in range(2):
        long_rows[k : k + 1, :] = long_lines[k][...].reshape(1, -1)
    slope[...] = slope_line[...].reshape(1, -1)
    total = days.shape[0]
    eye = lax.broadcasted_iota(jnp.int32, (total, total), 0) == lax.broadcasted_iota(
        jnp.int32, (total, total), 1
    )
    month = days[...].astype(F32).reshape(1, -1) / 30.0
    months[...] = jnp.broadcast_to(
        jnp.sum(jnp.where(eye, month, 0.0), axis=1, keepdims=True), months.shape
    )
    down = lax.broadcasted_iota(jnp.int32, (pixels, height), 0) // width
    pick = jnp.where(down == lax.broadcasted_iota(jnp.int32, (pixels, height), 1), 1.0, 0.0).astype(BF16)
    side = lax.rem(lax.broadcasted_iota(jnp.int32, (pixels, width), 0), width)
    place = side == lax.broadcasted_iota(jnp.int32, (pixels, width), 1)
    ones = jnp.ones((width, LANES), BF16)
    for e in range(epochs):
        plane = jnp.where(valid[e] > 0, 1.0, 0.0).astype(BF16)
        lines = jnp.dot(pick, plane, preferred_element_type=F32)
        mask[e * pixels : (e + 1) * pixels, :] = jnp.dot(
            jnp.where(place, lines, 0.0).astype(BF16), ones, preferred_element_type=F32
        )


def run_stage(frames, valid, days, dw_kernel, short, long, slope, w_expand, w_reduce, w_qkvo):
    epochs, height, width, channels = frames.shape
    pixels = height * width
    total = days.shape[0]
    operands = [frames, valid, days, dw_kernel]
    operands += [short[0], short[1], short[2], long[0], short[3], long[1], short[4], short[5], slope]
    operands += [w_expand, w_reduce, *w_qkvo]
    hbm = pl.BlockSpec(memory_space=pltpu.HBM)
    vmem = pl.BlockSpec(memory_space=pltpu.VMEM)
    out_shape = [
        jax.ShapeDtypeStruct((epochs, (height + 2) * width, channels), F32),
        jax.ShapeDtypeStruct((epochs * pixels, LANES), F32),
        jax.ShapeDtypeStruct((8, channels), F32),
        jax.ShapeDtypeStruct((8, long[0].size), F32),
        jax.ShapeDtypeStruct((total, LANES), F32),
        jax.ShapeDtypeStruct((1, slope.size), F32),
        jax.ShapeDtypeStruct(frames.shape, BF16),
        jax.ShapeDtypeStruct(dw_kernel.shape, F32),
        jax.ShapeDtypeStruct(w_expand.shape, BF16),
        jax.ShapeDtypeStruct(w_reduce.shape, BF16),
        jax.ShapeDtypeStruct((channels, 3 * channels), BF16),
        jax.ShapeDtypeStruct((channels, channels), BF16),
    ]
    return pl.pallas_call(
        stage_kernel,
        name="stage",
        out_shape=out_shape,
        in_specs=[hbm] * len(operands),
        out_specs=[vmem] * len(out_shape),
        scratch_shapes=[
            pltpu.VMEM((channels // LANES, epochs, height, width + 16, LANES), F32),
            pltpu.VMEM(valid.shape, jnp.int32),
            pltpu.VMEM(days.shape, jnp.int32),
            pltpu.VMEM(slope.shape, F32),
            [pltpu.VMEM((channels,), F32)] * 6,
            [pltpu.VMEM((long[0].size,), F32)] * 2,
            pltpu.SemaphoreType.DMA((len(operands),)),
        ],
        compiler_params=pltpu.CompilerParams(vmem_limit_bytes=24 * 2**20),
        cost_estimate=pl.CostEstimate(
            flops=10**10, bytes_accessed=8 * w_expand.size, transcendentals=0
        ),
    )(*operands)


def block_kernel(
    tiles,
    spread,
    recv_pair,
    recv_next,
    frames,
    mask,
    short_rows,
    long_rows,
    dw_kernel,
    w_expand,
    w_reduce,
    w_gates_hbm,
    send,
    decay0,
    inflow0,
    keep,
    block,
    open0,
    open1,
    rim,
    edge,
    taps,
    w_gates,
    sems,
):
    epochs, height, width, channels = frames.shape
    groups = channels // LANES
    hidden = w_expand.shape[1]
    rows = height + 2
    pixels = height * width
    wide = 4 * LANES

    gate_copies = [
        pltpu.make_async_copy(
            w_gates_hbm.at[:, pl.ds(j * wide, wide)],
            w_gates.at[:, pl.ds(j * wide, wide)],
            sems.at[j],
        )
        for j in range(groups)
    ]
    for copy in gate_copies:
        copy.start()

    dw_bias = short_rows[0:1, :]
    norm_gain = short_rows[1:2, :]
    norm_shift = short_rows[2:3, :]
    layer_scale = short_rows[3:4, :]
    forget_rate = short_rows[4:5, :]
    attn_gain = short_rows[5:6, :]
    b_expand = long_rows[0:1, :]
    b_gates = long_rows[1:2, :]

    me = lax.axis_index("tile")
    odd = lax.rem(me, 2)
    pair_row = (1 - odd) * REACH
    next_row = odd * REACH

    for c in range(groups):
        lanes = slice(c * LANES, (c + 1) * LANES)
        for e in range(epochs):
            rim[c, e, :, 0:8, :] = jnp.zeros((2 * REACH, 8, LANES), F32)
            rim[c, e, :, 8 + width : 16 + width, :] = jnp.zeros((2 * REACH, 8, LANES), F32)
            rim[c, e, pl.ds(pair_row, REACH), 8 : 8 + width, :] = recv_pair[e, :, :, lanes].astype(F32)
            rim[c, e, pl.ds(next_row, REACH), 8 : 8 + width, :] = recv_next[e, :, :, lanes].astype(F32)

    def depthwise(index, carry):
        c = index // epochs
        e = index - c * epochs
        lanes = pl.ds(pl.multiple_of(c * LANES, LANES), LANES)
        total = [None] * (2 * REACH)
        for ox in range(7):
            factors = [dw_kernel[oy, pl.ds(ox, 1), lanes] for oy in range(7)]
            for k in range(REACH):
                above = rim[c, e, k, pl.ds(5 + ox, width), :]
                below = rim[c, e, REACH + k, pl.ds(5 + ox, width), :]
                for y in range(k + 1):
                    term = above * factors[k - y]
                    total[y] = term if total[y] is None else total[y] + term
                for y in range(k, REACH):
                    term = below * factors[6 + k - y]
                    at = REACH + y
                    total[at] = term if total[at] is None else total[at] + term
        for y in range(2 * REACH):
            edge[e, pl.ds(y * width, width), lanes] = total[y]
        return carry

    lax.fori_loop(0, groups * epochs, depthwise, 0)

    count = rows * width
    rimmed = REACH * width
    column = lax.broadcasted_iota(jnp.int32, (count, LANES), 0)
    across = lax.rem(column, width)
    line = column // width
    first = jnp.where(me == 0, 1, 0)
    last = jnp.where(me == tiles - 1, rows - 2, rows - 1)
    inside = jnp.where((line >= first) & (line <= last), 1.0, 0.0)
    for e in range(epochs):
        values = (
            jnp.concatenate(
                [
                    spread[e, :rimmed] + edge[e, :rimmed],
                    spread[e, rimmed : count - rimmed],
                    spread[e, count - rimmed :] + edge[e, rimmed:],
                ],
                axis=0,
            )
            + dw_bias
        )
        center = jnp.mean(values, axis=-1, keepdims=True)
        centred = values - center
        variance = jnp.mean(centred * centred, axis=-1, keepdims=True)
        normed = (centred * lax.rsqrt(variance + 1e-06) * norm_gain + norm_shift).astype(BF16)
        reduced = None
        for k in range(hidden // 512):
            cols = slice(k * 512, (k + 1) * 512)
            grown = jnp.dot(normed, w_expand[:, cols], preferred_element_type=F32) + b_expand[:, cols]
            part = jnp.dot(gelu(grown).astype(BF16), w_reduce[cols, :], preferred_element_type=F32)
            reduced = part if reduced is None else reduced + part
        for c in range(groups):
            lanes = slice(c * LANES, (c + 1) * LANES)
            centre = jnp.concatenate(
                [
                    rim[c, e, REACH - 1, 8 : 8 + width, :],
                    frames[e, :, :, lanes].astype(F32).reshape(pixels, LANES),
                    rim[c, e, REACH, 8 : 8 + width, :],
                ],
                axis=0,
            )
            feature = centre + layer_scale[:, lanes] * reduced[:, lanes]
            feature = (feature * inside).astype(BF16).astype(F32)
            before = jnp.where(across == 0, 0.0, pltpu.roll(feature, 1, 0))
            after = jnp.where(across == width - 1, 0.0, pltpu.roll(feature, count - 1, 0))
            for ox, shifted in enumerate((before, feature, after)):
                packed = shifted.astype(BF16)
                for oy in range(3):
                    at = (oy * 3 + ox) * channels + c * LANES
                    taps[e * pixels : (e + 1) * pixels, at : at + LANES] = packed[
                        oy * width : oy * width + pixels
                    ]

    quarter = LANES // 4
    lane = lax.broadcasted_iota(jnp.int32, (epochs * pixels, LANES), 1)
    spot = lane // quarter
    within = lane - spot * quarter
    good = mask[...] > 0.5
    pooled = [[], []]
    for j in range(groups):
        gate_copies[j].wait()
        cols = slice(j * wide, (j + 1) * wide)
        lanes = slice(j * LANES, (j + 1) * LANES)
        preact = jnp.dot(taps[...], w_gates[:, cols], preferred_element_type=F32) + b_gates[:, cols]
        sorted_ = []
        for i in range(4):
            gate = lax.rem(spot - i + 4, 4)
            sorted_.append(
                jnp.take_along_axis(preact[:, i * LANES : (i + 1) * LANES], 4 * within + gate, axis=1)
            )
        gates = []
        for g in range(4):
            out = sorted_[0]
            for i in range(1, 4):
                out = jnp.where(spot == (g + i) % 4, sorted_[i], out)
            gates.append(out if g == 0 else pltpu.roll(out, LANES - g * quarter, 1))
        gate_in, gate_keep, gate_new, gate_out = gates
        decay = jnp.where(good, jnp.exp(-forget_rate[:, lanes] * softplus(gate_keep)), 1.0)
        inflow = jnp.where(good, sigmoid(gate_in) * jnp.tanh(gate_new), 0.0)
        opened = sigmoid(gate_out)
        d0, d1 = decay[:pixels], decay[pixels:]
        i0, i1 = inflow[:pixels], inflow[pixels:]
        decay0[:, lanes] = d0
        inflow0[:, lanes] = i0
        keep[:, lanes] = d0 * d1
        total = d1 * i0 + i1
        block[:, lanes] = total
        send[:pixels, lanes] = total.astype(BF16)
        open0[:, lanes] = opened[:pixels]
        open1[:, lanes] = opened[pixels:]
        pooled[0].append(pool(opened[:pixels] * jnp.tanh(i0)))
        pooled[1].append(pool(opened[pixels:] * jnp.tanh(total)))
    own = tokens_of([jnp.concatenate(parts, axis=1) for parts in pooled], attn_gain)
    known = jnp.zeros((send.shape[0] - pixels, channels), F32)
    send[pixels:, :] = put_tokens(known, own, 0).astype(BF16)


def run_block(tiles, staged, recv_pair, recv_next, w_gates, tail):
    spread, mask, short_rows, long_rows, frames, dw_kernel, w_expand, w_reduce = staged
    epochs, height, width, channels = frames.shape
    pixels = height * width
    plane = jax.ShapeDtypeStruct((pixels, channels), F32)
    vmem = pl.BlockSpec(memory_space=pltpu.VMEM)
    hbm = pl.BlockSpec(memory_space=pltpu.HBM)
    flops = 2 * epochs * pixels * (2 * w_expand.size + w_gates.size)
    return pl.pallas_call(
        functools.partial(block_kernel, tiles),
        name="block",
        out_shape=[jax.ShapeDtypeStruct((pixels + tail, channels), BF16)] + [plane] * 6,
        in_specs=[vmem] * 10 + [hbm],
        out_specs=[vmem] * 7,
        scratch_shapes=[
            pltpu.VMEM((channels // LANES, epochs, 2 * REACH, width + 16, LANES), F32),
            pltpu.VMEM((epochs, 2 * REACH * width, channels), F32),
            pltpu.VMEM((epochs * pixels, 9 * channels), BF16),
            pltpu.VMEM(w_gates.shape, BF16),
            pltpu.SemaphoreType.DMA((channels // LANES,)),
        ],
        compiler_params=pltpu.CompilerParams(vmem_limit_bytes=40 * 2**20),
        cost_estimate=pl.CostEstimate(flops=flops, bytes_accessed=2 * w_gates.size, transcendentals=0),
    )(spread, recv_pair, recv_next, frames, mask, short_rows, long_rows, dw_kernel, w_expand, w_reduce, w_gates)


def pool(memory):
    return jnp.mean(memory.astype(BF16).astype(F32), axis=0, keepdims=True)


def tokens_of(pooled, gain):
    both = jnp.concatenate(pooled, axis=0)
    center = jnp.mean(both, axis=-1, keepdims=True)
    centred = both - center
    variance = jnp.mean(centred * centred, axis=-1, keepdims=True)
    return (centred * lax.rsqrt(variance + 1e-06) * gain).astype(BF16).astype(F32)


def put_tokens(known, own, at):
    line = lax.broadcasted_iota(jnp.int32, known.shape, 0)
    return jnp.where(line == at, own[0:1], jnp.where(line == at + 1, own[1:2], known))


def relay_kernel(stage, arrived, decay0, inflow0, keep, block, open0, open1, short_rows, send):
    pixels = keep.shape[0]
    state = arrived[:pixels].astype(F32)
    cell = keep[...] * state + block[...]
    send[:pixels] = cell.astype(BF16)
    pooled = [
        pool(open0[...] * jnp.tanh(decay0[...] * state + inflow0[...])),
        pool(open1[...] * jnp.tanh(cell)),
    ]
    own = tokens_of(pooled, short_rows[5:6, :])
    send[pixels:] = put_tokens(arrived[pixels:].astype(F32), own, 2 * stage).astype(BF16)


def final_kernel(
    count,
    *refs,
):
    arrived = refs[:count]
    decay0, inflow0, keep, block, open0, open1, short_rows, months, slope, w_qkv, w_out = refs[count : count + 11]
    memory_hbm, change, memory, sems = refs[count + 11 :]
    pixels, channels = keep.shape
    total = months.shape[0]
    tail = arrived[0].shape[0] - pixels
    state = arrived[0][:pixels].astype(F32)
    known = arrived[0][pixels:].astype(F32)
    for more in arrived[1:]:
        state = state + more[:pixels].astype(F32)
        known = known + more[pixels:].astype(F32)
    cell0 = decay0[...] * state + inflow0[...]
    cell1 = keep[...] * state + block[...]
    outs = []
    copies = []
    for e, (gate, cell) in enumerate(((open0, cell0), (open1, cell1))):
        out = (gate[...] * jnp.tanh(cell)).astype(BF16)
        memory[e] = out
        copies.append(pltpu.make_async_copy(memory.at[e], memory_hbm.at[e], sems.at[e]))
        copies[-1].start()
        outs.append(out)
    own = tokens_of([pool(out) for out in outs], short_rows[5:6, :])
    stage = lax.axis_index("epoch")
    tokens = put_tokens(known, own, 2 * stage).astype(BF16)
    heads = slope.shape[1]
    depth = channels // heads
    qkv = jnp.dot(tokens, w_qkv[...], preferred_element_type=F32).astype(BF16).astype(F32)[:total]
    queries = qkv[:, :channels]
    keys = qkv[:, channels : 2 * channels]
    values = qkv[:, 2 * channels :]
    line = lax.broadcasted_iota(jnp.int32, (total, channels), 0)
    member = lax.broadcasted_iota(jnp.int32, (channels, heads), 0) // depth
    head_of = jnp.where(member == lax.broadcasted_iota(jnp.int32, (channels, heads), 1), 1.0, 0.0)
    member_t = lax.broadcasted_iota(jnp.int32, (heads, channels), 1) // depth
    channel_of = jnp.where(
        member_t == lax.broadcasted_iota(jnp.int32, (heads, channels), 0), 1.0, 0.0
    )
    key_index = lax.broadcasted_iota(jnp.int32, (total, heads), 0)
    month = months[:, :heads]
    results = []
    for step in range(2):
        mine = 2 * stage + step
        query = jnp.sum(jnp.where(line == mine, queries, 0.0), axis=0, keepdims=True)
        raw = jnp.dot(query * keys, head_of, preferred_element_type=F32, precision=lax.Precision.HIGHEST)
        now = jnp.sum(jnp.where(key_index == mine, month, 0.0), axis=0, keepdims=True)
        scores = raw / math.sqrt(depth) - slope[...] * (now - month)
        scores = jnp.where(key_index <= mine, scores, -1e30)
        expo = jnp.exp(scores - jnp.max(scores, axis=0, keepdims=True))
        weights = expo / jnp.sum(expo, axis=0, keepdims=True)
        spread = jnp.dot(weights, channel_of, preferred_element_type=F32, precision=lax.Precision.HIGHEST)
        results.append(jnp.sum(spread * values, axis=0, keepdims=True))
    mixed = jnp.concatenate(results, axis=0).astype(BF16)
    change[...] = jnp.dot(mixed, w_out[...], preferred_element_type=F32).astype(BF16)
    for copy in copies:
        copy.wait()


def pairs(count, start):
    links = []
    for i in range(start, count - 1, 2):
        links += [(i, i + 1), (i + 1, i)]
    return links


def body(
    frames,
    valid,
    days,
    dw_kernel,
    dw_bias,
    norm_gain,
    norm_shift,
    w_expand,
    b_expand,
    w_reduce,
    layer_scale,
    w_gates,
    b_gates,
    forget_rate,
    attn_gain,
    w_query,
    w_key,
    w_value,
    w_out,
    head_slope,
):

    epochs, height, width, channels = frames.shape
    pixels = height * width
    tiles = lax.axis_size("tile")
    stages = lax.axis_size("epoch")
    total = epochs * stages
    tail = -(-total // 16) * 16
    even = lax.rem(lax.axis_index("tile"), 2) == 0
    top = frames[:, :REACH]
    bottom = frames[:, height - REACH :]
    recv_pair = lax.ppermute(jnp.where(even, bottom, top), "tile", pairs(tiles, 0))
    recv_next = lax.ppermute(jnp.where(even, top, bottom), "tile", pairs(tiles, 1))
    (
        spread,
        mask,
        short_rows,
        long_rows,
        months,
        slope,
        frames_near,
        dw_near,
        expand_near,
        reduce_near,
        qkv_near,
        out_near,
    ) = run_stage(
        frames,
        valid,
        days,
        dw_kernel,
        [dw_bias, norm_gain, norm_shift, layer_scale, forget_rate, attn_gain],
        [b_expand, b_gates],
        head_slope,
        w_expand,
        w_reduce,
        [w_query, w_key, w_value, w_out],
    )
    send, *state = run_block(
        tiles,
        (spread, mask, short_rows, long_rows, frames_near, dw_near, expand_near, reduce_near),
        recv_pair,
        recv_next,
        w_gates.reshape(9 * channels, -1),
        tail,
    )
    vmem = pl.BlockSpec(memory_space=pltpu.VMEM)

    def relay(stage, arrived):
        return pl.pallas_call(
            functools.partial(relay_kernel, stage),
            name="relay",
            out_shape=jax.ShapeDtypeStruct((pixels + tail, channels), BF16),
            in_specs=[vmem] * 8,
            out_specs=vmem,
            compiler_params=pltpu.CompilerParams(vmem_limit_bytes=16 * 2**20),
        )(arrived, *state, short_rows)

    arrived = []
    if stages <= 8:
        for stage in range(stages - 1):
            if stage > 0:
                send = relay(stage, arrived[-1])
            arrived.append(lax.ppermute(send, "epoch", [(stage, stage + 1)]))
    else:
        chain = [(i, i + 1) for i in range(stages - 1)]
        keep, block = state[2], state[3]

        def turn(_, arriving):
            out = (keep * arriving.astype(F32) + block).astype(BF16)
            return lax.ppermute(out, "epoch", chain)

        incoming = lax.fori_loop(0, stages - 1, turn, jnp.zeros((pixels, channels), BF16))
        blank = jnp.zeros((tail, channels), BF16)
        own = relay(0, jnp.concatenate([incoming, blank]))[pixels : pixels + epochs]
        known = lax.all_gather(own, "epoch", axis=0, tiled=True)
        known = jnp.concatenate([known, jnp.zeros((tail - total, channels), BF16)])
        arrived.append(jnp.concatenate([incoming, known]))

    memory, change = pl.pallas_call(
        functools.partial(final_kernel, len(arrived)),
        name="final",
        out_shape=[
            jax.ShapeDtypeStruct((epochs, pixels, channels), BF16),
            jax.ShapeDtypeStruct((epochs, channels), BF16),
        ],
        in_specs=[vmem] * (len(arrived) + 11),
        out_specs=[pl.BlockSpec(memory_space=pltpu.HBM), vmem],
        scratch_shapes=[
            pltpu.VMEM((epochs, pixels, channels), BF16),
            pltpu.SemaphoreType.DMA((epochs,)),
        ],
        compiler_params=pltpu.CompilerParams(vmem_limit_bytes=24 * 2**20),
    )(*arrived, *state, short_rows, months, slope, qkv_near, out_near)
    return (
        memory.reshape(epochs, height, width, channels),
        change.reshape(epochs, 1, 1, channels),
    )


def solution(mesh):
    placed = (
        P("epoch", ("groups", "tile"), None, None),
        P("epoch", ("groups", "tile"), None),
        P("groups"),
    ) + (P(),) * 17
    return jax.shard_map(
        body,
        mesh=mesh,
        in_specs=placed,
        out_specs=(
            P("epoch", ("groups", "tile"), None, None),
            P("epoch", ("groups", "tile"), None, None),
        ),
        check_vma=False,
    )
```

time: 62.5 us -> 64 us (1.024)
  local copies, waits for them, and re-layouts: 11.2 us -> 15.8 us
  starting transfers between devices: 7.82 us -> 4.62 us
  Pallas kernels: 18.9 us -> 21.4 us
  other arithmetic: 2.78 us -> 0.97 us
    unnamed x22 -> x38, local copies, waits for them, and re-layouts: 5.42 us -> 15.8 us
    pallas_call x4, Pallas kernels: 3.53 us -> 8.83 us  [the longest x1 4.89 us: run_stage(): pl.pallas_call(stage_kernel, name='stage', out_shape=out_shape, in_specs=...]
    reshape x9 -> x0, local copies, waits for them, and re-layouts: 4.9 us -> none  [the longest x8 4.82 us: row(): return vector.reshape(1, -1)]
    pallas_call x1, Pallas kernels: 15.4 us -> 12.5 us  [run_block(): pl.pallas_call(functools.partial(block_kernel, tiles), name='block', out_...]
    ppermute x6 -> x3, starting transfers between devices: 5.22 us -> 2.63 us  [body(): arrived.append(lax.ppermute(send, 'epoch', [(stage, stage + 1)]))]
    add x3 -> x0, other arithmetic: 0.99 us -> none  [the longest x1 0.98 us: body(): incoming = incoming + arrived]
    broadcast_in_dim x3 -> x0, local copies, waits for them, and re-layouts: 0.93 us -> none  [the longest x2 0.92 us: body(): jnp.broadcast_to(valid.reshape(epochs * pixels, 1), (epochs * pixels, LAN...]
    convert_element_type x2 -> x0, other arithmetic: 0.82 us -> none  [body(): send = (keep * incoming.astype(F32) + block).astype(BF16)]
  transfers between devices with their start and end apart: 8 -> 5, of which waited for: 1 -> 1; matrix products, arithmetic and copies ran while one was open for 9% -> 0% of each run, Pallas kernels for 2% -> 8%
where the time goes in v2:
time: 64 us; the launch traced here: 63.2 us
  Pallas kernels  21.4 us (33%)
  waiting for transfers between devices  19.7 us (31%)
  local copies, waits for them, and re-layouts  15.8 us (25%)
  starting transfers between devices  4.62 us (7%)
  other arithmetic  0.97 us (2%)
  between operations  0.75 us (1%)
    ppermute x3, waiting for transfers between devices, body(): arrived.append(lax.ppermute(send, 'epoch', [(stage, stage + 1)]))  19.7 us
    unnamed x38, local copies, waits for them, and re-layouts  15.8 us
    pallas_call x1, Pallas kernels, run_block(): pl.pallas_call(functools.partial(block_kernel, tiles), name='block', out_...  12.5 us
    pallas_call x1, Pallas kernels, run_stage(): pl.pallas_call(stage_kernel, name='stage', out_shape=out_shape, in_specs=...  4.89 us
    pallas_call x1, Pallas kernels, body(): pl.pallas_call(functools.partial(final_kernel, len(arrived)), name='final...  2.95 us
    ppermute x3, starting transfers between devices, body(): arrived.append(lax.ppermute(send, 'epoch', [(stage, stage + 1)]))  2.63 us
    ppermute x1, starting transfers between devices, body(): lax.ppermute(jnp.where(even, top, bottom), 'tile', pairs(tiles, 1))  1.92 us
  transfers between devices with their start and end apart: 5, of which 1 were waited for; matrix products, arithmetic and copies ran while one was open for 0% of the time, Pallas kernels for 8%

profile of v2, /device:TPU:30, one launch (start us, length us, event | category | flops | bytes accessed | tf_op | source)
XLA Modules:
  0.0 63.2 jit_solution(11066015017436278601)
XLA Ops:
  0.6 1.0 %broadcast_select_fusion = (bf16[2,4,16,384]{3,2,1,0:T(8,128)(2,1)S(1)}, bf16[2,4,16,384]{3,2,1,0:T(8,128)(2,1)S(1)}) fusion(pred[]{:T(512)S(6)} %eq.3, bf16[2,16,16,384]{3,2,1,0:T(8,128)(2,1)} %frames_hbm.1), kind=kLoop, calls=%fused_computation | loop fusion | flops 98304 | bytes 393217 | tf_op jit(solution)/shard_map/jit(_where)/select_n | solution.py:553
  1.6 1.9 %collective-permute-start.1 = (bf16[2,4,16,384]{3,2,1,0:T(8,128)(2,1)S(1)}, bf16[2,4,16,384]{3,2,1,0:T(8,128)(2,1)S(1)}, u32[]{:S(2)}, u32[]{:S(2)}) collective-permute-start(bf16[2,4,16,384]{3,2,1,0:T(8,128)(2,1)S(1)} %get-tuple-element.44), channel_id=1, source_target_pairs={{1,2},{2,1},{5,6},{6,5},{9,10},{10,9},{13,14},{14,13},{17,18},{18,... | collective-permute-start | bytes 294920 | tf_op jit(solution)/shard_map/ppermute | solution.py:553
  3.5 0.1 collective-permute-start
  3.6 0.0 copy-start
  3.6 1.0 %copy-done = bf16[2,16,16,384]{3,2,1,0:T(8,128)(2,1)S(1)} copy-done((bf16[2,16,16,384]{3,2,1,0:T(8,128)(2,1)S(1)}, bf16[2,16,16,384]{3,2,1,0:T(8,128)(2,1)}, u32[]{:S(2)}) %copy-start) | copy-done | bytes 393240
  4.6 1.3 %copy-done.1 = bf16[384,1536]{1,0:T(8,128)(2,1)S(1)} copy-done((bf16[384,1536]{1,0:T(8,128)(2,1)S(1)}, bf16[384,1536]{1,0:T(8,128)(2,1)}, u32[]{:S(2)}) %copy-start.1) | copy-done | bytes 1179672
  5.9 1.3 %copy-done.2 = bf16[1536,384]{1,0:T(8,128)(2,1)S(1)} copy-done((bf16[1536,384]{1,0:T(8,128)(2,1)S(1)}, bf16[1536,384]{1,0:T(8,128)(2,1)}, u32[]{:S(2)}) %copy-start.2) | copy-done | bytes 1179672
  7.2 1.0 %copy-done.3 = bf16[384,384]{1,0:T(8,128)(2,1)S(1)} copy-done((bf16[384,384]{1,0:T(8,128)(2,1)S(1)}, bf16[384,384]{1,0:T(8,128)(2,1)}, u32[]{:S(2)}) %copy-start.3) | copy-done | bytes 294936
  8.1 1.0 %copy-done.4 = bf16[384,384]{1,0:T(8,128)(2,1)S(1)} copy-done((bf16[384,384]{1,0:T(8,128)(2,1)S(1)}, bf16[384,384]{1,0:T(8,128)(2,1)}, u32[]{:S(2)}) %copy-start.4) | copy-done | bytes 294936
  9.1 1.0 %copy-done.5 = bf16[384,384]{1,0:T(8,128)(2,1)S(1)} copy-done((bf16[384,384]{1,0:T(8,128)(2,1)S(1)}, bf16[384,384]{1,0:T(8,128)(2,1)}, u32[]{:S(2)}) %copy-start.5) | copy-done | bytes 294936
  10.0 1.0 %copy-done.6 = bf16[384,384]{1,0:T(8,128)(2,1)S(1)} copy-done((bf16[384,384]{1,0:T(8,128)(2,1)S(1)}, bf16[384,384]{1,0:T(8,128)(2,1)}, u32[]{:S(2)}) %copy-start.6) | copy-done | bytes 294936
  11.0 0.9 %copy-done.7 = f32[7,7,384]{2,1,0:T(8,128)S(1)} copy-done((f32[7,7,384]{2,1,0:T(8,128)S(1)}, f32[7,7,384]{2,1,0:T(8,128)}, u32[]{:S(2)}) %copy-start.7) | copy-done | bytes 75288
  11.9 0.7 %copy-done.8 = s32[2,16,16]{2,1,0:T(8,128)S(1)} copy-done((s32[2,16,16]{2,1,0:T(8,128)S(1)}, s32[2,16,16]{2,1,0:T(8,128)}, u32[]{:S(2)}) %copy-start.8) | copy-done | bytes 2072
  12.6 0.7 %copy-done.9 = f32[1536]{0:T(1024)S(1)} copy-done((f32[1536]{0:T(1024)S(1)}, f32[1536]{0:T(1024)}, u32[]{:S(2)}) %copy-start.9) | copy-done | bytes 6168
  13.3 0.7 %copy-done.10 = f32[1536]{0:T(1024)S(1)} copy-done((f32[1536]{0:T(1024)S(1)}, f32[1536]{0:T(1024)}, u32[]{:S(2)}) %copy-start.10) | copy-done | bytes 6168
  14.0 0.7 %copy-done.11 = f32[384]{0:T(512)S(1)} copy-done((f32[384]{0:T(512)S(1)}, f32[384]{0:T(512)}, u32[]{:S(2)}) %copy-start.11) | copy-done | bytes 1560
  14.7 0.7 %copy-done.12 = f32[384]{0:T(512)S(1)} copy-done((f32[384]{0:T(512)S(1)}, f32[384]{0:T(512)}, u32[]{:S(2)}) %copy-start.12) | copy-done | bytes 1560
  15.4 0.7 %copy-done.13 = f32[384]{0:T(512)S(1)} copy-done((f32[384]{0:T(512)S(1)}, f32[384]{0:T(512)}, u32[]{:S(2)}) %copy-start.13) | copy-done | bytes 1560
  16.1 0.7 %copy-done.14 = f32[384]{0:T(512)S(1)} copy-done((f32[384]{0:T(512)S(1)}, f32[384]{0:T(512)}, u32[]{:S(2)}) %copy-start.14) | copy-done | bytes 1560
  16.7 0.7 %copy-done.15 = f32[384]{0:T(512)S(1)} copy-done((f32[384]{0:T(512)S(1)}, f32[384]{0:T(512)}, u32[]{:S(2)}) %copy-start.15) | copy-done | bytes 1560
  17.4 0.7 %copy-done.16 = f32[384]{0:T(512)S(1)} copy-done((f32[384]{0:T(512)S(1)}, f32[384]{0:T(512)}, u32[]{:S(2)}) %copy-start.16) | copy-done | bytes 1560
  18.1 0.7 %copy-done.17 = s32[8]{0:T(128)S(1)} copy-done((s32[8]{0:T(128)S(1)}, s32[8]{0:T(128)}, u32[]{:S(2)}) %copy-start.17) | copy-done | bytes 56
  18.8 0.7 %copy-done.18 = f32[8]{0:T(128)S(1)} copy-done((f32[8]{0:T(128)S(1)}, f32[8]{0:T(128)}, u32[]{:S(2)}) %copy-start.18) | copy-done | bytes 56
  19.4 4.9 %stage.1 = (f32[2,288,384]{2,1,0:T(8,128)S(1)}, f32[512,128]{1,0:T(8,128)S(1)}, f32[8,384]{1,0:T(8,128)S(1)}, f32[8,1536]{1,0:T(8,128)S(1)}, f32[8,128]{1,0:T(8,...) custom-call(bf16[2,16,16,384]{3,2,1,0:T(8,128)(2,1)S(1)} %copy-done,, ...), custom_call_target="tpu_custom_call" | custom-call | flops 10000000000 | bytes 4718592 | tf_op jit(solution)/shard_map/stage/pallas_call | solution.py:189
  24.3 12.5 %block.1 = (bf16[272,384]{1,0:T(8,128)(2,1)S(1)}, f32[256,384]{1,0:T(8,128)S(1)}, f32[256,384]{1,0:T(8,128)S(1)}, f32[256,384]{1,0:T(8,128)S(1)}, f32[256,384]{1...) custom-call(f32[2,288,384]{2,1,0:T(8,128)S(1)} %get-tuple-element.23.spread, ...), custom_call_target="tpu_custom_call" | custom-call | flops 6643777536 | bytes 10616832 | tf_op jit(solution)/shard_map/block/pallas_call | solution.py:404
  36.9 0.7 %collective-permute-start.2 = (bf16[272,384]{1,0:T(8,128)(2,1)S(1)}, bf16[272,384]{1,0:T(8,128)(2,1)S(1)}, u32[]{:S(2)}, u32[]{:S(2)}) collective-permute-start(bf16[272,384]{1,0:T(8,128)(2,1)S(1)} %get-tuple-element.31), channel_id=1, source_target_pairs={{0,4},{1,5},{2,6},{3,7},{16,20},{17,21},{18,22},{19,23}} | collective-permute-start | bytes 626696 | tf_op jit(solution)/shard_map/ppermute | solution.py:604
  37.6 0.5 relay.2
  38.1 0.7 %collective-permute-start.3 = (bf16[272,384]{1,0:T(8,128)(2,1)S(1)}, bf16[272,384]{1,0:T(8,128)(2,1)S(1)}, u32[]{:S(2)}, u32[]{:S(2)}) collective-permute-start(bf16[272,384]{1,0:T(8,128)(2,1)S(1)} %relay.2), channel_id=1, source_target_pairs={{4,8},{5,9},{6,10},{7,11},{20,24},{21,25},{22,26},{23,27}} | collective-permute-start | bytes 626696 | tf_op jit(solution)/shard_map/ppermute | solution.py:604
  38.8 0.5 relay.3
  39.3 1.3 %collective-permute-start.4 = (bf16[272,384]{1,0:T(8,128)(2,1)S(1)}, bf16[272,384]{1,0:T(8,128)(2,1)S(1)}, u32[]{:S(2)}, u32[]{:S(2)}) collective-permute-start(bf16[272,384]{1,0:T(8,128)(2,1)S(1)} %relay.3), channel_id=1, source_target_pairs={{8,12},{9,13},{10,14},{11,15},{24,28},{25,29},{26,30},{27,31}} | collective-permute-start | bytes 626696 | tf_op jit(solution)/shard_map/ppermute | solution.py:604
  40.5 19.7 %collective-permute-done.4.refs_2_ = bf16[272,384]{1,0:T(8,128)(2,1)S(1)} collective-permute-done((bf16[272,384]{1,0:T(8,128)(2,1)S(1)}, bf16[272,384]{1,0:T(8,128)(2,1)S(1)}, u32[]{:S(2)}, u32[]{:S(2)}) %collective-permute-start.4) | collective-permute-done | bytes 208928 | tf_op jit(solution)/shard_map/ppermute | solution.py:604
  60.3 3.0 %final.1 = (bf16[2,256,384]{2,1,0:T(8,128)(2,1)}, bf16[2,384]{1,0:T(2,128)(2,1)}) custom-call(bf16[272,384]{1,0:T(8,128)(2,1)S(1)} %collective-permute-done.2.arrived.refs_0_, bf16[272,384]{1,0:T(8,128)(2,1)S(1)} %collective-permute-done.3.arrived.refs_1_, bf16[272,384]{1,0:T(8,128)(2,1)S(1)} %collective-permute-done.4.refs_2_, ...), custom_call_target="tpu_custom_call" | custom-call | tf_op jit(solution)/shard_map/final/pallas_call | solution.py:620
  (22 shorter events, 0.0 us)
Async XLA Ops:
  1.6 22.7 %collective-permute-start.1 = (bf16[2,4,16,384]{3,2,1,0:T(8,128)(2,1)S(1)}, bf16[2,4,16,384]{3,2,1,0:T(8,128)(2,1)S(1)}, u32[]{:S(2)}, u32[]{:S(2)}) collective-permute-start(bf16[2,4,16,384]{3,2,1,0:T(8,128)(2,1)S(1)} %get-tuple-element.44), channel_id=1, source_target_pairs={{1,2},{2,1},{5,6},{6,5},{9,10},{10,9},{13,14},{14,13},{17,18},{18,... | collective-permute-start | bytes 294920 | tf_op jit(solution)/shard_map/ppermute | solution.py:553
  3.5 20.8 %collective-permute-start = (bf16[2,4,16,384]{3,2,1,0:T(8,128)(2,1)S(1)}, bf16[2,4,16,384]{3,2,1,0:T(8,128)(2,1)S(1)}, u32[]{:S(2)}, u32[]{:S(2)}) collective-permute-start(bf16[2,4,16,384]{3,2,1,0:T(8,128)(2,1)S(1)} %get-tuple-element.45), channel_id=1, source_target_pairs={{0,1},{1,0},{2,3},{3,2},{4,5},{5,4},{6,7},{7,6},{8,9},{9,8},{10,11... | collective-permute-start | bytes 294920 | tf_op jit(solution)/shard_map/ppermute | solution.py:552
  3.6 1.0 %copy-start = (bf16[2,16,16,384]{3,2,1,0:T(8,128)(2,1)S(1)}, bf16[2,16,16,384]{3,2,1,0:T(8,128)(2,1)}, u32[]{:S(2)}) copy-start(bf16[2,16,16,384]{3,2,1,0:T(8,128)(2,1)} %frames_hbm.1) | copy-start | bytes 1179652
  4.6 1.3 %copy-start.1 = (bf16[384,1536]{1,0:T(8,128)(2,1)S(1)}, bf16[384,1536]{1,0:T(8,128)(2,1)}, u32[]{:S(2)}) copy-start(bf16[384,1536]{1,0:T(8,128)(2,1)} %w_expand_hbm.1) | copy-start | bytes 3538948
  5.9 1.3 %copy-start.2 = (bf16[1536,384]{1,0:T(8,128)(2,1)S(1)}, bf16[1536,384]{1,0:T(8,128)(2,1)}, u32[]{:S(2)}) copy-start(bf16[1536,384]{1,0:T(8,128)(2,1)} %w_reduce_hbm.1) | copy-start | bytes 3538948
  7.2 1.0 %copy-start.3 = (bf16[384,384]{1,0:T(8,128)(2,1)S(1)}, bf16[384,384]{1,0:T(8,128)(2,1)}, u32[]{:S(2)}) copy-start(bf16[384,384]{1,0:T(8,128)(2,1)} %w_query_hbm.1) | copy-start | bytes 884740
  8.1 1.0 %copy-start.4 = (bf16[384,384]{1,0:T(8,128)(2,1)S(1)}, bf16[384,384]{1,0:T(8,128)(2,1)}, u32[]{:S(2)}) copy-start(bf16[384,384]{1,0:T(8,128)(2,1)} %w_key_hbm.1) | copy-start | bytes 884740
  9.1 1.0 %copy-start.5 = (bf16[384,384]{1,0:T(8,128)(2,1)S(1)}, bf16[384,384]{1,0:T(8,128)(2,1)}, u32[]{:S(2)}) copy-start(bf16[384,384]{1,0:T(8,128)(2,1)} %w_value_hbm.1) | copy-start | bytes 884740
  10.0 1.0 %copy-start.6 = (bf16[384,384]{1,0:T(8,128)(2,1)S(1)}, bf16[384,384]{1,0:T(8,128)(2,1)}, u32[]{:S(2)}) copy-start(bf16[384,384]{1,0:T(8,128)(2,1)} %w_out_hbm.1) | copy-start | bytes 884740
  11.0 0.9 %copy-start.7 = (f32[7,7,384]{2,1,0:T(8,128)S(1)}, f32[7,7,384]{2,1,0:T(8,128)}, u32[]{:S(2)}) copy-start(f32[7,7,384]{2,1,0:T(8,128)} %dw_hbm.1) | copy-start | bytes 225796
  11.9 0.7 %copy-start.8 = (s32[2,16,16]{2,1,0:T(8,128)S(1)}, s32[2,16,16]{2,1,0:T(8,128)}, u32[]{:S(2)}) copy-start(s32[2,16,16]{2,1,0:T(8,128)} %valid_hbm.1) | copy-start | bytes 6148
  12.6 0.7 %copy-start.9 = (f32[1536]{0:T(1024)S(1)}, f32[1536]{0:T(1024)}, u32[]{:S(2)}) copy-start(f32[1536]{0:T(1024)} %b_expand_hbm.1) | copy-start | bytes 18436
  13.3 0.7 %copy-start.10 = (f32[1536]{0:T(1024)S(1)}, f32[1536]{0:T(1024)}, u32[]{:S(2)}) copy-start(f32[1536]{0:T(1024)} %b_gates_hbm.1) | copy-start | bytes 18436
  14.0 0.7 %copy-start.11 = (f32[384]{0:T(512)S(1)}, f32[384]{0:T(512)}, u32[]{:S(2)}) copy-start(f32[384]{0:T(512)} %dw_bias_hbm.1) | copy-start | bytes 4612
  14.7 0.7 %copy-start.12 = (f32[384]{0:T(512)S(1)}, f32[384]{0:T(512)}, u32[]{:S(2)}) copy-start(f32[384]{0:T(512)} %norm_gain_hbm.1) | copy-start | bytes 4612
  15.4 0.7 %copy-start.13 = (f32[384]{0:T(512)S(1)}, f32[384]{0:T(512)}, u32[]{:S(2)}) copy-start(f32[384]{0:T(512)} %norm_shift_hbm.1) | copy-start | bytes 4612
  16.1 0.7 %copy-start.14 = (f32[384]{0:T(512)S(1)}, f32[384]{0:T(512)}, u32[]{:S(2)}) copy-start(f32[384]{0:T(512)} %layer_scale_hbm.1) | copy-start | bytes 4612
  16.7 0.7 %copy-start.15 = (f32[384]{0:T(512)S(1)}, f32[384]{0:T(512)}, u32[]{:S(2)}) copy-start(f32[384]{0:T(512)} %forget_rate_hbm.1) | copy-start | bytes 4612
  17.4 0.7 %copy-start.16 = (f32[384]{0:T(512)S(1)}, f32[384]{0:T(512)}, u32[]{:S(2)}) copy-start(f32[384]{0:T(512)} %attn_gain_hbm.1) | copy-start | bytes 4612
  18.1 0.7 %copy-start.17 = (s32[8]{0:T(128)S(1)}, s32[8]{0:T(128)}, u32[]{:S(2)}) copy-start(s32[8]{0:T(128)} %days_hbm.1) | copy-start | bytes 100
  18.8 0.7 %copy-start.18 = (f32[8]{0:T(128)S(1)}, f32[8]{0:T(128)}, u32[]{:S(2)}) copy-start(f32[8]{0:T(128)} %head_slope_hbm.1) | copy-start | bytes 100
  36.9 0.7 %collective-permute-start.2 = (bf16[272,384]{1,0:T(8,128)(2,1)S(1)}, bf16[272,384]{1,0:T(8,128)(2,1)S(1)}, u32[]{:S(2)}, u32[]{:S(2)}) collective-permute-start(bf16[272,384]{1,0:T(8,128)(2,1)S(1)} %get-tuple-element.31), channel_id=1, source_target_pairs={{0,4},{1,5},{2,6},{3,7},{16,20},{17,21},{18,22},{19,23}} | collective-permute-start | bytes 626696 | tf_op jit(solution)/shard_map/ppermute | solution.py:604
  38.1 0.7 %collective-permute-start.3 = (bf16[272,384]{1,0:T(8,128)(2,1)S(1)}, bf16[272,384]{1,0:T(8,128)(2,1)S(1)}, u32[]{:S(2)}, u32[]{:S(2)}) collective-permute-start(bf16[272,384]{1,0:T(8,128)(2,1)S(1)} %relay.2), channel_id=1, source_target_pairs={{4,8},{5,9},{6,10},{7,11},{20,24},{21,25},{22,26},{23,27}} | collective-permute-start | bytes 626696 | tf_op jit(solution)/shard_map/ppermute | solution.py:604
  39.3 21.0 %collective-permute-start.4 = (bf16[272,384]{1,0:T(8,128)(2,1)S(1)}, bf16[272,384]{1,0:T(8,128)(2,1)S(1)}, u32[]{:S(2)}, u32[]{:S(2)}) collective-permute-start(bf16[272,384]{1,0:T(8,128)(2,1)S(1)} %relay.3), channel_id=1, source_target_pairs={{8,12},{9,13},{10,14},{11,15},{24,28},{25,29},{26,30},{27,31}} | collective-permute-start | bytes 626696 | tf_op jit(solution)/shard_map/ppermute | solution.py:604

commit v3 on v2

--- a/solution.py
+++ b/solution.py
@@ -170,6 +170,7 @@
     operands = [frames, valid, days, dw_kernel]
     operands += [short[0], short[1], short[2], long[0], short[3], long[1], short[4], short[5], slope]
     operands += [w_expand, w_reduce, *w_qkvo]
+    operands = [pltpu.with_memory_space_constraint(x, pltpu.HBM) for x in operands]
     hbm = pl.BlockSpec(memory_space=pltpu.HBM)
     vmem = pl.BlockSpec(memory_space=pltpu.VMEM)
     out_shape = [

time: 64 us -> 47.7 us (0.75)
  local copies, waits for them, and re-layouts: 15.8 us -> 0 us
    unnamed x38 -> x0, local copies, waits for them, and re-layouts: 15.8 us -> none
  transfers between devices with their start and end apart: 5 -> 5, of which waited for: 1 -> 1; matrix products, arithmetic and copies ran while one was open for 0% -> 0% of each run, Pallas kernels for 8% -> 10%
where the time goes in v3:
time: 47.7 us; the launch traced here: 47.2 us
  Pallas kernels  21.3 us (45%)
  waiting for transfers between devices  19.5 us (41%)
  starting transfers between devices  4.62 us (10%)
  other arithmetic  0.97 us (2%)
  between operations  0.73 us (2%)
    ppermute x3, waiting for transfers between devices, body(): arrived.append(lax.ppermute(send, 'epoch', [(stage, stage + 1)]))  19.5 us
    pallas_call x1, Pallas kernels, run_block(): pl.pallas_call(functools.partial(block_kernel, tiles), name='block', out_...  12.5 us
    pallas_call x1, Pallas kernels, run_stage(): pl.pallas_call(stage_kernel, name='stage', out_shape=out_shape, in_specs=...  4.85 us
    pallas_call x1, Pallas kernels, body(): pl.pallas_call(functools.partial(final_kernel, len(arrived)), name='final...  2.95 us
    ppermute x3, starting transfers between devices, body(): arrived.append(lax.ppermute(send, 'epoch', [(stage, stage + 1)]))  2.63 us
    ppermute x1, starting transfers between devices, body(): lax.ppermute(jnp.where(even, top, bottom), 'tile', pairs(tiles, 1))  1.92 us
    pallas_call x2, Pallas kernels, relay(): pl.pallas_call(functools.partial(relay_kernel, stage), name='relay', out_...  0.99 us
    select_n x1, other arithmetic, body(): jnp.where(even, top, bottom)  0.97 us
  transfers between devices with their start and end apart: 5, of which 1 were waited for; matrix products, arithmetic and copies ran while one was open for 0% of the time, Pallas kernels for 10%

profile of v3, /device:TPU:30, one launch (start us, length us, event | category | flops | bytes accessed | tf_op | source)
XLA Modules:
  0.0 47.2 jit_solution(1891796233833285549)
XLA Ops:
  0.6 1.0 %broadcast_select_fusion = (bf16[2,4,16,384]{3,2,1,0:T(8,128)(2,1)S(1)}, bf16[2,4,16,384]{3,2,1,0:T(8,128)(2,1)S(1)}) fusion(pred[]{:T(512)S(6)} %eq.3, bf16[2,16,16,384]{3,2,1,0:T(8,128)(2,1)} %frames_hbm.1), kind=kLoop, calls=%fused_computation | loop fusion | flops 98304 | bytes 393217 | tf_op jit(solution)/shard_map/jit(_where)/select_n | solution.py:554
  1.6 1.9 %collective-permute-start.1 = (bf16[2,4,16,384]{3,2,1,0:T(8,128)(2,1)S(1)}, bf16[2,4,16,384]{3,2,1,0:T(8,128)(2,1)S(1)}, u32[]{:S(2)}, u32[]{:S(2)}) collective-permute-start(bf16[2,4,16,384]{3,2,1,0:T(8,128)(2,1)S(1)} %get-tuple-element.44), channel_id=1, source_target_pairs={{1,2},{2,1},{5,6},{6,5},{9,10},{10,9},{13,14},{14,13},{17,18},{18,... | collective-permute-start | bytes 294920 | tf_op jit(solution)/shard_map/ppermute | solution.py:554
  3.5 0.1 collective-permute-start
  3.6 4.9 %stage.1 = (f32[2,288,384]{2,1,0:T(8,128)S(1)}, f32[512,128]{1,0:T(8,128)S(1)}, f32[8,384]{1,0:T(8,128)S(1)}, f32[8,1536]{1,0:T(8,128)S(1)}, f32[8,128]{1,0:T(8,...) custom-call(bf16[2,16,16,384]{3,2,1,0:T(8,128)(2,1)} %frames_hbm.1, ...), custom_call_target="tpu_custom_call" | custom-call | flops 10000000000 | bytes 4718592 | tf_op jit(solution)/shard_map/stage/pallas_call | solution.py:190
  8.5 0.0 collective-permute-done.1.recv_next
  8.5 0.0 collective-permute-done.recv_pair
  8.5 12.5 %block.1 = (bf16[272,384]{1,0:T(8,128)(2,1)S(1)}, f32[256,384]{1,0:T(8,128)S(1)}, f32[256,384]{1,0:T(8,128)S(1)}, f32[256,384]{1,0:T(8,128)S(1)}, f32[256,384]{1...) custom-call(f32[2,288,384]{2,1,0:T(8,128)S(1)} %get-tuple-element.23.spread, ...), custom_call_target="tpu_custom_call" | custom-call | flops 6643777536 | bytes 10616832 | tf_op jit(solution)/shard_map/block/pallas_call | solution.py:405
  21.0 0.7 %collective-permute-start.2 = (bf16[272,384]{1,0:T(8,128)(2,1)S(1)}, bf16[272,384]{1,0:T(8,128)(2,1)S(1)}, u32[]{:S(2)}, u32[]{:S(2)}) collective-permute-start(bf16[272,384]{1,0:T(8,128)(2,1)S(1)} %get-tuple-element.31), channel_id=1, source_target_pairs={{0,4},{1,5},{2,6},{3,7},{16,20},{17,21},{18,22},{19,23}} | collective-permute-start | bytes 626696 | tf_op jit(solution)/shard_map/ppermute | solution.py:605
  21.7 0.0 collective-permute-done.2.arrived.refs_0_
  21.7 0.5 %relay.2 = bf16[272,384]{1,0:T(8,128)(2,1)S(1)} custom-call(bf16[272,384]{1,0:T(8,128)(2,1)S(1)} %collective-permute-done.2.arrived.refs_0_, f32[256,384]{1,0:T(8,128)S(1)} %get-tuple-element.32.decay0.refs_3_, f32[256,384]{1,0:T(8,128)S(1)} %get-tuple-element.33.inflow0.refs_4_, f32[256,384]{1,0:T(8,128)S(1)} %get-tuple-element.34.keep.refs_5_, ...), custom_call_target="tpu_custom_call" | custom-call | tf_op jit(solution)/shard_map/relay/pallas_call | solution.py:591
  22.2 0.7 %collective-permute-start.3 = (bf16[272,384]{1,0:T(8,128)(2,1)S(1)}, bf16[272,384]{1,0:T(8,128)(2,1)S(1)}, u32[]{:S(2)}, u32[]{:S(2)}) collective-permute-start(bf16[272,384]{1,0:T(8,128)(2,1)S(1)} %relay.2), channel_id=1, source_target_pairs={{4,8},{5,9},{6,10},{7,11},{20,24},{21,25},{22,26},{23,27}} | collective-permute-start | bytes 626696 | tf_op jit(solution)/shard_map/ppermute | solution.py:605
  22.9 0.0 collective-permute-done.3.arrived.refs_1_
  22.9 0.5 %relay.3 = bf16[272,384]{1,0:T(8,128)(2,1)S(1)} custom-call(bf16[272,384]{1,0:T(8,128)(2,1)S(1)} %collective-permute-done.3.arrived.refs_1_, f32[256,384]{1,0:T(8,128)S(1)} %get-tuple-element.32.decay0.refs_3_, f32[256,384]{1,0:T(8,128)S(1)} %get-tuple-element.33.inflow0.refs_4_, f32[256,384]{1,0:T(8,128)S(1)} %get-tuple-element.34.keep.refs_5_, ...), custom_call_target="tpu_custom_call" | custom-call | tf_op jit(solution)/shard_map/relay/pallas_call | solution.py:591
  23.4 1.3 %collective-permute-start.4 = (bf16[272,384]{1,0:T(8,128)(2,1)S(1)}, bf16[272,384]{1,0:T(8,128)(2,1)S(1)}, u32[]{:S(2)}, u32[]{:S(2)}) collective-permute-start(bf16[272,384]{1,0:T(8,128)(2,1)S(1)} %relay.3), channel_id=1, source_target_pairs={{8,12},{9,13},{10,14},{11,15},{24,28},{25,29},{26,30},{27,31}} | collective-permute-start | bytes 626696 | tf_op jit(solution)/shard_map/ppermute | solution.py:605
  24.7 19.5 %collective-permute-done.4.refs_2_ = bf16[272,384]{1,0:T(8,128)(2,1)S(1)} collective-permute-done((bf16[272,384]{1,0:T(8,128)(2,1)S(1)}, bf16[272,384]{1,0:T(8,128)(2,1)S(1)}, u32[]{:S(2)}, u32[]{:S(2)}) %collective-permute-start.4) | collective-permute-done | bytes 208928 | tf_op jit(solution)/shard_map/ppermute | solution.py:605
  44.2 3.0 %final.1 = (bf16[2,256,384]{2,1,0:T(8,128)(2,1)}, bf16[2,384]{1,0:T(2,128)(2,1)}) custom-call(bf16[272,384]{1,0:T(8,128)(2,1)S(1)} %collective-permute-done.2.arrived.refs_0_, bf16[272,384]{1,0:T(8,128)(2,1)S(1)} %collective-permute-done.3.arrived.refs_1_, bf16[272,384]{1,0:T(8,128)(2,1)S(1)} %collective-permute-done.4.refs_2_, ...), custom_call_target="tpu_custom_call" | custom-call | tf_op jit(solution)/shard_map/final/pallas_call | solution.py:621
Async XLA Ops:
  1.6 6.9 %collective-permute-start.1 = (bf16[2,4,16,384]{3,2,1,0:T(8,128)(2,1)S(1)}, bf16[2,4,16,384]{3,2,1,0:T(8,128)(2,1)S(1)}, u32[]{:S(2)}, u32[]{:S(2)}) collective-permute-start(bf16[2,4,16,384]{3,2,1,0:T(8,128)(2,1)S(1)} %get-tuple-element.44), channel_id=1, source_target_pairs={{1,2},{2,1},{5,6},{6,5},{9,10},{10,9},{13,14},{14,13},{17,18},{18,... | collective-permute-start | bytes 294920 | tf_op jit(solution)/shard_map/ppermute | solution.py:554
  3.5 5.0 %collective-permute-start = (bf16[2,4,16,384]{3,2,1,0:T(8,128)(2,1)S(1)}, bf16[2,4,16,384]{3,2,1,0:T(8,128)(2,1)S(1)}, u32[]{:S(2)}, u32[]{:S(2)}) collective-permute-start(bf16[2,4,16,384]{3,2,1,0:T(8,128)(2,1)S(1)} %get-tuple-element.45), channel_id=1, source_target_pairs={{0,1},{1,0},{2,3},{3,2},{4,5},{5,4},{6,7},{7,6},{8,9},{9,8},{10,11... | collective-permute-start | bytes 294920 | tf_op jit(solution)/shard_map/ppermute | solution.py:553
  21.0 0.7 %collective-permute-start.2 = (bf16[272,384]{1,0:T(8,128)(2,1)S(1)}, bf16[272,384]{1,0:T(8,128)(2,1)S(1)}, u32[]{:S(2)}, u32[]{:S(2)}) collective-permute-start(bf16[272,384]{1,0:T(8,128)(2,1)S(1)} %get-tuple-element.31), channel_id=1, source_target_pairs={{0,4},{1,5},{2,6},{3,7},{16,20},{17,21},{18,22},{19,23}} | collective-permute-start | bytes 626696 | tf_op jit(solution)/shard_map/ppermute | solution.py:605
  22.2 0.7 %collective-permute-start.3 = (bf16[272,384]{1,0:T(8,128)(2,1)S(1)}, bf16[272,384]{1,0:T(8,128)(2,1)S(1)}, u32[]{:S(2)}, u32[]{:S(2)}) collective-permute-start(bf16[272,384]{1,0:T(8,128)(2,1)S(1)} %relay.2), channel_id=1, source_target_pairs={{4,8},{5,9},{6,10},{7,11},{20,24},{21,25},{22,26},{23,27}} | collective-permute-start | bytes 626696 | tf_op jit(solution)/shard_map/ppermute | solution.py:605
  23.4 20.8 %collective-permute-start.4 = (bf16[272,384]{1,0:T(8,128)(2,1)S(1)}, bf16[272,384]{1,0:T(8,128)(2,1)S(1)}, u32[]{:S(2)}, u32[]{:S(2)}) collective-permute-start(bf16[272,384]{1,0:T(8,128)(2,1)S(1)} %relay.3), channel_id=1, source_target_pairs={{8,12},{9,13},{10,14},{11,15},{24,28},{25,29},{26,30},{27,31}} | collective-permute-start | bytes 626696 | tf_op jit(solution)/shard_map/ppermute | solution.py:605

commit v4 on v3

--- a/solution.py
+++ b/solution.py
@@ -223,15 +223,17 @@
     w_reduce,
     w_gates_hbm,
     send,
+    pooled,
     decay0,
     inflow0,
     keep,
     block,
     open0,
     open1,
+    taps,
+    w_later,
     rim,
     edge,
-    taps,
     w_gates,
     sems,
 ):
@@ -242,10 +244,11 @@
     pixels = height * width
     wide = 4 * LANES
 
+    early = w_gates.shape[1] // wide
     gate_copies = [
         pltpu.make_async_copy(
             w_gates_hbm.at[:, pl.ds(j * wide, wide)],
-            w_gates.at[:, pl.ds(j * wide, wide)],
+            w_gates.at[:, pl.ds(j * wide, wide)] if j < early else w_later.at[:, pl.ds((j - early) * wide, wide)],
             sems.at[j],
         )
         for j in range(groups)
@@ -257,10 +260,7 @@
     norm_gain = short_rows[1:2, :]
     norm_shift = short_rows[2:3, :]
     layer_scale = short_rows[3:4, :]
-    forget_rate = short_rows[4:5, :]
-    attn_gain = short_rows[5:6, :]
     b_expand = long_rows[0:1, :]
-    b_gates = long_rows[1:2, :]
 
     me = lax.axis_index("tile")
     odd = lax.rem(me, 2)
@@ -350,17 +350,31 @@
                         oy * width : oy * width + pixels
                     ]
 
+    for j in range(early):
+        gate_copies[j].wait()
+    cells_of(
+        range(early), 0, taps, w_gates, mask, short_rows, long_rows,
+        send, pooled, (decay0, inflow0, keep, block, open0, open1),
+    )
+    for copy in gate_copies[early:]:
+        copy.wait()
+
+
+def cells_of(parts, first, taps, w_gates, mask, short_rows, long_rows, send, pooled, state):
+    decay0, inflow0, keep, block, open0, open1 = state
+    pixels = keep.shape[0]
+    wide = 4 * LANES
     quarter = LANES // 4
-    lane = lax.broadcasted_iota(jnp.int32, (epochs * pixels, LANES), 1)
+    lane = lax.broadcasted_iota(jnp.int32, mask.shape, 1)
     spot = lane // quarter
     within = lane - spot * quarter
     good = mask[...] > 0.5
-    pooled = [[], []]
-    for j in range(groups):
-        gate_copies[j].wait()
-        cols = slice(j * wide, (j + 1) * wide)
-        lanes = slice(j * LANES, (j + 1) * LANES)
-        preact = jnp.dot(taps[...], w_gates[:, cols], preferred_element_type=F32) + b_gates[:, cols]
+    for j in parts:
+        cols = slice((j - first) * wide, (j - first + 1) * wide)
+        lanes = slice((j - first) * LANES, (j - first + 1) * LANES)
+        bias = long_rows[1:2, j * wide : (j + 1) * wide]
+        rate = short_rows[4:5, j * LANES : (j + 1) * LANES]
+        preact = jnp.dot(taps[...], w_gates[:, cols], preferred_element_type=F32) + bias
         sorted_ = []
         for i in range(4):
             gate = lax.rem(spot - i + 4, 4)
@@ -374,7 +388,7 @@
                 out = jnp.where(spot == (g + i) % 4, sorted_[i], out)
             gates.append(out if g == 0 else pltpu.roll(out, LANES - g * quarter, 1))
         gate_in, gate_keep, gate_new, gate_out = gates
-        decay = jnp.where(good, jnp.exp(-forget_rate[:, lanes] * softplus(gate_keep)), 1.0)
+        decay = jnp.where(good, jnp.exp(-rate * softplus(gate_keep)), 1.0)
         inflow = jnp.where(good, sigmoid(gate_in) * jnp.tanh(gate_new), 0.0)
         opened = sigmoid(gate_out)
         d0, d1 = decay[:pixels], decay[pixels:]
@@ -387,45 +401,126 @@
         send[:pixels, lanes] = total.astype(BF16)
         open0[:, lanes] = opened[:pixels]
         open1[:, lanes] = opened[pixels:]
-        pooled[0].append(pool(opened[:pixels] * jnp.tanh(i0)))
-        pooled[1].append(pool(opened[pixels:] * jnp.tanh(total)))
-    own = tokens_of([jnp.concatenate(parts, axis=1) for parts in pooled], attn_gain)
-    known = jnp.zeros((send.shape[0] - pixels, channels), F32)
-    send[pixels:, :] = put_tokens(known, own, 0).astype(BF16)
-
-
-def run_block(tiles, staged, recv_pair, recv_next, w_gates, tail):
+        pooled[0:1, lanes] = pool(opened[:pixels] * jnp.tanh(i0))
+        pooled[1:2, lanes] = pool(opened[pixels:] * jnp.tanh(total))
+
+
+def later_kernel(
+    first,
+    taps,
+    w_gates,
+    mask,
+    short_rows,
+    long_rows,
+    pooled_early,
+    send_early,
+    send,
+    decay0,
+    inflow0,
+    keep,
+    block,
+    open0,
+    open1,
+    pooled,
+):
+    channels = short_rows.shape[1]
+    cells_of(
+        range(first, channels // LANES), first, taps, w_gates, mask, short_rows, long_rows,
+        send, pooled, (decay0, inflow0, keep, block, open0, open1),
+    )
+    pixels = keep.shape[0]
+    both = jnp.concatenate([pooled_early[0:2, :], pooled[0:2, :]], axis=1)
+    own = tokens_of(both, short_rows[5:6, :])
+    tail = (send.shape[0] - pixels) * LANES // channels
+    known = jnp.zeros((tail, channels), F32)
+    write_tail(send, pixels, put_tokens(known, own, 0))
+
+
+def write_tail(send, pixels, tokens):
+    tail, channels = tokens.shape
+    for c in range(channels // LANES):
+        at = pixels + c * tail
+        send[at : at + tail, :] = tokens[:, c * LANES : (c + 1) * LANES].astype(BF16)
+
+
+def read_tail(arrived, pixels, channels):
+    tail = (arrived.shape[0] - pixels) * LANES // channels
+    parts = [
+        arrived[pixels + c * tail : pixels + (c + 1) * tail, :].astype(F32)
+        for c in range(channels // LANES)
+    ]
+    return jnp.concatenate(parts, axis=1)
+
+
+def run_block(tiles, early, staged, recv_pair, recv_next, w_gates, tail):
     spread, mask, short_rows, long_rows, frames, dw_kernel, w_expand, w_reduce = staged
     epochs, height, width, channels = frames.shape
     pixels = height * width
-    plane = jax.ShapeDtypeStruct((pixels, channels), F32)
+    depth = w_gates.shape[0]
     vmem = pl.BlockSpec(memory_space=pltpu.VMEM)
     hbm = pl.BlockSpec(memory_space=pltpu.HBM)
+    near = early * LANES
+    far = channels - near
+
+    def state(lanes):
+        return [jax.ShapeDtypeStruct((pixels, lanes), F32)] * 6
+
     flops = 2 * epochs * pixels * (2 * w_expand.size + w_gates.size)
-    return pl.pallas_call(
+    send, pooled, *rest = pl.pallas_call(
         functools.partial(block_kernel, tiles),
         name="block",
-        out_shape=[jax.ShapeDtypeStruct((pixels + tail, channels), BF16)] + [plane] * 6,
+        out_shape=[
+            jax.ShapeDtypeStruct((pixels, near), BF16),
+            jax.ShapeDtypeStruct((8, near), F32),
+            *state(near),
+            jax.ShapeDtypeStruct((epochs * pixels, depth), BF16),
+            jax.ShapeDtypeStruct((depth, 4 * far), BF16),
+        ],
         in_specs=[vmem] * 10 + [hbm],
-        out_specs=[vmem] * 7,
+        out_specs=[vmem] * 10,
         scratch_shapes=[
             pltpu.VMEM((channels // LANES, epochs, 2 * REACH, width + 16, LANES), F32),
             pltpu.VMEM((epochs, 2 * REACH * width, channels), F32),
-            pltpu.VMEM((epochs * pixels, 9 * channels), BF16),
-            pltpu.VMEM(w_gates.shape, BF16),
+            pltpu.VMEM((depth, 4 * near), BF16),
             pltpu.SemaphoreType.DMA((channels // LANES,)),
         ],
-        compiler_params=pltpu.CompilerParams(vmem_limit_bytes=40 * 2**20),
+        compiler_params=pltpu.CompilerParams(vmem_limit_bytes=32 * 2**20),
         cost_estimate=pl.CostEstimate(flops=flops, bytes_accessed=2 * w_gates.size, transcendentals=0),
-    )(spread, recv_pair, recv_next, frames, mask, short_rows, long_rows, dw_kernel, w_expand, w_reduce, w_gates)
+    )(
+        spread,
+        recv_pair,
+        recv_next,
+        frames,
+        mask,
+        short_rows,
+        long_rows,
+        dw_kernel,
+        w_expand,
+        w_reduce,
+        pltpu.with_memory_space_constraint(w_gates, pltpu.HBM),
+    )
+    *state_near, taps, w_later = rest
+    send_far, *state_far = pl.pallas_call(
+        functools.partial(later_kernel, early),
+        name="later",
+        out_shape=[
+            jax.ShapeDtypeStruct((pixels + tail * channels // LANES, far), BF16),
+            *state(far),
+        ],
+        in_specs=[vmem] * 6 + [pl.BlockSpec(memory_space=pl.ANY)],
+        out_specs=[vmem] * 7,
+        scratch_shapes=[pltpu.VMEM((8, far), F32)],
+        compiler_params=pltpu.CompilerParams(vmem_limit_bytes=24 * 2**20),
+        cost_estimate=pl.CostEstimate(flops=10**10, bytes_accessed=0, transcendentals=0),
+    )(taps, w_later, mask, short_rows, long_rows, pooled, send)
+    return (send, state_near), (send_far, state_far)
 
 
 def pool(memory):
     return jnp.mean(memory.astype(BF16).astype(F32), axis=0, keepdims=True)
 
 
-def tokens_of(pooled, gain):
-    both = jnp.concatenate(pooled, axis=0)
+def tokens_of(both, gain):
     center = jnp.mean(both, axis=-1, keepdims=True)
     centred = both - center
     variance = jnp.mean(centred * centred, axis=-1, keepdims=True)
@@ -437,45 +532,67 @@
     return jnp.where(line == at, own[0:1], jnp.where(line == at + 1, own[1:2], known))
 
 
-def relay_kernel(stage, arrived, decay0, inflow0, keep, block, open0, open1, short_rows, send):
+def step_cells(arrived, decay0, inflow0, keep, block):
+    state = arrived[: keep.shape[0]].astype(F32)
+    return decay0[...] * state + inflow0[...], keep[...] * state + block[...]
+
+
+def relay_kernel(arrived, decay0, inflow0, keep, block, open0, open1, before, send, pooled):
+    cell0, cell1 = step_cells(arrived, decay0, inflow0, keep, block)
+    send[...] = cell1.astype(BF16)
+    pooled[0:1, :] = pool(open0[...] * jnp.tanh(cell0))
+    pooled[1:2, :] = pool(open1[...] * jnp.tanh(cell1))
+
+
+def relay_later_kernel(
+    stage, arrived, decay0, inflow0, keep, block, open0, open1, pooled_early, short_rows, send
+):
     pixels = keep.shape[0]
-    state = arrived[:pixels].astype(F32)
-    cell = keep[...] * state + block[...]
-    send[:pixels] = cell.astype(BF16)
-    pooled = [
-        pool(open0[...] * jnp.tanh(decay0[...] * state + inflow0[...])),
-        pool(open1[...] * jnp.tanh(cell)),
-    ]
-    own = tokens_of(pooled, short_rows[5:6, :])
-    send[pixels:] = put_tokens(arrived[pixels:].astype(F32), own, 2 * stage).astype(BF16)
+    cell0, cell1 = step_cells(arrived, decay0, inflow0, keep, block)
+    send[:pixels] = cell1.astype(BF16)
+    pooled = jnp.concatenate(
+        [pool(open0[...] * jnp.tanh(cell0)), pool(open1[...] * jnp.tanh(cell1))], axis=0
+    )
+    both = jnp.concatenate([pooled_early[0:2, :], pooled], axis=1)
+    own = tokens_of(both, short_rows[5:6, :])
+    known = read_tail(arrived, pixels, short_rows.shape[1])
+    write_tail(send, pixels, put_tokens(known, own, 2 * stage))
 
 
 def final_kernel(
     count,
     *refs,
 ):
-    arrived = refs[:count]
-    decay0, inflow0, keep, block, open0, open1, short_rows, months, slope, w_qkv, w_out = refs[count : count + 11]
-    memory_hbm, change, memory, sems = refs[count + 11 :]
-    pixels, channels = keep.shape
+    halves = [
+        (refs[:count], refs[2 * count : 2 * count + 6]),
+        (refs[count : 2 * count], refs[2 * count + 6 : 2 * count + 12]),
+    ]
+    short_rows, months, slope, w_qkv, w_out = refs[2 * count + 12 : 2 * count + 17]
+    memory_hbm, change, memory, sems = refs[2 * count + 17 :]
+    epochs, pixels, channels = memory.shape
     total = months.shape[0]
-    tail = arrived[0].shape[0] - pixels
-    state = arrived[0][:pixels].astype(F32)
-    known = arrived[0][pixels:].astype(F32)
-    for more in arrived[1:]:
-        state = state + more[:pixels].astype(F32)
-        known = known + more[pixels:].astype(F32)
-    cell0 = decay0[...] * state + inflow0[...]
-    cell1 = keep[...] * state + block[...]
-    outs = []
-    copies = []
-    for e, (gate, cell) in enumerate(((open0, cell0), (open1, cell1))):
-        out = (gate[...] * jnp.tanh(cell)).astype(BF16)
-        memory[e] = out
-        copies.append(pltpu.make_async_copy(memory.at[e], memory_hbm.at[e], sems.at[e]))
-        copies[-1].start()
-        outs.append(out)
-    own = tokens_of([pool(out) for out in outs], short_rows[5:6, :])
+    pooled = [[], []]
+    at = 0
+    for arrived, (decay0, inflow0, keep, block, open0, open1) in halves:
+        lanes = slice(at, at + keep.shape[1])
+        at += keep.shape[1]
+        state = arrived[0][:pixels].astype(F32)
+        for more in arrived[1:]:
+            state = state + more[:pixels].astype(F32)
+        cell0 = decay0[...] * state + inflow0[...]
+        cell1 = keep[...] * state + block[...]
+        for e, (gate, cell) in enumerate(((open0, cell0), (open1, cell1))):
+            out = (gate[...] * jnp.tanh(cell)).astype(BF16)
+            memory[e, :, lanes] = out
+            pooled[e].append(pool(out))
+    copies = [pltpu.make_async_copy(memory.at[e], memory_hbm.at[e], sems.at[e]) for e in range(epochs)]
+    for copy in copies:
+        copy.start()
+    known = read_tail(halves[1][0][0], pixels, channels)
+    for more in halves[1][0][1:]:
+        known = known + read_tail(more, pixels, channels)
+    both = jnp.concatenate([jnp.concatenate(parts, axis=1) for parts in pooled], axis=0)
+    own = tokens_of(both, short_rows[5:6, :])
     stage = lax.axis_index("epoch")
     tokens = put_tokens(known, own, 2 * stage).astype(BF16)
     heads = slope.shape[1]
@@ -577,8 +694,10 @@
         w_reduce,
         [w_query, w_key, w_value, w_out],
     )
-    send, *state = run_block(
+    early = max(1, channels // LANES - 1)
+    (send, near), (send_far, far) = run_block(
         tiles,
+        early,
         (spread, mask, short_rows, long_rows, frames_near, dw_near, expand_near, reduce_near),
         recv_pair,
         recv_next,
@@ -586,37 +705,70 @@
         tail,
     )
     vmem = pl.BlockSpec(memory_space=pltpu.VMEM)
-
-    def relay(stage, arrived):
+    params = pltpu.CompilerParams(vmem_limit_bytes=16 * 2**20)
+    cost = pl.CostEstimate(flops=10**10, bytes_accessed=0, transcendentals=0)
+
+    def relay(arrived, before):
         return pl.pallas_call(
-            functools.partial(relay_kernel, stage),
+            relay_kernel,
             name="relay",
-            out_shape=jax.ShapeDtypeStruct((pixels + tail, channels), BF16),
-            in_specs=[vmem] * 8,
+            out_shape=[
+                jax.ShapeDtypeStruct((pixels, early * LANES), BF16),
+                jax.ShapeDtypeStruct((8, early * LANES), F32),
+            ],
+            in_specs=[vmem] * 7 + [pl.BlockSpec(memory_space=pl.ANY)],
+            out_specs=[vmem] * 2,
+            compiler_params=params,
+            cost_estimate=cost,
+        )(arrived, *near, before)
+
+    def relay_later(stage, arrived, pooled):
+        return pl.pallas_call(
+            functools.partial(relay_later_kernel, stage),
+            name="relay_later",
+            out_shape=jax.ShapeDtypeStruct(send_far.shape, BF16),
+            in_specs=[vmem] * 9,
             out_specs=vmem,
-            compiler_params=pltpu.CompilerParams(vmem_limit_bytes=16 * 2**20),
-        )(arrived, *state, short_rows)
+            compiler_params=params,
+            cost_estimate=cost,
+        )(arrived, *far, pooled, short_rows)
 
     arrived = []
+    arrived_far = []
     if stages <= 8:
         for stage in range(stages - 1):
+            link = [(stage, stage + 1)]
             if stage > 0:
-                send = relay(stage, arrived[-1])
-            arrived.append(lax.ppermute(send, "epoch", [(stage, stage + 1)]))
+                send, pooled = relay(arrived[-1], send_far)
+                send_far = relay_later(stage, arrived_far[-1], pooled)
+            arrived.append(lax.ppermute(send, "epoch", link))
+            arrived_far.append(lax.ppermute(send_far, "epoch", link))
     else:
         chain = [(i, i + 1) for i in range(stages - 1)]
-        keep, block = state[2], state[3]
-
-        def turn(_, arriving):
-            out = (keep * arriving.astype(F32) + block).astype(BF16)
-            return lax.ppermute(out, "epoch", chain)
-
-        incoming = lax.fori_loop(0, stages - 1, turn, jnp.zeros((pixels, channels), BF16))
-        blank = jnp.zeros((tail, channels), BF16)
-        own = relay(0, jnp.concatenate([incoming, blank]))[pixels : pixels + epochs]
-        known = lax.all_gather(own, "epoch", axis=0, tiled=True)
+
+        def along(state, width):
+            keep, block = state[2], state[3]
+
+            def turn(_, arriving):
+                out = (keep * arriving.astype(F32) + block).astype(BF16)
+                return lax.ppermute(out, "epoch", chain)
+
+            return lax.fori_loop(0, stages - 1, turn, jnp.zeros((pixels, width), BF16))
+
+        def unfold(tokens):
+            parts = jnp.split(tokens, channels // LANES, axis=1)
+            return jnp.concatenate(parts, axis=0)
+
+        incoming = along(near, early * LANES)
+        incoming_far = along(far, channels - early * LANES)
+        _, pooled = relay(incoming, send_far)
+        blank = jnp.zeros((tail * channels // LANES, LANES), BF16)
+        told = relay_later(0, jnp.concatenate([incoming_far, blank]), pooled)[pixels:]
+        told = jnp.concatenate(jnp.split(told, channels // LANES, axis=0), axis=1)
+        known = lax.all_gather(told[:epochs], "epoch", axis=0, tiled=True)
         known = jnp.concatenate([known, jnp.zeros((tail - total, channels), BF16)])
-        arrived.append(jnp.concatenate([incoming, known]))
+        arrived.append(incoming)
+        arrived_far.append(jnp.concatenate([incoming_far, unfold(known)]))
 
     memory, change = pl.pallas_call(
         functools.partial(final_kernel, len(arrived)),
@@ -625,14 +777,14 @@
             jax.ShapeDtypeStruct((epochs, pixels, channels), BF16),
             jax.ShapeDtypeStruct((epochs, channels), BF16),
         ],
-        in_specs=[vmem] * (len(arrived) + 11),
+        in_specs=[vmem] * (2 * len(arrived) + 17),
         out_specs=[pl.BlockSpec(memory_space=pltpu.HBM), vmem],
         scratch_shapes=[
             pltpu.VMEM((epochs, pixels, channels), BF16),
             pltpu.SemaphoreType.DMA((epochs,)),
         ],
         compiler_params=pltpu.CompilerParams(vmem_limit_bytes=24 * 2**20),
-    )(*arrived, *state, short_rows, months, slope, qkv_near, out_near)
+    )(*arrived, *arrived_far, *near, *far, short_rows, months, slope, qkv_near, out_near)
     return (
         memory.reshape(epochs, height, width, channels),
         change.reshape(epochs, 1, 1, channels),

time: 47.7 us -> 40.6 us (0.85)
  the two profiles are of different devices: /device:TPU:30 before, /device:TPU:24 now
where the time goes in v4:
time: 40.6 us; the launch traced here: 40.4 us
  Pallas kernels  19.6 us (48%)
  waiting for transfers between devices  10.2 us (25%)
  starting transfers between devices  8.82 us (22%)
  other arithmetic  0.97 us (2%)
  between operations  0.77 us (2%)
    ppermute x3, waiting for transfers between devices, body(): arrived_far.append(lax.ppermute(send_far, 'epoch', link))  10.1 us
    pallas_call x1, Pallas kernels, run_block(): pl.pallas_call(functools.partial(block_kernel, tiles), name='block', out_...  8.79 us
    pallas_call x1, Pallas kernels, run_stage(): pl.pallas_call(stage_kernel, name='stage', out_shape=out_shape, in_specs=...  4.77 us
    pallas_call x1, Pallas kernels, run_block(): pl.pallas_call(functools.partial(later_kernel, early), name='later', out_...  2.95 us
    ppermute x1, starting transfers between devices, body(): lax.ppermute(jnp.where(even, bottom, top), 'tile', pairs(tiles, 0))  2.91 us
    ppermute x3, starting transfers between devices, body(): arrived.append(lax.ppermute(send, 'epoch', link))  2.63 us
    ppermute x3, starting transfers between devices, body(): arrived_far.append(lax.ppermute(send_far, 'epoch', link))  2.61 us
    pallas_call x1, Pallas kernels, body(): pl.pallas_call(functools.partial(final_kernel, len(arrived)), name='final...  2.31 us
  transfers between devices with their start and end apart: 8, of which 1 were waited for; matrix products, arithmetic and copies ran while one was open for 0% of the time, Pallas kernels for 21%

profile of v4, /device:TPU:24, one launch (start us, length us, event | category | flops | bytes accessed | tf_op | source)
XLA Modules:
  0.0 40.4 jit_solution(4424224641316984138)
XLA Ops:
  0.6 1.0 %broadcast_select_fusion = (bf16[2,4,16,384]{3,2,1,0:T(8,128)(2,1)S(1)}, bf16[2,4,16,384]{3,2,1,0:T(8,128)(2,1)S(1)}) fusion(pred[]{:T(512)S(6)} %eq.3, bf16[2,16,16,384]{3,2,1,0:T(8,128)(2,1)} %frames_hbm.1), kind=kLoop, calls=%fused_computation | loop fusion | flops 98304 | bytes 393217 | tf_op jit(solution)/shard_map/jit(_where)/select_n | solution.py:671
  1.6 0.7 %collective-permute-start.1 = (bf16[2,4,16,384]{3,2,1,0:T(8,128)(2,1)S(1)}, bf16[2,4,16,384]{3,2,1,0:T(8,128)(2,1)S(1)}, u32[]{:S(2)}, u32[]{:S(2)}) collective-permute-start(bf16[2,4,16,384]{3,2,1,0:T(8,128)(2,1)S(1)} %get-tuple-element.72), channel_id=1, source_target_pairs={{1,2},{2,1},{5,6},{6,5},{9,10},{10,9},{13,14},{14,13},{17,18},{18,... | collective-permute-start | bytes 294920 | tf_op jit(solution)/shard_map/ppermute | solution.py:671
  2.3 2.9 %collective-permute-start = (bf16[2,4,16,384]{3,2,1,0:T(8,128)(2,1)S(1)}, bf16[2,4,16,384]{3,2,1,0:T(8,128)(2,1)S(1)}, u32[]{:S(2)}, u32[]{:S(2)}) collective-permute-start(bf16[2,4,16,384]{3,2,1,0:T(8,128)(2,1)S(1)} %get-tuple-element.73), channel_id=1, source_target_pairs={{0,1},{1,0},{2,3},{3,2},{4,5},{5,4},{6,7},{7,6},{8,9},{9,8},{10,11... | collective-permute-start | bytes 294920 | tf_op jit(solution)/shard_map/ppermute | solution.py:670
  5.2 4.8 %stage.1 = (f32[2,288,384]{2,1,0:T(8,128)S(1)}, f32[512,128]{1,0:T(8,128)S(1)}, f32[8,384]{1,0:T(8,128)S(1)}, f32[8,1536]{1,0:T(8,128)S(1)}, f32[8,128]{1,0:T(8,...) custom-call(bf16[2,16,16,384]{3,2,1,0:T(8,128)(2,1)} %frames_hbm.1, ...), custom_call_target="tpu_custom_call" | custom-call | flops 10000000000 | bytes 4718592 | tf_op jit(solution)/shard_map/stage/pallas_call | solution.py:190
  10.0 0.0 collective-permute-done.1.recv_next
  10.0 0.0 collective-permute-done.recv_pair
  10.0 8.8 %block.1 = (bf16[256,256]{1,0:T(8,128)(2,1)S(1)}, f32[8,256]{1,0:T(8,128)S(1)}, f32[256,256]{1,0:T(8,128)S(1)}, f32[256,256]{1,0:T(8,128)S(1)}, f32[256,256]{1,0...) custom-call(f32[2,288,384]{2,1,0:T(8,128)S(1)} %get-tuple-element.37, ...), custom_call_target="tpu_custom_call" | custom-call | flops 6643777536 | bytes 10616832 | tf_op jit(solution)/shard_map/block/pallas_call | solution.py:469
  18.8 0.7 %collective-permute-start.2 = (bf16[256,256]{1,0:T(8,128)(2,1)S(1)}, bf16[256,256]{1,0:T(8,128)(2,1)S(1)}, u32[]{:S(2)}, u32[]{:S(2)}) collective-permute-start(bf16[256,256]{1,0:T(8,128)(2,1)S(1)} %get-tuple-element.45.send_early), channel_id=1, source_target_pairs={{0,4},{1,5},{2,6},{3,7},{16,20},{17,21},{18,22},{19,23}} | collective-permute-start | bytes 393224 | tf_op jit(solution)/shard_map/ppermute | solution.py:744
  19.5 2.9 %later.1 = (bf16[304,128]{1,0:T(8,128)(2,1)S(1)}, f32[256,128]{1,0:T(8,128)S(1)}, f32[256,128]{1,0:T(8,128)S(1)}, f32[256,128]{1,0:T(8,128)S(1)}, f32[256,128]{1...) custom-call(bf16[512,3456]{1,0:T(8,128)(2,1)S(1)} %get-tuple-element.52.taps, ...), custom_call_target="tpu_custom_call" | custom-call | flops 10000000000 | tf_op jit(solution)/shard_map/later/pallas_call | solution.py:503
  22.4 0.7 %collective-permute-start.4 = (bf16[304,128]{1,0:T(8,128)(2,1)S(1)}, bf16[304,128]{1,0:T(8,128)(2,1)S(1)}, u32[]{:S(2)}, u32[]{:S(2)}) collective-permute-start(bf16[304,128]{1,0:T(8,128)(2,1)S(1)} %get-tuple-element.55.before), channel_id=1, source_target_pairs={{0,4},{1,5},{2,6},{3,7},{16,20},{17,21},{18,22},{19,23}} | collective-permute-start | bytes 233480 | tf_op jit(solution)/shard_map/ppermute | solution.py:745
  23.1 0.0 collective-permute-done.2.arrived.refs_0_
  23.1 0.1 relay.2
  23.3 0.7 %collective-permute-start.3 = (bf16[256,256]{1,0:T(8,128)(2,1)S(1)}, bf16[256,256]{1,0:T(8,128)(2,1)S(1)}, u32[]{:S(2)}, u32[]{:S(2)}) collective-permute-start(bf16[256,256]{1,0:T(8,128)(2,1)S(1)} %get-tuple-element.56), channel_id=1, source_target_pairs={{4,8},{5,9},{6,10},{7,11},{20,24},{21,25},{22,26},{23,27}} | collective-permute-start | bytes 393224 | tf_op jit(solution)/shard_map/ppermute | solution.py:744
  23.9 0.0 collective-permute-done.4.arrived.refs_3_
  23.9 0.3 relay_later.2.before
  24.2 0.7 %collective-permute-start.6 = (bf16[304,128]{1,0:T(8,128)(2,1)S(1)}, bf16[304,128]{1,0:T(8,128)(2,1)S(1)}, u32[]{:S(2)}, u32[]{:S(2)}) collective-permute-start(bf16[304,128]{1,0:T(8,128)(2,1)S(1)} %relay_later.2.before), channel_id=1, source_target_pairs={{4,8},{5,9},{6,10},{7,11},{20,24},{21,25},{22,26},{23,27}} | collective-permute-start | bytes 233480 | tf_op jit(solution)/shard_map/ppermute | solution.py:745
  24.9 0.0 collective-permute-done.3.arrived.refs_1_
  24.9 0.1 relay.3
  25.0 1.3 %collective-permute-start.5 = (bf16[256,256]{1,0:T(8,128)(2,1)S(1)}, bf16[256,256]{1,0:T(8,128)(2,1)S(1)}, u32[]{:S(2)}, u32[]{:S(2)}) collective-permute-start(bf16[256,256]{1,0:T(8,128)(2,1)S(1)} %get-tuple-element.64), channel_id=1, source_target_pairs={{8,12},{9,13},{10,14},{11,15},{24,28},{25,29},{26,30},{27,31}} | collective-permute-start | bytes 393224 | tf_op jit(solution)/shard_map/ppermute | solution.py:744
  26.3 0.0 collective-permute-done.6.arrived.refs_4_
  26.3 0.3 relay_later.3
  26.6 1.3 %collective-permute-start.7 = (bf16[304,128]{1,0:T(8,128)(2,1)S(1)}, bf16[304,128]{1,0:T(8,128)(2,1)S(1)}, u32[]{:S(2)}, u32[]{:S(2)}) collective-permute-start(bf16[304,128]{1,0:T(8,128)(2,1)S(1)} %relay_later.3), channel_id=1, source_target_pairs={{8,12},{9,13},{10,14},{11,15},{24,28},{25,29},{26,30},{27,31}} | collective-permute-start | bytes 233480 | tf_op jit(solution)/shard_map/ppermute | solution.py:745
  27.9 10.1 %collective-permute-done.7.refs_5_ = bf16[304,128]{1,0:T(8,128)(2,1)S(1)} collective-permute-done((bf16[304,128]{1,0:T(8,128)(2,1)S(1)}, bf16[304,128]{1,0:T(8,128)(2,1)S(1)}, u32[]{:S(2)}, u32[]{:S(2)}) %collective-permute-start.7) | collective-permute-done | bytes 77856 | tf_op jit(solution)/shard_map/ppermute | solution.py:745
  38.0 0.0 collective-permute-done.5.refs_2_
  38.0 2.3 %final.1 = (bf16[2,256,384]{2,1,0:T(8,128)(2,1)}, bf16[2,384]{1,0:T(2,128)(2,1)}) custom-call(bf16[256,256]{1,0:T(8,128)(2,1)S(1)} %collective-permute-done.2.arrived.refs_0_, bf16[256,256]{1,0:T(8,128)(2,1)S(1)} %collective-permute-done.3.arrived.refs_1_, bf16[256,256]{1,0:T(8,128)(2,1)S(1)} %collective-permute-done.5.refs_2_, ...), custom_call_target="tpu_custom_call" | custom-call | tf_op jit(solution)/shard_map/final/pallas_call | solution.py:773
Async XLA Ops:
  1.6 8.4 %collective-permute-start.1 = (bf16[2,4,16,384]{3,2,1,0:T(8,128)(2,1)S(1)}, bf16[2,4,16,384]{3,2,1,0:T(8,128)(2,1)S(1)}, u32[]{:S(2)}, u32[]{:S(2)}) collective-permute-start(bf16[2,4,16,384]{3,2,1,0:T(8,128)(2,1)S(1)} %get-tuple-element.72), channel_id=1, source_target_pairs={{1,2},{2,1},{5,6},{6,5},{9,10},{10,9},{13,14},{14,13},{17,18},{18,... | collective-permute-start | bytes 294920 | tf_op jit(solution)/shard_map/ppermute | solution.py:671
  2.3 7.7 %collective-permute-start = (bf16[2,4,16,384]{3,2,1,0:T(8,128)(2,1)S(1)}, bf16[2,4,16,384]{3,2,1,0:T(8,128)(2,1)S(1)}, u32[]{:S(2)}, u32[]{:S(2)}) collective-permute-start(bf16[2,4,16,384]{3,2,1,0:T(8,128)(2,1)S(1)} %get-tuple-element.73), channel_id=1, source_target_pairs={{0,1},{1,0},{2,3},{3,2},{4,5},{5,4},{6,7},{7,6},{8,9},{9,8},{10,11... | collective-permute-start | bytes 294920 | tf_op jit(solution)/shard_map/ppermute | solution.py:670
  18.8 4.3 %collective-permute-start.2 = (bf16[256,256]{1,0:T(8,128)(2,1)S(1)}, bf16[256,256]{1,0:T(8,128)(2,1)S(1)}, u32[]{:S(2)}, u32[]{:S(2)}) collective-permute-start(bf16[256,256]{1,0:T(8,128)(2,1)S(1)} %get-tuple-element.45.send_early), channel_id=1, source_target_pairs={{0,4},{1,5},{2,6},{3,7},{16,20},{17,21},{18,22},{19,23}} | collective-permute-start | bytes 393224 | tf_op jit(solution)/shard_map/ppermute | solution.py:744
  22.4 1.5 %collective-permute-start.4 = (bf16[304,128]{1,0:T(8,128)(2,1)S(1)}, bf16[304,128]{1,0:T(8,128)(2,1)S(1)}, u32[]{:S(2)}, u32[]{:S(2)}) collective-permute-start(bf16[304,128]{1,0:T(8,128)(2,1)S(1)} %get-tuple-element.55.before), channel_id=1, source_target_pairs={{0,4},{1,5},{2,6},{3,7},{16,20},{17,21},{18,22},{19,23}} | collective-permute-start | bytes 233480 | tf_op jit(solution)/shard_map/ppermute | solution.py:745
  23.3 1.6 %collective-permute-start.3 = (bf16[256,256]{1,0:T(8,128)(2,1)S(1)}, bf16[256,256]{1,0:T(8,128)(2,1)S(1)}, u32[]{:S(2)}, u32[]{:S(2)}) collective-permute-start(bf16[256,256]{1,0:T(8,128)(2,1)S(1)} %get-tuple-element.56), channel_id=1, source_target_pairs={{4,8},{5,9},{6,10},{7,11},{20,24},{21,25},{22,26},{23,27}} | collective-permute-start | bytes 393224 | tf_op jit(solution)/shard_map/ppermute | solution.py:744
  24.2 2.1 %collective-permute-start.6 = (bf16[304,128]{1,0:T(8,128)(2,1)S(1)}, bf16[304,128]{1,0:T(8,128)(2,1)S(1)}, u32[]{:S(2)}, u32[]{:S(2)}) collective-permute-start(bf16[304,128]{1,0:T(8,128)(2,1)S(1)} %relay_later.2.before), channel_id=1, source_target_pairs={{4,8},{5,9},{6,10},{7,11},{20,24},{21,25},{22,26},{23,27}} | collective-permute-start | bytes 233480 | tf_op jit(solution)/shard_map/ppermute | solution.py:745
  25.0 13.0 %collective-permute-start.5 = (bf16[256,256]{1,0:T(8,128)(2,1)S(1)}, bf16[256,256]{1,0:T(8,128)(2,1)S(1)}, u32[]{:S(2)}, u32[]{:S(2)}) collective-permute-start(bf16[256,256]{1,0:T(8,128)(2,1)S(1)} %get-tuple-element.64), channel_id=1, source_target_pairs={{8,12},{9,13},{10,14},{11,15},{24,28},{25,29},{26,30},{27,31}} | collective-permute-start | bytes 393224 | tf_op jit(solution)/shard_map/ppermute | solution.py:744
  26.6 11.4 %collective-permute-start.7 = (bf16[304,128]{1,0:T(8,128)(2,1)S(1)}, bf16[304,128]{1,0:T(8,128)(2,1)S(1)}, u32[]{:S(2)}, u32[]{:S(2)}) collective-permute-start(bf16[304,128]{1,0:T(8,128)(2,1)S(1)} %relay_later.3), channel_id=1, source_target_pairs={{8,12},{9,13},{10,14},{11,15},{24,28},{25,29},{26,30},{27,31}} | collective-permute-start | bytes 233480 | tf_op jit(solution)/shard_map/ppermute | solution.py:745

commit v5 on v4

--- a/solution.py
+++ b/solution.py
@@ -23,28 +23,62 @@
     return jnp.maximum(x, 0.0) + jnp.log(1.0 + jnp.exp(-jnp.abs(x)))
 
 
-def gelu(x):
+def gelu_twice(x):
     inner = x * (0.7978845608028654 + (0.7978845608028654 * 0.044715) * (x * x))
-    half = 0.5 * x
-    return half + half * jnp.tanh(inner)
+    return x + x * jnp.tanh(inner)
+
+
+def near_kernel(*refs):
+    count = len(refs) // 2 - 1
+    sources, outs = refs[:count], refs[count : 2 * count]
+    to_pair, to_next, sems = refs[2 * count :]
+    copies = [pltpu.make_async_copy(a, b, sems.at[i]) for i, (a, b) in enumerate(zip(sources, outs))]
+    for copy in copies:
+        copy.start()
+    copies[0].wait()
+    frames = outs[0]
+    bottom = frames.shape[1] - REACH
+    odd = lax.rem(lax.axis_index("tile"), 2)
+    to_pair[...] = frames[:, pl.ds((1 - odd) * bottom, REACH)]
+    to_next[...] = frames[:, pl.ds(odd * bottom, REACH)]
+    for copy in copies[1:]:
+        copy.wait()
+
+
+def run_near(arrays):
+    frames = arrays[0]
+    rim = jax.ShapeDtypeStruct((frames.shape[0], REACH) + frames.shape[2:], frames.dtype)
+    hbm = pl.BlockSpec(memory_space=pltpu.HBM)
+    vmem = pl.BlockSpec(memory_space=pltpu.VMEM)
+    out = pl.pallas_call(
+        near_kernel,
+        name="near",
+        out_shape=[jax.ShapeDtypeStruct(x.shape, x.dtype) for x in arrays] + [rim] * 2,
+        in_specs=[hbm] * len(arrays),
+        out_specs=[vmem] * (len(arrays) + 2),
+        scratch_shapes=[pltpu.SemaphoreType.DMA((len(arrays),))],
+        compiler_params=pltpu.CompilerParams(vmem_limit_bytes=16 * 2**20),
+    )(*[pltpu.with_memory_space_constraint(x, pltpu.HBM) for x in arrays])
+    return out[: len(arrays)], out[-2], out[-1]
 
 
 def stage_kernel(
-    frames_hbm,
-    valid_hbm,
-    days_hbm,
-    dw_hbm,
-    dw_bias_hbm,
-    norm_gain_hbm,
-    norm_shift_hbm,
-    b_expand_hbm,
-    layer_scale_hbm,
-    b_gates_hbm,
-    forget_rate_hbm,
-    attn_gain_hbm,
-    head_slope_hbm,
+    frames,
+    dw_kernel,
+    valid,
+    days,
+    slope_line,
+    b_expand,
+    b_gates,
+    dw_bias,
+    norm_gain,
+    norm_shift,
+    layer_scale,
+    forget_rate,
+    attn_gain,
     w_expand_hbm,
     w_reduce_hbm,
+    w_gates_hbm,
     w_query_hbm,
     w_key_hbm,
     w_value_hbm,
@@ -55,18 +89,12 @@
     long_rows,
     months,
     slope,
-    frames,
-    dw_kernel,
     w_expand,
     w_reduce,
+    w_first,
     w_qkv,
     w_out,
     padded,
-    valid,
-    days,
-    slope_line,
-    short_lines,
-    long_lines,
     sems,
 ):
     epochs, height, width, channels = frames.shape
@@ -74,21 +102,9 @@
     rows = height + 2
     pixels = height * width
     moves = [
-        (frames_hbm, frames),
-        (dw_hbm, dw_kernel),
-        (valid_hbm, valid),
-        (days_hbm, days),
-        (head_slope_hbm, slope_line),
-        (b_expand_hbm, long_lines[0]),
-        (b_gates_hbm, long_lines[1]),
-        (dw_bias_hbm, short_lines[0]),
-        (norm_gain_hbm, short_lines[1]),
-        (norm_shift_hbm, short_lines[2]),
-        (layer_scale_hbm, short_lines[3]),
-        (forget_rate_hbm, short_lines[4]),
-        (attn_gain_hbm, short_lines[5]),
         (w_expand_hbm, w_expand),
         (w_reduce_hbm, w_reduce),
+        (w_gates_hbm.at[:, pl.ds(0, w_first.shape[1])], w_first),
         (w_query_hbm, w_qkv.at[:, pl.ds(0, channels)]),
         (w_key_hbm, w_qkv.at[:, pl.ds(channels, channels)]),
         (w_value_hbm, w_qkv.at[:, pl.ds(2 * channels, channels)]),
@@ -100,14 +116,10 @@
 
     for c in range(groups):
         for e in range(epochs):
+            lanes = slice(c * LANES, (c + 1) * LANES)
             padded[c, e, :, 0:8, :] = jnp.zeros((height, 8, LANES), F32)
             padded[c, e, :, 8 + width : 16 + width, :] = jnp.zeros((height, 8, LANES), F32)
-    copies[0].wait()
-    for c in range(groups):
-        for e in range(epochs):
-            lanes = slice(c * LANES, (c + 1) * LANES)
             padded[c, e, :, 8 : 8 + width, :] = frames[e, :, :, lanes].astype(F32)
-    copies[1].wait()
 
     half = rows // 2
 
@@ -135,12 +147,11 @@
 
     lax.fori_loop(0, groups * epochs, depthwise, 0)
 
-    for copy in copies[2:]:
-        copy.wait()
-    for k in range(6):
-        short_rows[k : k + 1, :] = short_lines[k][...].reshape(1, -1)
-    for k in range(2):
-        long_rows[k : k + 1, :] = long_lines[k][...].reshape(1, -1)
+    short = (dw_bias, norm_gain, norm_shift, layer_scale, forget_rate, attn_gain)
+    for k, line in enumerate(short):
+        short_rows[k : k + 1, :] = line[...].reshape(1, -1)
+    for k, line in enumerate((b_expand, b_gates)):
+        long_rows[k : k + 1, :] = line[...].reshape(1, -1)
     slope[...] = slope_line[...].reshape(1, -1)
     total = days.shape[0]
     eye = lax.broadcasted_iota(jnp.int32, (total, total), 0) == lax.broadcasted_iota(
@@ -161,29 +172,28 @@
         mask[e * pixels : (e + 1) * pixels, :] = jnp.dot(
             jnp.where(place, lines, 0.0).astype(BF16), ones, preferred_element_type=F32
         )
-
-
-def run_stage(frames, valid, days, dw_kernel, short, long, slope, w_expand, w_reduce, w_qkvo):
+    for copy in copies:
+        copy.wait()
+
+
+def run_stage(near, w_expand, w_reduce, w_gates, w_qkvo):
+    frames, dw_kernel, valid, days, slope = near[:5]
     epochs, height, width, channels = frames.shape
     pixels = height * width
     total = days.shape[0]
-    operands = [frames, valid, days, dw_kernel]
-    operands += [short[0], short[1], short[2], long[0], short[3], long[1], short[4], short[5], slope]
-    operands += [w_expand, w_reduce, *w_qkvo]
-    operands = [pltpu.with_memory_space_constraint(x, pltpu.HBM) for x in operands]
+    far = [w_expand, w_reduce, w_gates, *w_qkvo]
     hbm = pl.BlockSpec(memory_space=pltpu.HBM)
     vmem = pl.BlockSpec(memory_space=pltpu.VMEM)
     out_shape = [
         jax.ShapeDtypeStruct((epochs, (height + 2) * width, channels), F32),
         jax.ShapeDtypeStruct((epochs * pixels, LANES), F32),
         jax.ShapeDtypeStruct((8, channels), F32),
-        jax.ShapeDtypeStruct((8, long[0].size), F32),
+        jax.ShapeDtypeStruct((8, w_gates.shape[1]), F32),
         jax.ShapeDtypeStruct((total, LANES), F32),
         jax.ShapeDtypeStruct((1, slope.size), F32),
-        jax.ShapeDtypeStruct(frames.shape, BF16),
-        jax.ShapeDtypeStruct(dw_kernel.shape, F32),
         jax.ShapeDtypeStruct(w_expand.shape, BF16),
         jax.ShapeDtypeStruct(w_reduce.shape, BF16),
+        jax.ShapeDtypeStruct((w_gates.shape[0], 4 * LANES), BF16),
         jax.ShapeDtypeStruct((channels, 3 * channels), BF16),
         jax.ShapeDtypeStruct((channels, channels), BF16),
     ]
@@ -191,22 +201,17 @@
         stage_kernel,
         name="stage",
         out_shape=out_shape,
-        in_specs=[hbm] * len(operands),
+        in_specs=[vmem] * len(near) + [hbm] * len(far),
         out_specs=[vmem] * len(out_shape),
         scratch_shapes=[
             pltpu.VMEM((channels // LANES, epochs, height, width + 16, LANES), F32),
-            pltpu.VMEM(valid.shape, jnp.int32),
-            pltpu.VMEM(days.shape, jnp.int32),
-            pltpu.VMEM(slope.shape, F32),
-            [pltpu.VMEM((channels,), F32)] * 6,
-            [pltpu.VMEM((long[0].size,), F32)] * 2,
-            pltpu.SemaphoreType.DMA((len(operands),)),
+            pltpu.SemaphoreType.DMA((len(far),)),
         ],
         compiler_params=pltpu.CompilerParams(vmem_limit_bytes=24 * 2**20),
         cost_estimate=pl.CostEstimate(
             flops=10**10, bytes_accessed=8 * w_expand.size, transcendentals=0
         ),
-    )(*operands)
+    )(*near, *[pltpu.with_memory_space_constraint(x, pltpu.HBM) for x in far])
 
 
 def block_kernel(
@@ -221,6 +226,7 @@
     dw_kernel,
     w_expand,
     w_reduce,
+    w_first,
     w_gates_hbm,
     send,
     pooled,
@@ -239,19 +245,15 @@
 ):
     epochs, height, width, channels = frames.shape
     groups = channels // LANES
-    hidden = w_expand.shape[1]
     rows = height + 2
     pixels = height * width
     wide = 4 * LANES
 
-    early = w_gates.shape[1] // wide
+    early = send.shape[1] // LANES
+    places = [w_gates.at[j] for j in range(early - 1)] + [w_later.at[j] for j in range(groups - early)]
     gate_copies = [
-        pltpu.make_async_copy(
-            w_gates_hbm.at[:, pl.ds(j * wide, wide)],
-            w_gates.at[:, pl.ds(j * wide, wide)] if j < early else w_later.at[:, pl.ds((j - early) * wide, wide)],
-            sems.at[j],
-        )
-        for j in range(groups)
+        pltpu.make_async_copy(w_gates_hbm.at[:, pl.ds((j + 1) * wide, wide)], place, sems.at[j])
+        for j, place in enumerate(places)
     ]
     for copy in gate_copies:
         copy.start()
@@ -259,7 +261,7 @@
     dw_bias = short_rows[0:1, :]
     norm_gain = short_rows[1:2, :]
     norm_shift = short_rows[2:3, :]
-    layer_scale = short_rows[3:4, :]
+    half_scale = 0.5 * short_rows[3:4, :]
     b_expand = long_rows[0:1, :]
 
     me = lax.axis_index("tile")
@@ -322,12 +324,8 @@
         centred = values - center
         variance = jnp.mean(centred * centred, axis=-1, keepdims=True)
         normed = (centred * lax.rsqrt(variance + 1e-06) * norm_gain + norm_shift).astype(BF16)
-        reduced = None
-        for k in range(hidden // 512):
-            cols = slice(k * 512, (k + 1) * 512)
-            grown = jnp.dot(normed, w_expand[:, cols], preferred_element_type=F32) + b_expand[:, cols]
-            part = jnp.dot(gelu(grown).astype(BF16), w_reduce[cols, :], preferred_element_type=F32)
-            reduced = part if reduced is None else reduced + part
+        grown = jnp.dot(normed, w_expand[...], preferred_element_type=F32) + b_expand
+        reduced = jnp.dot(gelu_twice(grown).astype(BF16), w_reduce[...], preferred_element_type=F32)
         for c in range(groups):
             lanes = slice(c * LANES, (c + 1) * LANES)
             centre = jnp.concatenate(
@@ -338,7 +336,7 @@
                 ],
                 axis=0,
             )
-            feature = centre + layer_scale[:, lanes] * reduced[:, lanes]
+            feature = centre + half_scale[:, lanes] * reduced[:, lanes]
             feature = (feature * inside).astype(BF16).astype(F32)
             before = jnp.where(across == 0, 0.0, pltpu.roll(feature, 1, 0))
             after = jnp.where(across == width - 1, 0.0, pltpu.roll(feature, count - 1, 0))
@@ -350,59 +348,61 @@
                         oy * width : oy * width + pixels
                     ]
 
-    for j in range(early):
-        gate_copies[j].wait()
-    cells_of(
-        range(early), 0, taps, w_gates, mask, short_rows, long_rows,
-        send, pooled, (decay0, inflow0, keep, block, open0, open1),
-    )
-    for copy in gate_copies[early:]:
+    state = (decay0, inflow0, keep, block, open0, open1)
+    cells_of(0, 0, taps, w_first, mask, short_rows, long_rows, send, pooled, state)
+    for j in range(1, early):
+        gate_copies[j - 1].wait()
+        cells_of(j, j, taps, w_gates.at[j - 1], mask, short_rows, long_rows, send, pooled, state)
+    for copy in gate_copies[early - 1 :]:
         copy.wait()
 
 
-def cells_of(parts, first, taps, w_gates, mask, short_rows, long_rows, send, pooled, state):
+def gates_of(preact):
+    quarter = LANES // 4
+    lane = lax.broadcasted_iota(jnp.int32, (preact.shape[0], LANES), 1)
+    spot = lane // quarter
+    within = lane - spot * quarter
+    sorted_ = []
+    for i in range(4):
+        gate = lax.rem(spot - i + 4, 4)
+        sorted_.append(
+            jnp.take_along_axis(preact[:, i * LANES : (i + 1) * LANES], 4 * within + gate, axis=1)
+        )
+    gates = []
+    for g in range(4):
+        out = sorted_[0]
+        for i in range(1, 4):
+            out = jnp.where(spot == (g + i) % 4, sorted_[i], out)
+        gates.append(out if g == 0 else pltpu.roll(out, LANES - g * quarter, 1))
+    return gates
+
+
+def cells_of(j, at, taps, weights, mask, short_rows, long_rows, send, pooled, state):
     decay0, inflow0, keep, block, open0, open1 = state
     pixels = keep.shape[0]
-    wide = 4 * LANES
-    quarter = LANES // 4
-    lane = lax.broadcasted_iota(jnp.int32, mask.shape, 1)
-    spot = lane // quarter
-    within = lane - spot * quarter
-    good = mask[...] > 0.5
-    for j in parts:
-        cols = slice((j - first) * wide, (j - first + 1) * wide)
-        lanes = slice((j - first) * LANES, (j - first + 1) * LANES)
-        bias = long_rows[1:2, j * wide : (j + 1) * wide]
-        rate = short_rows[4:5, j * LANES : (j + 1) * LANES]
-        preact = jnp.dot(taps[...], w_gates[:, cols], preferred_element_type=F32) + bias
-        sorted_ = []
-        for i in range(4):
-            gate = lax.rem(spot - i + 4, 4)
-            sorted_.append(
-                jnp.take_along_axis(preact[:, i * LANES : (i + 1) * LANES], 4 * within + gate, axis=1)
-            )
-        gates = []
-        for g in range(4):
-            out = sorted_[0]
-            for i in range(1, 4):
-                out = jnp.where(spot == (g + i) % 4, sorted_[i], out)
-            gates.append(out if g == 0 else pltpu.roll(out, LANES - g * quarter, 1))
-        gate_in, gate_keep, gate_new, gate_out = gates
+    lanes = slice(at * LANES, (at + 1) * LANES)
+    bias = long_rows[1:2, j * 4 * LANES : (j + 1) * 4 * LANES]
+    rate = short_rows[4:5, j * LANES : (j + 1) * LANES]
+    cell = None
+    for e, opens in enumerate((open0, open1)):
+        rows = slice(e * pixels, (e + 1) * pixels)
+        preact = jnp.dot(taps[rows, :], weights[...], preferred_element_type=F32) + bias
+        gate_in, gate_keep, gate_new, gate_out = gates_of(preact)
+        good = mask[rows, :] > 0.5
         decay = jnp.where(good, jnp.exp(-rate * softplus(gate_keep)), 1.0)
         inflow = jnp.where(good, sigmoid(gate_in) * jnp.tanh(gate_new), 0.0)
         opened = sigmoid(gate_out)
-        d0, d1 = decay[:pixels], decay[pixels:]
-        i0, i1 = inflow[:pixels], inflow[pixels:]
-        decay0[:, lanes] = d0
-        inflow0[:, lanes] = i0
-        keep[:, lanes] = d0 * d1
-        total = d1 * i0 + i1
-        block[:, lanes] = total
-        send[:pixels, lanes] = total.astype(BF16)
-        open0[:, lanes] = opened[:pixels]
-        open1[:, lanes] = opened[pixels:]
-        pooled[0:1, lanes] = pool(opened[:pixels] * jnp.tanh(i0))
-        pooled[1:2, lanes] = pool(opened[pixels:] * jnp.tanh(total))
+        opens[:, lanes] = opened
+        if e == 0:
+            decay0[:, lanes] = decay
+            inflow0[:, lanes] = inflow
+            cell = inflow
+        else:
+            keep[:, lanes] = decay0[:, lanes] * decay
+            cell = decay * inflow0[:, lanes] + inflow
+            block[:, lanes] = cell
+            send[:pixels, lanes] = cell.astype(BF16)
+        pooled[e : e + 1, lanes] = pool(opened * jnp.tanh(cell))
 
 
 def later_kernel(
@@ -424,10 +424,10 @@
     pooled,
 ):
     channels = short_rows.shape[1]
-    cells_of(
-        range(first, channels // LANES), first, taps, w_gates, mask, short_rows, long_rows,
-        send, pooled, (decay0, inflow0, keep, block, open0, open1),
-    )
+    state = (decay0, inflow0, keep, block, open0, open1)
+    for j in range(first, channels // LANES):
+        at = j - first
+        cells_of(j, at, taps, w_gates.at[at], mask, short_rows, long_rows, send, pooled, state)
     pixels = keep.shape[0]
     both = jnp.concatenate([pooled_early[0:2, :], pooled[0:2, :]], axis=1)
     own = tokens_of(both, short_rows[5:6, :])
@@ -453,7 +453,7 @@
 
 
 def run_block(tiles, early, staged, recv_pair, recv_next, w_gates, tail):
-    spread, mask, short_rows, long_rows, frames, dw_kernel, w_expand, w_reduce = staged
+    spread, mask, short_rows, long_rows, frames, dw_kernel, w_expand, w_reduce, w_first = staged
     epochs, height, width, channels = frames.shape
     pixels = height * width
     depth = w_gates.shape[0]
@@ -474,15 +474,15 @@
             jax.ShapeDtypeStruct((8, near), F32),
             *state(near),
             jax.ShapeDtypeStruct((epochs * pixels, depth), BF16),
-            jax.ShapeDtypeStruct((depth, 4 * far), BF16),
+            jax.ShapeDtypeStruct((far // LANES, depth, 4 * LANES), BF16),
         ],
-        in_specs=[vmem] * 10 + [hbm],
+        in_specs=[vmem] * 11 + [hbm],
         out_specs=[vmem] * 10,
         scratch_shapes=[
             pltpu.VMEM((channels // LANES, epochs, 2 * REACH, width + 16, LANES), F32),
             pltpu.VMEM((epochs, 2 * REACH * width, channels), F32),
-            pltpu.VMEM((depth, 4 * near), BF16),
-            pltpu.SemaphoreType.DMA((channels // LANES,)),
+            pltpu.VMEM((max(1, early - 1), depth, 4 * LANES), BF16),
+            pltpu.SemaphoreType.DMA((channels // LANES - 1,)),
         ],
         compiler_params=pltpu.CompilerParams(vmem_limit_bytes=32 * 2**20),
         cost_estimate=pl.CostEstimate(flops=flops, bytes_accessed=2 * w_gates.size, transcendentals=0),
@@ -497,6 +497,7 @@
         dw_kernel,
         w_expand,
         w_reduce,
+        w_first,
         pltpu.with_memory_space_constraint(w_gates, pltpu.HBM),
     )
     *state_near, taps, w_later = rest
@@ -601,27 +602,45 @@
     queries = qkv[:, :channels]
     keys = qkv[:, channels : 2 * channels]
     values = qkv[:, 2 * channels :]
-    line = lax.broadcasted_iota(jnp.int32, (total, channels), 0)
     member = lax.broadcasted_iota(jnp.int32, (channels, heads), 0) // depth
     head_of = jnp.where(member == lax.broadcasted_iota(jnp.int32, (channels, heads), 1), 1.0, 0.0)
     member_t = lax.broadcasted_iota(jnp.int32, (heads, channels), 1) // depth
     channel_of = jnp.where(
         member_t == lax.broadcasted_iota(jnp.int32, (heads, channels), 0), 1.0, 0.0
     )
+
+    def exact_dot(x, zero_one):
+        high = x.astype(BF16)
+        rest = x - high.astype(F32)
+        low = rest.astype(BF16)
+        least = (rest - low.astype(F32)).astype(BF16)
+        out = jnp.dot(
+            jnp.concatenate([high, low, least], axis=0), zero_one.astype(BF16), preferred_element_type=F32
+        )
+        count = x.shape[0]
+        return out[:count] + out[count : 2 * count] + out[2 * count :]
+
+    line = lax.broadcasted_iota(jnp.int32, (total, channels), 0)
     key_index = lax.broadcasted_iota(jnp.int32, (total, heads), 0)
     month = months[:, :heads]
-    results = []
-    for step in range(2):
-        mine = 2 * stage + step
+    places = [epochs * stage + step for step in range(epochs)]
+    products = []
+    for mine in places:
         query = jnp.sum(jnp.where(line == mine, queries, 0.0), axis=0, keepdims=True)
-        raw = jnp.dot(query * keys, head_of, preferred_element_type=F32, precision=lax.Precision.HIGHEST)
+        products.append(query * keys)
+    raw = exact_dot(jnp.concatenate(products, axis=0), head_of)
+    weights = []
+    for step, mine in enumerate(places):
         now = jnp.sum(jnp.where(key_index == mine, month, 0.0), axis=0, keepdims=True)
-        scores = raw / math.sqrt(depth) - slope[...] * (now - month)
+        scores = raw[step * total : (step + 1) * total] / math.sqrt(depth) - slope[...] * (now - month)
         scores = jnp.where(key_index <= mine, scores, -1e30)
         expo = jnp.exp(scores - jnp.max(scores, axis=0, keepdims=True))
-        weights = expo / jnp.sum(expo, axis=0, keepdims=True)
-        spread = jnp.dot(weights, channel_of, preferred_element_type=F32, precision=lax.Precision.HIGHEST)
-        results.append(jnp.sum(spread * values, axis=0, keepdims=True))
+        weights.append(expo / jnp.sum(expo, axis=0, keepdims=True))
+    wide = exact_dot(jnp.concatenate(weights, axis=0), channel_of)
+    results = [
+        jnp.sum(wide[step * total : (step + 1) * total] * values, axis=0, keepdims=True)
+        for step in range(epochs)
+    ]
     mixed = jnp.concatenate(results, axis=0).astype(BF16)
     change[...] = jnp.dot(mixed, w_out[...], preferred_element_type=F32).astype(BF16)
     for copy in copies:
@@ -664,11 +683,26 @@
     stages = lax.axis_size("epoch")
     total = epochs * stages
     tail = -(-total // 16) * 16
-    even = lax.rem(lax.axis_index("tile"), 2) == 0
-    top = frames[:, :REACH]
-    bottom = frames[:, height - REACH :]
-    recv_pair = lax.ppermute(jnp.where(even, bottom, top), "tile", pairs(tiles, 0))
-    recv_next = lax.ppermute(jnp.where(even, top, bottom), "tile", pairs(tiles, 1))
+    gate_weights = w_gates.reshape(9 * channels, -1)
+    near, to_pair, to_next = run_near(
+        [
+            frames,
+            dw_kernel,
+            valid,
+            days,
+            head_slope,
+            b_expand,
+            b_gates,
+            dw_bias,
+            norm_gain,
+            norm_shift,
+            layer_scale,
+            forget_rate,
+            attn_gain,
+        ]
+    )
+    recv_pair = lax.ppermute(to_pair, "tile", pairs(tiles, 0))
+    recv_next = lax.ppermute(to_next, "tile", pairs(tiles, 1))
     (
         spread,
         mask,
@@ -676,32 +710,30 @@
         long_rows,
         months,
         slope,
-        frames_near,
-        dw_near,
         expand_near,
         reduce_near,
+        w_first,
         qkv_near,
         out_near,
-    ) = run_stage(
-        frames,
-        valid,
-        days,
-        dw_kernel,
-        [dw_bias, norm_gain, norm_shift, layer_scale, forget_rate, attn_gain],
-        [b_expand, b_gates],
-        head_slope,
-        w_expand,
-        w_reduce,
-        [w_query, w_key, w_value, w_out],
-    )
+    ) = run_stage(near, w_expand, w_reduce, gate_weights, [w_query, w_key, w_value, w_out])
     early = max(1, channels // LANES - 1)
-    (send, near), (send_far, far) = run_block(
+    (send, state_near), (send_far, state_far) = run_block(
         tiles,
         early,
-        (spread, mask, short_rows, long_rows, frames_near, dw_near, expand_near, reduce_near),
+        (
+            spread,
+            mask,
+            short_rows,
+            long_rows,
+            near[0],
+            near[1],
+            expand_near,
+            reduce_near,
+            w_first,
+        ),
         recv_pair,
         recv_next,
-        w_gates.reshape(9 * channels, -1),
+        gate_weights,
         tail,
     )
     vmem = pl.BlockSpec(memory_space=pltpu.VMEM)
@@ -720,7 +752,7 @@
             out_specs=[vmem] * 2,
             compiler_params=params,
             cost_estimate=cost,
-        )(arrived, *near, before)
+        )(arrived, *state_near, before)
 
     def relay_later(stage, arrived, pooled):
         return pl.pallas_call(
@@ -731,7 +763,7 @@
             out_specs=vmem,
             compiler_params=params,
             cost_estimate=cost,
-        )(arrived, *far, pooled, short_rows)
+        )(arrived, *state_far, pooled, short_rows)
 
     arrived = []
     arrived_far = []
@@ -759,8 +791,8 @@
             parts = jnp.split(tokens, channels // LANES, axis=1)
             return jnp.concatenate(parts, axis=0)
 
-        incoming = along(near, early * LANES)
-        incoming_far = along(far, channels - early * LANES)
+        incoming = along(state_near, early * LANES)
+        incoming_far = along(state_far, channels - early * LANES)
         _, pooled = relay(incoming, send_far)
         blank = jnp.zeros((tail * channels // LANES, LANES), BF16)
         told = relay_later(0, jnp.concatenate([incoming_far, blank]), pooled)[pixels:]
@@ -784,7 +816,7 @@
             pltpu.SemaphoreType.DMA((epochs,)),
         ],
         compiler_params=pltpu.CompilerParams(vmem_limit_bytes=24 * 2**20),
-    )(*arrived, *arrived_far, *near, *far, short_rows, months, slope, qkv_near, out_near)
+    )(*arrived, *arrived_far, *state_near, *state_far, short_rows, months, slope, qkv_near, out_near)
     return (
         memory.reshape(epochs, height, width, channels),
         change.reshape(epochs, 1, 1, channels),

time: 40.6 us -> 37.9 us (0.933)
  the two profiles are of different devices: /device:TPU:24 before, /device:TPU:30 now
where the time goes in v5:
time: 37.9 us; the launch traced here: 37.7 us
  Pallas kernels  18.9 us (50%)
  waiting for transfers between devices  10.2 us (27%)
  starting transfers between devices  7.84 us (21%)
  between operations  0.79 us (2%)
    ppermute x3, waiting for transfers between devices, body(): arrived_far.append(lax.ppermute(send_far, 'epoch', link))  10.2 us
    pallas_call x1, Pallas kernels, run_block(): pl.pallas_call(functools.partial(block_kernel, tiles), name='block', out_...  8.16 us
    pallas_call x1, Pallas kernels, run_stage(): pl.pallas_call(stage_kernel, name='stage', out_shape=out_shape, in_specs=...  3.73 us
    pallas_call x1, Pallas kernels, run_block(): pl.pallas_call(functools.partial(later_kernel, early), name='later', out_...  2.68 us
    ppermute x3, starting transfers between devices, body(): arrived.append(lax.ppermute(send, 'epoch', link))  2.63 us
    ppermute x3, starting transfers between devices, body(): arrived_far.append(lax.ppermute(send_far, 'epoch', link))  2.61 us
    ppermute x1, starting transfers between devices, body(): recv_next = lax.ppermute(to_next, 'tile', pairs(tiles, 1))  2.53 us
    pallas_call x1, Pallas kernels, body(): pl.pallas_call(functools.partial(final_kernel, len(arrived)), name='final...  2.33 us
  transfers between devices with their start and end apart: 8, of which 1 were waited for; matrix products, arithmetic and copies ran while one was open for 0% of the time, Pallas kernels for 19%

profile of v5, /device:TPU:30, one launch (start us, length us, event | category | flops | bytes accessed | tf_op | source)
XLA Modules:
  0.0 37.7 jit_solution(15599403458765605548)
XLA Ops:
  0.6 1.2 %near.1 = (bf16[2,16,16,384]{3,2,1,0:T(8,128)(2,1)S(1)}, f32[7,7,384]{2,1,0:T(8,128)S(1)}, s32[2,16,16]{2,1,0:T(8,128)S(1)}, s32[8]{0:T(128)S(1)}, f32[8]{0:T(12...) custom-call(bf16[2,16,16,384]{3,2,1,0:T(8,128)(2,1)} %refs_0_.1, ...), custom_call_target="tpu_custom_call" | custom-call | tf_op jit(solution)/shard_map/near/pallas_call | solution.py:53
  1.8 0.1 collective-permute-start
  1.9 2.5 %collective-permute-start.1 = (bf16[2,4,16,384]{3,2,1,0:T(8,128)(2,1)S(1)}, bf16[2,4,16,384]{3,2,1,0:T(8,128)(2,1)S(1)}, u32[]{:S(2)}, u32[]{:S(2)}) collective-permute-start(bf16[2,4,16,384]{3,2,1,0:T(8,128)(2,1)S(1)} %get-tuple-element.66), channel_id=1, source_target_pairs={{1,2},{2,1},{5,6},{6,5},{9,10},{10,9},{13,14},{14,13},{17,18},{18,... | collective-permute-start | bytes 294920 | tf_op jit(solution)/shard_map/ppermute | solution.py:705
  4.4 3.7 %stage.1 = (f32[2,288,384]{2,1,0:T(8,128)S(1)}, f32[512,128]{1,0:T(8,128)S(1)}, f32[8,384]{1,0:T(8,128)S(1)}, f32[8,1536]{1,0:T(8,128)S(1)}, f32[8,128]{1,0:T(8,...) custom-call(bf16[2,16,16,384]{3,2,1,0:T(8,128)(2,1)S(1)} %get-tuple-, ...), custom_call_target="tpu_custom_call" | custom-call | flops 10000000000 | bytes 4718592 | tf_op jit(solution)/shard_map/stage/pallas_call | solution.py:200
  8.2 0.0 collective-permute-done.recv_pair
  8.2 0.0 collective-permute-done.1.recv_next
  8.2 8.2 %block.1 = (bf16[256,256]{1,0:T(8,128)(2,1)S(1)}, f32[8,256]{1,0:T(8,128)S(1)}, f32[256,256]{1,0:T(8,128)S(1)}, f32[256,256]{1,0:T(8,128)S(1)}, f32[256,256]{1,0...) custom-call(f32[2,288,384]{2,1,0:T(8,128)S(1)} %get-tuple-element.64, ...), custom_call_target="tpu_custom_call" | custom-call | flops 6643777536 | bytes 10616832 | tf_op jit(solution)/shard_map/block/pallas_call | solution.py:469
  16.3 0.7 %collective-permute-start.2 = (bf16[256,256]{1,0:T(8,128)(2,1)S(1)}, bf16[256,256]{1,0:T(8,128)(2,1)S(1)}, u32[]{:S(2)}, u32[]{:S(2)}) collective-permute-start(bf16[256,256]{1,0:T(8,128)(2,1)S(1)} %get-tuple-element.73.send_early), channel_id=1, source_target_pairs={{0,4},{1,5},{2,6},{3,7},{16,20},{17,21},{18,22},{19,23}} | collective-permute-start | bytes 393224 | tf_op jit(solution)/shard_map/ppermute | solution.py:776
  17.0 2.7 %later.1 = (bf16[304,128]{1,0:T(8,128)(2,1)S(1)}, f32[256,128]{1,0:T(8,128)S(1)}, f32[256,128]{1,0:T(8,128)S(1)}, f32[256,128]{1,0:T(8,128)S(1)}, f32[256,128]{1...) custom-call(bf16[512,3456]{1,0:T(8,128)(2,1)S(1)} %get-tuple-element.80.taps, ...), custom_call_target="tpu_custom_call" | custom-call | flops 10000000000 | tf_op jit(solution)/shard_map/later/pallas_call | solution.py:504
  19.7 0.7 %collective-permute-start.4 = (bf16[304,128]{1,0:T(8,128)(2,1)S(1)}, bf16[304,128]{1,0:T(8,128)(2,1)S(1)}, u32[]{:S(2)}, u32[]{:S(2)}) collective-permute-start(bf16[304,128]{1,0:T(8,128)(2,1)S(1)} %get-tuple-element.83.before), channel_id=1, source_target_pairs={{0,4},{1,5},{2,6},{3,7},{16,20},{17,21},{18,22},{19,23}} | collective-permute-start | bytes 233480 | tf_op jit(solution)/shard_map/ppermute | solution.py:777
  20.4 0.0 collective-permute-done.2.arrived.refs_0_
  20.4 0.1 relay.2
  20.5 0.7 %collective-permute-start.3 = (bf16[256,256]{1,0:T(8,128)(2,1)S(1)}, bf16[256,256]{1,0:T(8,128)(2,1)S(1)}, u32[]{:S(2)}, u32[]{:S(2)}) collective-permute-start(bf16[256,256]{1,0:T(8,128)(2,1)S(1)} %get-tuple-element.84), channel_id=1, source_target_pairs={{4,8},{5,9},{6,10},{7,11},{20,24},{21,25},{22,26},{23,27}} | collective-permute-start | bytes 393224 | tf_op jit(solution)/shard_map/ppermute | solution.py:776
  21.2 0.0 collective-permute-done.4.arrived.refs_3_
  21.2 0.3 relay_later.2.before
  21.5 0.7 %collective-permute-start.6 = (bf16[304,128]{1,0:T(8,128)(2,1)S(1)}, bf16[304,128]{1,0:T(8,128)(2,1)S(1)}, u32[]{:S(2)}, u32[]{:S(2)}) collective-permute-start(bf16[304,128]{1,0:T(8,128)(2,1)S(1)} %relay_later.2.before), channel_id=1, source_target_pairs={{4,8},{5,9},{6,10},{7,11},{20,24},{21,25},{22,26},{23,27}} | collective-permute-start | bytes 233480 | tf_op jit(solution)/shard_map/ppermute | solution.py:777
  22.1 0.0 collective-permute-done.3.arrived.refs_1_
  22.2 0.1 relay.3
  22.3 1.3 %collective-permute-start.5 = (bf16[256,256]{1,0:T(8,128)(2,1)S(1)}, bf16[256,256]{1,0:T(8,128)(2,1)S(1)}, u32[]{:S(2)}, u32[]{:S(2)}) collective-permute-start(bf16[256,256]{1,0:T(8,128)(2,1)S(1)} %get-tuple-element.92), channel_id=1, source_target_pairs={{8,12},{9,13},{10,14},{11,15},{24,28},{25,29},{26,30},{27,31}} | collective-permute-start | bytes 393224 | tf_op jit(solution)/shard_map/ppermute | solution.py:776
  23.6 0.0 collective-permute-done.6.arrived.refs_4_
  23.6 0.3 relay_later.3
  23.9 1.3 %collective-permute-start.7 = (bf16[304,128]{1,0:T(8,128)(2,1)S(1)}, bf16[304,128]{1,0:T(8,128)(2,1)S(1)}, u32[]{:S(2)}, u32[]{:S(2)}) collective-permute-start(bf16[304,128]{1,0:T(8,128)(2,1)S(1)} %relay_later.3), channel_id=1, source_target_pairs={{8,12},{9,13},{10,14},{11,15},{24,28},{25,29},{26,30},{27,31}} | collective-permute-start | bytes 233480 | tf_op jit(solution)/shard_map/ppermute | solution.py:777
  25.2 10.1 %collective-permute-done.7.refs_5_ = bf16[304,128]{1,0:T(8,128)(2,1)S(1)} collective-permute-done((bf16[304,128]{1,0:T(8,128)(2,1)S(1)}, bf16[304,128]{1,0:T(8,128)(2,1)S(1)}, u32[]{:S(2)}, u32[]{:S(2)}) %collective-permute-start.7) | collective-permute-done | bytes 77856 | tf_op jit(solution)/shard_map/ppermute | solution.py:777
  35.3 0.0 collective-permute-done.5.refs_2_
  35.3 2.3 %final.1 = (bf16[2,256,384]{2,1,0:T(8,128)(2,1)}, bf16[2,384]{1,0:T(2,128)(2,1)}) custom-call(bf16[256,256]{1,0:T(8,128)(2,1)S(1)} %collective-permute-done.2.arrived.refs_0_, bf16[256,256]{1,0:T(8,128)(2,1)S(1)} %collective-permute-done.3.arrived.refs_1_, bf16[256,256]{1,0:T(8,128)(2,1)S(1)} %collective-permute-done.5.refs_2_, ...), custom_call_target="tpu_custom_call" | custom-call | tf_op jit(solution)/shard_map/final/pallas_call | solution.py:805
Async XLA Ops:
  1.8 6.4 %collective-permute-start = (bf16[2,4,16,384]{3,2,1,0:T(8,128)(2,1)S(1)}, bf16[2,4,16,384]{3,2,1,0:T(8,128)(2,1)S(1)}, u32[]{:S(2)}, u32[]{:S(2)}) collective-permute-start(bf16[2,4,16,384]{3,2,1,0:T(8,128)(2,1)S(1)} %get-tuple-element.65), channel_id=1, source_target_pairs={{0,1},{1,0},{2,3},{3,2},{4,5},{5,4},{6,7},{7,6},{8,9},{9,8},{10,11... | collective-permute-start | bytes 294920 | tf_op jit(solution)/shard_map/ppermute | solution.py:704
  1.9 6.3 %collective-permute-start.1 = (bf16[2,4,16,384]{3,2,1,0:T(8,128)(2,1)S(1)}, bf16[2,4,16,384]{3,2,1,0:T(8,128)(2,1)S(1)}, u32[]{:S(2)}, u32[]{:S(2)}) collective-permute-start(bf16[2,4,16,384]{3,2,1,0:T(8,128)(2,1)S(1)} %get-tuple-element.66), channel_id=1, source_target_pairs={{1,2},{2,1},{5,6},{6,5},{9,10},{10,9},{13,14},{14,13},{17,18},{18,... | collective-permute-start | bytes 294920 | tf_op jit(solution)/shard_map/ppermute | solution.py:705
  16.3 4.0 %collective-permute-start.2 = (bf16[256,256]{1,0:T(8,128)(2,1)S(1)}, bf16[256,256]{1,0:T(8,128)(2,1)S(1)}, u32[]{:S(2)}, u32[]{:S(2)}) collective-permute-start(bf16[256,256]{1,0:T(8,128)(2,1)S(1)} %get-tuple-element.73.send_early), channel_id=1, source_target_pairs={{0,4},{1,5},{2,6},{3,7},{16,20},{17,21},{18,22},{19,23}} | collective-permute-start | bytes 393224 | tf_op jit(solution)/shard_map/ppermute | solution.py:776
  19.7 1.5 %collective-permute-start.4 = (bf16[304,128]{1,0:T(8,128)(2,1)S(1)}, bf16[304,128]{1,0:T(8,128)(2,1)S(1)}, u32[]{:S(2)}, u32[]{:S(2)}) collective-permute-start(bf16[304,128]{1,0:T(8,128)(2,1)S(1)} %get-tuple-element.83.before), channel_id=1, source_target_pairs={{0,4},{1,5},{2,6},{3,7},{16,20},{17,21},{18,22},{19,23}} | collective-permute-start | bytes 233480 | tf_op jit(solution)/shard_map/ppermute | solution.py:777
  20.5 1.6 %collective-permute-start.3 = (bf16[256,256]{1,0:T(8,128)(2,1)S(1)}, bf16[256,256]{1,0:T(8,128)(2,1)S(1)}, u32[]{:S(2)}, u32[]{:S(2)}) collective-permute-start(bf16[256,256]{1,0:T(8,128)(2,1)S(1)} %get-tuple-element.84), channel_id=1, source_target_pairs={{4,8},{5,9},{6,10},{7,11},{20,24},{21,25},{22,26},{23,27}} | collective-permute-start | bytes 393224 | tf_op jit(solution)/shard_map/ppermute | solution.py:776
  21.5 2.1 %collective-permute-start.6 = (bf16[304,128]{1,0:T(8,128)(2,1)S(1)}, bf16[304,128]{1,0:T(8,128)(2,1)S(1)}, u32[]{:S(2)}, u32[]{:S(2)}) collective-permute-start(bf16[304,128]{1,0:T(8,128)(2,1)S(1)} %relay_later.2.before), channel_id=1, source_target_pairs={{4,8},{5,9},{6,10},{7,11},{20,24},{21,25},{22,26},{23,27}} | collective-permute-start | bytes 233480 | tf_op jit(solution)/shard_map/ppermute | solution.py:777
  22.3 13.0 %collective-permute-start.5 = (bf16[256,256]{1,0:T(8,128)(2,1)S(1)}, bf16[256,256]{1,0:T(8,128)(2,1)S(1)}, u32[]{:S(2)}, u32[]{:S(2)}) collective-permute-start(bf16[256,256]{1,0:T(8,128)(2,1)S(1)} %get-tuple-element.92), channel_id=1, source_target_pairs={{8,12},{9,13},{10,14},{11,15},{24,28},{25,29},{26,30},{27,31}} | collective-permute-start | bytes 393224 | tf_op jit(solution)/shard_map/ppermute | solution.py:776
  23.9 11.4 %collective-permute-start.7 = (bf16[304,128]{1,0:T(8,128)(2,1)S(1)}, bf16[304,128]{1,0:T(8,128)(2,1)S(1)}, u32[]{:S(2)}, u32[]{:S(2)}) collective-permute-start(bf16[304,128]{1,0:T(8,128)(2,1)S(1)} %relay_later.3), channel_id=1, source_target_pairs={{8,12},{9,13},{10,14},{11,15},{24,28},{25,29},{26,30},{27,31}} | collective-permute-start | bytes 233480 | tf_op jit(solution)/shard_map/ppermute | solution.py:777

commit v6 on v5

--- a/solution.py
+++ b/solution.py
@@ -214,7 +214,24 @@
     )(*near, *[pltpu.with_memory_space_constraint(x, pltpu.HBM) for x in far])
 
 
-def block_kernel(
+FIRST, REST, ALL = 0, 1, 2
+
+
+def on_devices(turn, work):
+    if turn == ALL:
+        work()
+    else:
+        mine = (lax.axis_index("epoch") == 0) == (turn == FIRST)
+        pl.when(mine)(work)
+
+
+def block_kernel(tiles, turn, count, *refs):
+    ins = refs[:12]
+    outs = refs[count:]
+    on_devices(turn, lambda: block_work(tiles, *ins, *outs))
+
+
+def block_work(
     tiles,
     spread,
     recv_pair,
@@ -405,7 +422,11 @@
         pooled[e : e + 1, lanes] = pool(opened * jnp.tanh(cell))
 
 
-def later_kernel(
+def later_kernel(first, turn, count, *refs):
+    on_devices(turn, lambda: later_work(first, *refs[:7], *refs[count:]))
+
+
+def later_work(
     first,
     taps,
     w_gates,
@@ -452,22 +473,24 @@
     return jnp.concatenate(parts, axis=1)
 
 
-def run_block(tiles, early, staged, recv_pair, recv_next, w_gates, tail):
+def run_block(tiles, early, turn, staged, recv_pair, recv_next, w_gates, tail, before):
     spread, mask, short_rows, long_rows, frames, dw_kernel, w_expand, w_reduce, w_first = staged
     epochs, height, width, channels = frames.shape
     pixels = height * width
     depth = w_gates.shape[0]
     vmem = pl.BlockSpec(memory_space=pltpu.VMEM)
     hbm = pl.BlockSpec(memory_space=pltpu.HBM)
+    anywhere = pl.BlockSpec(memory_space=pl.ANY)
     near = early * LANES
     far = channels - near
 
     def state(lanes):
         return [jax.ShapeDtypeStruct((pixels, lanes), F32)] * 6
 
+    kept = [] if before is None else [*before[0][1], before[1][0]]
     flops = 2 * epochs * pixels * (2 * w_expand.size + w_gates.size)
     send, pooled, *rest = pl.pallas_call(
-        functools.partial(block_kernel, tiles),
+        functools.partial(block_kernel, tiles, turn, 12 + len(kept)),
         name="block",
         out_shape=[
             jax.ShapeDtypeStruct((pixels, near), BF16),
@@ -476,15 +499,16 @@
             jax.ShapeDtypeStruct((epochs * pixels, depth), BF16),
             jax.ShapeDtypeStruct((far // LANES, depth, 4 * LANES), BF16),
         ],
-        in_specs=[vmem] * 11 + [hbm],
+        in_specs=[vmem] * 11 + [hbm] + [vmem] * (len(kept) - 1) + [anywhere] * min(1, len(kept)),
         out_specs=[vmem] * 10,
+        input_output_aliases={12 + k: 2 + k for k in range(len(kept) - 1)},
         scratch_shapes=[
             pltpu.VMEM((channels // LANES, epochs, 2 * REACH, width + 16, LANES), F32),
             pltpu.VMEM((epochs, 2 * REACH * width, channels), F32),
             pltpu.VMEM((max(1, early - 1), depth, 4 * LANES), BF16),
             pltpu.SemaphoreType.DMA((channels // LANES - 1,)),
         ],
-        compiler_params=pltpu.CompilerParams(vmem_limit_bytes=32 * 2**20),
+        compiler_params=pltpu.CompilerParams(vmem_limit_bytes=20 * 2**20),
         cost_estimate=pl.CostEstimate(flops=flops, bytes_accessed=2 * w_gates.size, transcendentals=0),
     )(
         spread,
@@ -499,21 +523,24 @@
         w_reduce,
         w_first,
         pltpu.with_memory_space_constraint(w_gates, pltpu.HBM),
+        *kept,
     )
     *state_near, taps, w_later = rest
+    kept = [] if before is None else before[1][1]
     send_far, *state_far = pl.pallas_call(
-        functools.partial(later_kernel, early),
+        functools.partial(later_kernel, early, turn, 7 + len(kept)),
         name="later",
         out_shape=[
             jax.ShapeDtypeStruct((pixels + tail * channels // LANES, far), BF16),
             *state(far),
         ],
-        in_specs=[vmem] * 6 + [pl.BlockSpec(memory_space=pl.ANY)],
+        in_specs=[vmem] * 6 + [anywhere] + [vmem] * len(kept),
         out_specs=[vmem] * 7,
+        input_output_aliases={7 + k: 1 + k for k in range(len(kept))},
         scratch_shapes=[pltpu.VMEM((8, far), F32)],
-        compiler_params=pltpu.CompilerParams(vmem_limit_bytes=24 * 2**20),
+        compiler_params=pltpu.CompilerParams(vmem_limit_bytes=16 * 2**20),
         cost_estimate=pl.CostEstimate(flops=10**10, bytes_accessed=0, transcendentals=0),
-    )(taps, w_later, mask, short_rows, long_rows, pooled, send)
+    )(taps, w_later, mask, short_rows, long_rows, pooled, send, *kept)
     return (send, state_near), (send_far, state_far)
 
 
@@ -717,25 +744,17 @@
         out_near,
     ) = run_stage(near, w_expand, w_reduce, gate_weights, [w_query, w_key, w_value, w_out])
     early = max(1, channels // LANES - 1)
-    (send, state_near), (send_far, state_far) = run_block(
-        tiles,
-        early,
-        (
-            spread,
-            mask,
-            short_rows,
-            long_rows,
-            near[0],
-            near[1],
-            expand_near,
-            reduce_near,
-            w_first,
-        ),
-        recv_pair,
-        recv_next,
-        gate_weights,
-        tail,
-    )
+    staged = (spread, mask, short_rows, long_rows, near[0], near[1], expand_near, reduce_near, w_first)
+
+    def blocks(turn, before):
+        return run_block(
+            tiles, early, turn, staged, recv_pair, recv_next, gate_weights, tail, before
+        )
+
+    short_chain = 1 < stages <= 8
+    (send, state_near), (send_far, state_far) = first = blocks(FIRST if short_chain else ALL, None)
+    if short_chain:
+        (_, state_near), (_, state_far) = blocks(REST, first)
     vmem = pl.BlockSpec(memory_space=pltpu.VMEM)
     params = pltpu.CompilerParams(vmem_limit_bytes=16 * 2**20)
     cost = pl.CostEstimate(flops=10**10, bytes_accessed=0, transcendentals=0)

time: 37.9 us -> 37.4 us (0.987)
  waiting for transfers between devices: 10.2 us -> 8.12 us
  Pallas kernels: 18.9 us -> 20 us
    ppermute x3, waiting for transfers between devices: 10.2 us -> 8.1 us  [body(): arrived_far.append(lax.ppermute(send_far, 'epoch', link))]
    pallas_call x2 -> x4, Pallas kernels: 10.8 us -> 12 us  [the longest x2 8.59 us: run_block(): pl.pallas_call(functools.partial(block_kernel, tiles, turn, 12 + len(kept...]
  transfers between devices with their start and end apart: 8 -> 8, of which waited for: 1 -> 1; matrix products, arithmetic and copies ran while one was open for 0% -> 0% of each run, Pallas kernels for 19% -> 45%
where the time goes in v6:
time: 37.4 us; the launch traced here: 36.9 us
  Pallas kernels  20 us (53%)
  waiting for transfers between devices  8.12 us (22%)
  starting transfers between devices  7.84 us (21%)
  between operations  0.95 us (3%)
    pallas_call x2, Pallas kernels, run_block(): pl.pallas_call(functools.partial(block_kernel, tiles, turn, 12 + len(kept...  8.59 us
    ppermute x3, waiting for transfers between devices, body(): arrived_far.append(lax.ppermute(send_far, 'epoch', link))  8.1 us
    pallas_call x1, Pallas kernels, run_stage(): pl.pallas_call(stage_kernel, name='stage', out_shape=out_shape, in_specs=...  3.72 us
    pallas_call x2, Pallas kernels, run_block(): pl.pallas_call(functools.partial(later_kernel, early, turn, 7 + len(kept)...  3.37 us
    ppermute x3, starting transfers between devices, body(): arrived.append(lax.ppermute(send, 'epoch', link))  2.63 us
    ppermute x3, starting transfers between devices, body(): arrived_far.append(lax.ppermute(send_far, 'epoch', link))  2.61 us
    ppermute x1, starting transfers between devices, body(): recv_next = lax.ppermute(to_next, 'tile', pairs(tiles, 1))  2.53 us
    pallas_call x1, Pallas kernels, body(): pl.pallas_call(functools.partial(final_kernel, len(arrived)), name='final...  2.33 us
  transfers between devices with their start and end apart: 8, of which 1 were waited for; matrix products, arithmetic and copies ran while one was open for 0% of the time, Pallas kernels for 45%

profile of v6, /device:TPU:30, one launch (start us, length us, event | category | flops | bytes accessed | tf_op | source)
XLA Modules:
  0.0 36.9 jit_solution(17681614962323702547)
XLA Ops:
  0.6 1.2 %near.1 = (bf16[2,16,16,384]{3,2,1,0:T(8,128)(2,1)S(1)}, f32[7,7,384]{2,1,0:T(8,128)S(1)}, s32[2,16,16]{2,1,0:T(8,128)S(1)}, s32[8]{0:T(128)S(1)}, f32[8]{0:T(12...) custom-call(bf16[2,16,16,384]{3,2,1,0:T(8,128)(2,1)} %refs_0_.1, ...), custom_call_target="tpu_custom_call" | custom-call | tf_op jit(solution)/shard_map/near/pallas_call | solution.py:53
  1.8 0.1 collective-permute-start
  1.9 2.5 %collective-permute-start.1 = (bf16[2,4,16,384]{3,2,1,0:T(8,128)(2,1)S(1)}, bf16[2,4,16,384]{3,2,1,0:T(8,128)(2,1)S(1)}, u32[]{:S(2)}, u32[]{:S(2)}) collective-permute-start(bf16[2,4,16,384]{3,2,1,0:T(8,128)(2,1)S(1)} %get-tuple-element.82), channel_id=1, source_target_pairs={{1,2},{2,1},{5,6},{6,5},{9,10},{10,9},{13,14},{14,13},{17,18},{18,... | collective-permute-start | bytes 294920 | tf_op jit(solution)/shard_map/ppermute | solution.py:732
  4.4 3.7 %stage.1 = (f32[2,288,384]{2,1,0:T(8,128)S(1)}, f32[512,128]{1,0:T(8,128)S(1)}, f32[8,384]{1,0:T(8,128)S(1)}, f32[8,1536]{1,0:T(8,128)S(1)}, f32[8,128]{1,0:T(8,...) custom-call(bf16[2,16,16,384]{3,2,1,0:T(8,128)(2,1)S(1)} %get-tuple-, ...), custom_call_target="tpu_custom_call" | custom-call | flops 10000000000 | bytes 4718592 | tf_op jit(solution)/shard_map/stage/pallas_call | solution.py:200
  8.2 0.0 collective-permute-done.refs_1_
  8.2 0.0 collective-permute-done.1.refs_2_
  8.2 0.7 %collective-permute-start.2 = (bf16[256,256]{1,0:T(8,128)(2,1)S(1)}, bf16[256,256]{1,0:T(8,128)(2,1)S(1)}, u32[]{:S(2)}, u32[]{:S(2)}) collective-permute-start(bf16[256,256]{1,0:T(8,128)(2,1)S(1)} %get-tuple-element.89.refs_6_), channel_id=1, source_target_pairs={{0,4},{1,5},{2,6},{3,7},{16,20},{17,21},{18,22},{19,23}} | collective-permute-start | bytes 393224 | tf_op jit(solution)/shard_map/ppermute | solution.py:795
  8.9 0.7 %collective-permute-start.4 = (bf16[304,128]{1,0:T(8,128)(2,1)S(1)}, bf16[304,128]{1,0:T(8,128)(2,1)S(1)}, u32[]{:S(2)}, u32[]{:S(2)}) collective-permute-start(bf16[304,128]{1,0:T(8,128)(2,1)S(1)} %get-tuple-element.99.refs_18_.before), channel_id=1, source_target_pairs={{0,4},{1,5},{2,6},{3,7},{16,20},{17,21},{18,22},{19,23}} | collective-permute-start | bytes 233480 | tf_op jit(solution)/shard_map/ppermute | solution.py:796
  9.6 8.6 %block.3 = (bf16[256,256]{1,0:T(8,128)(2,1)S(1)}, f32[8,256]{1,0:T(8,128)S(1)}, f32[256,256]{1,0:T(8,128)S(1)}, f32[256,256]{1,0:T(8,128)S(1)}, f32[256,256]{1,0...) custom-call(f32[2,288,384]{2,1,0:T(8,128)S(1)} %get-tuple-element.80, ...), custom_call_target="tpu_custom_call", output_to_operand_aliasing={{2}: (12, {}), {3}: (13, {}), {4}: (14, {}), {5}: (15, {}),... | custom-call | flops 6643777536 | bytes 10616832 | tf_op jit(solution)/shard_map/block/pallas_call | solution.py:492
  18.2 3.4 %later.3 = (bf16[304,128]{1,0:T(8,128)(2,1)}, f32[256,128]{1,0:T(8,128)S(1)}, f32[256,128]{1,0:T(8,128)S(1)}, f32[256,128]{1,0:T(8,128)S(1)}, f32[256,128]{1,0:T...) custom-call(bf16[512,3456]{1,0:T(8,128)(2,1)S(1)} %get-tuple-element, ...), custom_call_target="tpu_custom_call", output_to_operand_aliasing={{1}: (7, {}), {2}: (8, {}), {3}: (9, {}), {4}: (10, {}), {5... | custom-call | flops 10000000000 | tf_op jit(solution)/shard_map/later/pallas_call | solution.py:530
  21.5 0.0 collective-permute-done.2.arrived.refs_0_
  21.5 0.2 relay.2
  21.7 0.7 %collective-permute-start.3 = (bf16[256,256]{1,0:T(8,128)(2,1)S(1)}, bf16[256,256]{1,0:T(8,128)(2,1)S(1)}, u32[]{:S(2)}, u32[]{:S(2)}) collective-permute-start(bf16[256,256]{1,0:T(8,128)(2,1)S(1)} %get-tuple-element.106), channel_id=1, source_target_pairs={{4,8},{5,9},{6,10},{7,11},{20,24},{21,25},{22,26},{23,27}} | collective-permute-start | bytes 393224 | tf_op jit(solution)/shard_map/ppermute | solution.py:795
  22.4 0.0 collective-permute-done.4.arrived.refs_3_
  22.4 0.3 relay_later.2.before
  22.6 0.7 %collective-permute-start.6 = (bf16[304,128]{1,0:T(8,128)(2,1)S(1)}, bf16[304,128]{1,0:T(8,128)(2,1)S(1)}, u32[]{:S(2)}, u32[]{:S(2)}) collective-permute-start(bf16[304,128]{1,0:T(8,128)(2,1)S(1)} %relay_later.2.before), channel_id=1, source_target_pairs={{4,8},{5,9},{6,10},{7,11},{20,24},{21,25},{22,26},{23,27}} | collective-permute-start | bytes 233480 | tf_op jit(solution)/shard_map/ppermute | solution.py:796
  23.3 0.0 collective-permute-done.3.arrived.refs_1_
  23.3 0.2 relay.3
  23.5 1.3 %collective-permute-start.5 = (bf16[256,256]{1,0:T(8,128)(2,1)S(1)}, bf16[256,256]{1,0:T(8,128)(2,1)S(1)}, u32[]{:S(2)}, u32[]{:S(2)}) collective-permute-start(bf16[256,256]{1,0:T(8,128)(2,1)S(1)} %get-tuple-element.124), channel_id=1, source_target_pairs={{8,12},{9,13},{10,14},{11,15},{24,28},{25,29},{26,30},{27,31}} | collective-permute-start | bytes 393224 | tf_op jit(solution)/shard_map/ppermute | solution.py:795
  24.8 0.0 collective-permute-done.6.arrived.refs_4_
  24.8 0.3 relay_later.3
  25.1 1.3 %collective-permute-start.7 = (bf16[304,128]{1,0:T(8,128)(2,1)S(1)}, bf16[304,128]{1,0:T(8,128)(2,1)S(1)}, u32[]{:S(2)}, u32[]{:S(2)}) collective-permute-start(bf16[304,128]{1,0:T(8,128)(2,1)S(1)} %relay_later.3), channel_id=1, source_target_pairs={{8,12},{9,13},{10,14},{11,15},{24,28},{25,29},{26,30},{27,31}} | collective-permute-start | bytes 233480 | tf_op jit(solution)/shard_map/ppermute | solution.py:796
  26.3 8.1 %collective-permute-done.7.refs_5_ = bf16[304,128]{1,0:T(8,128)(2,1)S(1)} collective-permute-done((bf16[304,128]{1,0:T(8,128)(2,1)S(1)}, bf16[304,128]{1,0:T(8,128)(2,1)S(1)}, u32[]{:S(2)}, u32[]{:S(2)}) %collective-permute-start.7) | collective-permute-done | bytes 77856 | tf_op jit(solution)/shard_map/ppermute | solution.py:796
  34.4 0.0 collective-permute-done.5.refs_2_
  34.5 2.3 %final.1 = (bf16[2,256,384]{2,1,0:T(8,128)(2,1)}, bf16[2,384]{1,0:T(2,128)(2,1)}) custom-call(bf16[256,256]{1,0:T(8,128)(2,1)S(1)} %collective-permute-done.2.arrived.refs_0_, bf16[256,256]{1,0:T(8,128)(2,1)S(1)} %collective-permute-done.3.arrived.refs_1_, bf16[256,256]{1,0:T(8,128)(2,1)S(1)} %collective-permute-done.5.refs_2_, ...), custom_call_target="tpu_custom_call" | custom-call | tf_op jit(solution)/shard_map/final/pallas_call | solution.py:824
  (2 shorter events, 0.1 us)
Async XLA Ops:
  1.8 6.4 %collective-permute-start = (bf16[2,4,16,384]{3,2,1,0:T(8,128)(2,1)S(1)}, bf16[2,4,16,384]{3,2,1,0:T(8,128)(2,1)S(1)}, u32[]{:S(2)}, u32[]{:S(2)}) collective-permute-start(bf16[2,4,16,384]{3,2,1,0:T(8,128)(2,1)S(1)} %get-tuple-element.81), channel_id=1, source_target_pairs={{0,1},{1,0},{2,3},{3,2},{4,5},{5,4},{6,7},{7,6},{8,9},{9,8},{10,11... | collective-permute-start | bytes 294920 | tf_op jit(solution)/shard_map/ppermute | solution.py:731
  1.9 6.3 %collective-permute-start.1 = (bf16[2,4,16,384]{3,2,1,0:T(8,128)(2,1)S(1)}, bf16[2,4,16,384]{3,2,1,0:T(8,128)(2,1)S(1)}, u32[]{:S(2)}, u32[]{:S(2)}) collective-permute-start(bf16[2,4,16,384]{3,2,1,0:T(8,128)(2,1)S(1)} %get-tuple-element.82), channel_id=1, source_target_pairs={{1,2},{2,1},{5,6},{6,5},{9,10},{10,9},{13,14},{14,13},{17,18},{18,... | collective-permute-start | bytes 294920 | tf_op jit(solution)/shard_map/ppermute | solution.py:732
  8.2 13.3 %collective-permute-start.2 = (bf16[256,256]{1,0:T(8,128)(2,1)S(1)}, bf16[256,256]{1,0:T(8,128)(2,1)S(1)}, u32[]{:S(2)}, u32[]{:S(2)}) collective-permute-start(bf16[256,256]{1,0:T(8,128)(2,1)S(1)} %get-tuple-element.89.refs_6_), channel_id=1, source_target_pairs={{0,4},{1,5},{2,6},{3,7},{16,20},{17,21},{18,22},{19,23}} | collective-permute-start | bytes 393224 | tf_op jit(solution)/shard_map/ppermute | solution.py:795
  8.9 13.4 %collective-permute-start.4 = (bf16[304,128]{1,0:T(8,128)(2,1)S(1)}, bf16[304,128]{1,0:T(8,128)(2,1)S(1)}, u32[]{:S(2)}, u32[]{:S(2)}) collective-permute-start(bf16[304,128]{1,0:T(8,128)(2,1)S(1)} %get-tuple-element.99.refs_18_.before), channel_id=1, source_target_pairs={{0,4},{1,5},{2,6},{3,7},{16,20},{17,21},{18,22},{19,23}} | collective-permute-start | bytes 233480 | tf_op jit(solution)/shard_map/ppermute | solution.py:796
  21.7 1.6 %collective-permute-start.3 = (bf16[256,256]{1,0:T(8,128)(2,1)S(1)}, bf16[256,256]{1,0:T(8,128)(2,1)S(1)}, u32[]{:S(2)}, u32[]{:S(2)}) collective-permute-start(bf16[256,256]{1,0:T(8,128)(2,1)S(1)} %get-tuple-element.106), channel_id=1, source_target_pairs={{4,8},{5,9},{6,10},{7,11},{20,24},{21,25},{22,26},{23,27}} | collective-permute-start | bytes 393224 | tf_op jit(solution)/shard_map/ppermute | solution.py:795
  22.6 2.2 %collective-permute-start.6 = (bf16[304,128]{1,0:T(8,128)(2,1)S(1)}, bf16[304,128]{1,0:T(8,128)(2,1)S(1)}, u32[]{:S(2)}, u32[]{:S(2)}) collective-permute-start(bf16[304,128]{1,0:T(8,128)(2,1)S(1)} %relay_later.2.before), channel_id=1, source_target_pairs={{4,8},{5,9},{6,10},{7,11},{20,24},{21,25},{22,26},{23,27}} | collective-permute-start | bytes 233480 | tf_op jit(solution)/shard_map/ppermute | solution.py:796
  23.5 11.0 %collective-permute-start.5 = (bf16[256,256]{1,0:T(8,128)(2,1)S(1)}, bf16[256,256]{1,0:T(8,128)(2,1)S(1)}, u32[]{:S(2)}, u32[]{:S(2)}) collective-permute-start(bf16[256,256]{1,0:T(8,128)(2,1)S(1)} %get-tuple-element.124), channel_id=1, source_target_pairs={{8,12},{9,13},{10,14},{11,15},{24,28},{25,29},{26,30},{27,31}} | collective-permute-start | bytes 393224 | tf_op jit(solution)/shard_map/ppermute | solution.py:795
  25.1 9.4 %collective-permute-start.7 = (bf16[304,128]{1,0:T(8,128)(2,1)S(1)}, bf16[304,128]{1,0:T(8,128)(2,1)S(1)}, u32[]{:S(2)}, u32[]{:S(2)}) collective-permute-start(bf16[304,128]{1,0:T(8,128)(2,1)S(1)} %relay_later.3), channel_id=1, source_target_pairs={{8,12},{9,13},{10,14},{11,15},{24,28},{25,29},{26,30},{27,31}} | collective-permute-start | bytes 233480 | tf_op jit(solution)/shard_map/ppermute | solution.py:796

commit v7 on v6

--- a/solution.py
+++ b/solution.py
@@ -214,21 +214,19 @@
     )(*near, *[pltpu.with_memory_space_constraint(x, pltpu.HBM) for x in far])
 
 
-FIRST, REST, ALL = 0, 1, 2
-
-
 def on_devices(turn, work):
-    if turn == ALL:
+    if turn is None:
         work()
     else:
-        mine = (lax.axis_index("epoch") == 0) == (turn == FIRST)
-        pl.when(mine)(work)
-
-
-def block_kernel(tiles, turn, count, *refs):
-    ins = refs[:12]
+        stage = lax.axis_index("epoch")
+        pl.when((stage >= turn[0]) & (stage < turn[1]))(work)
+
+
+def block_kernel(tiles, turn, count, sends, *refs):
     outs = refs[count:]
-    on_devices(turn, lambda: block_work(tiles, *ins, *outs))
+    if not sends:
+        outs = (None, None) + outs
+    on_devices(turn, lambda: block_work(tiles, *refs[:12], *outs))
 
 
 def block_work(
@@ -266,7 +264,7 @@
     pixels = height * width
     wide = 4 * LANES
 
-    early = send.shape[1] // LANES
+    early = keep.shape[1] // LANES
     places = [w_gates.at[j] for j in range(early - 1)] + [w_later.at[j] for j in range(groups - early)]
     gate_copies = [
         pltpu.make_async_copy(w_gates_hbm.at[:, pl.ds((j + 1) * wide, wide)], place, sems.at[j])
@@ -418,12 +416,17 @@
             keep[:, lanes] = decay0[:, lanes] * decay
             cell = decay * inflow0[:, lanes] + inflow
             block[:, lanes] = cell
-            send[:pixels, lanes] = cell.astype(BF16)
-        pooled[e : e + 1, lanes] = pool(opened * jnp.tanh(cell))
-
-
-def later_kernel(first, turn, count, *refs):
-    on_devices(turn, lambda: later_work(first, *refs[:7], *refs[count:]))
+            if send is not None:
+                send[:pixels, lanes] = cell.astype(BF16)
+        if pooled is not None:
+            pooled[e : e + 1, lanes] = pool(opened * jnp.tanh(cell))
+
+
+def later_kernel(first, turn, count, sends, *refs):
+    outs = refs[count:]
+    if not sends:
+        outs = (None,) + outs + (None,)
+    on_devices(turn, lambda: later_work(first, *refs[:6], *outs))
 
 
 def later_work(
@@ -434,7 +437,6 @@
     short_rows,
     long_rows,
     pooled_early,
-    send_early,
     send,
     decay0,
     inflow0,
@@ -449,6 +451,8 @@
     for j in range(first, channels // LANES):
         at = j - first
         cells_of(j, at, taps, w_gates.at[at], mask, short_rows, long_rows, send, pooled, state)
+    if send is None:
+        return
     pixels = keep.shape[0]
     both = jnp.concatenate([pooled_early[0:2, :], pooled[0:2, :]], axis=1)
     own = tokens_of(both, short_rows[5:6, :])
@@ -473,7 +477,7 @@
     return jnp.concatenate(parts, axis=1)
 
 
-def run_block(tiles, early, turn, staged, recv_pair, recv_next, w_gates, tail, before):
+def run_block(tiles, early, turn, staged, recv_pair, recv_next, w_gates, kept, after):
     spread, mask, short_rows, long_rows, frames, dw_kernel, w_expand, w_reduce, w_first = staged
     epochs, height, width, channels = frames.shape
     pixels = height * width
@@ -483,25 +487,25 @@
     anywhere = pl.BlockSpec(memory_space=pl.ANY)
     near = early * LANES
     far = channels - near
-
-    def state(lanes):
-        return [jax.ShapeDtypeStruct((pixels, lanes), F32)] * 6
-
-    kept = [] if before is None else [*before[0][1], before[1][0]]
+    sends = not kept
+    sent = [
+        jax.ShapeDtypeStruct((pixels, near), BF16),
+        jax.ShapeDtypeStruct((8, near), F32),
+    ] * sends
+    state = [jax.ShapeDtypeStruct((pixels, near), F32)] * 6
     flops = 2 * epochs * pixels * (2 * w_expand.size + w_gates.size)
-    send, pooled, *rest = pl.pallas_call(
-        functools.partial(block_kernel, tiles, turn, 12 + len(kept)),
+    out = pl.pallas_call(
+        functools.partial(block_kernel, tiles, turn, 12 + len(kept) + len(after), sends),
         name="block",
         out_shape=[
-            jax.ShapeDtypeStruct((pixels, near), BF16),
-            jax.ShapeDtypeStruct((8, near), F32),
-            *state(near),
+            *sent,
+            *state,
             jax.ShapeDtypeStruct((epochs * pixels, depth), BF16),
             jax.ShapeDtypeStruct((far // LANES, depth, 4 * LANES), BF16),
         ],
-        in_specs=[vmem] * 11 + [hbm] + [vmem] * (len(kept) - 1) + [anywhere] * min(1, len(kept)),
-        out_specs=[vmem] * 10,
-        input_output_aliases={12 + k: 2 + k for k in range(len(kept) - 1)},
+        in_specs=[vmem] * 11 + [hbm] + [vmem] * len(kept) + [anywhere] * len(after),
+        out_specs=[vmem] * (len(sent) + 8),
+        input_output_aliases={12 + k: len(sent) + k for k in range(len(kept))},
         scratch_shapes=[
             pltpu.VMEM((channels // LANES, epochs, 2 * REACH, width + 16, LANES), F32),
             pltpu.VMEM((epochs, 2 * REACH * width, channels), F32),
@@ -524,24 +528,33 @@
         w_first,
         pltpu.with_memory_space_constraint(w_gates, pltpu.HBM),
         *kept,
+        *after,
     )
-    *state_near, taps, w_later = rest
-    kept = [] if before is None else before[1][1]
-    send_far, *state_far = pl.pallas_call(
-        functools.partial(later_kernel, early, turn, 7 + len(kept)),
+    return out[: len(sent)], out[len(sent) : -2], out[-2:]
+
+
+def run_later(early, turn, staged, pooled, weighed, tail, kept, after):
+    _, mask, short_rows, long_rows = staged[:4]
+    taps, w_later = weighed
+    pixels = taps.shape[0] // 2
+    channels = short_rows.shape[1]
+    far = channels - early * LANES
+    vmem = pl.BlockSpec(memory_space=pltpu.VMEM)
+    anywhere = pl.BlockSpec(memory_space=pl.ANY)
+    sends = not kept
+    sent = [jax.ShapeDtypeStruct((pixels + tail * channels // LANES, far), BF16)] * sends
+    out = pl.pallas_call(
+        functools.partial(later_kernel, early, turn, 6 + len(kept) + len(after), sends),
         name="later",
-        out_shape=[
-            jax.ShapeDtypeStruct((pixels + tail * channels // LANES, far), BF16),
-            *state(far),
-        ],
-        in_specs=[vmem] * 6 + [anywhere] + [vmem] * len(kept),
-        out_specs=[vmem] * 7,
-        input_output_aliases={7 + k: 1 + k for k in range(len(kept))},
-        scratch_shapes=[pltpu.VMEM((8, far), F32)],
+        out_shape=[*sent] + [jax.ShapeDtypeStruct((pixels, far), F32)] * 6,
+        in_specs=[vmem] * 6 + [vmem] * len(kept) + [anywhere] * len(after),
+        out_specs=[vmem] * (len(sent) + 6),
+        input_output_aliases={6 + k: len(sent) + k for k in range(len(kept))},
+        scratch_shapes=[pltpu.VMEM((8, far), F32)] * sends,
         compiler_params=pltpu.CompilerParams(vmem_limit_bytes=16 * 2**20),
         cost_estimate=pl.CostEstimate(flops=10**10, bytes_accessed=0, transcendentals=0),
-    )(taps, w_later, mask, short_rows, long_rows, pooled, send, *kept)
-    return (send, state_near), (send_far, state_far)
+    )(taps, w_later, mask, short_rows, long_rows, pooled, *kept, *after)
+    return out[: len(sent)], out[len(sent) :]
 
 
 def pool(memory):
@@ -746,15 +759,18 @@
     early = max(1, channels // LANES - 1)
     staged = (spread, mask, short_rows, long_rows, near[0], near[1], expand_near, reduce_near, w_first)
 
-    def blocks(turn, before):
+    def blocks(turn, kept, after):
         return run_block(
-            tiles, early, turn, staged, recv_pair, recv_next, gate_weights, tail, before
+            tiles, early, turn, staged, recv_pair, recv_next, gate_weights, kept, after
         )
 
     short_chain = 1 < stages <= 8
-    (send, state_near), (send_far, state_far) = first = blocks(FIRST if short_chain else ALL, None)
+    first = (0, 1) if short_chain else None
+    (send, pooled), state_near, weighed = blocks(first, [], [])
+    (send_far,), state_far = run_later(early, first, staged, pooled, weighed, tail, [], [send])
     if short_chain:
-        (_, state_near), (_, state_far) = blocks(REST, first)
+        _, state_near, weighed = blocks((1, stages), state_near, [send_far])
+        _, state_far = run_later(early, (1, 2), staged, pooled, weighed, tail, state_far, [])
     vmem = pl.BlockSpec(memory_space=pltpu.VMEM)
     params = pltpu.CompilerParams(vmem_limit_bytes=16 * 2**20)
     cost = pl.CostEstimate(flops=10**10, bytes_accessed=0, transcendentals=0)
@@ -773,7 +789,7 @@
             cost_estimate=cost,
         )(arrived, *state_near, before)
 
-    def relay_later(stage, arrived, pooled):
+    def relay_later(stage, arrived, pooled, state_far):
         return pl.pallas_call(
             functools.partial(relay_later_kernel, stage),
             name="relay_later",
@@ -791,7 +807,11 @@
             link = [(stage, stage + 1)]
             if stage > 0:
                 send, pooled = relay(arrived[-1], send_far)
-                send_far = relay_later(stage, arrived_far[-1], pooled)
+                if stage == 1 and stages > 2:
+                    _, state_far = run_later(
+                        early, (2, stages), staged, pooled, weighed, tail, state_far, [send]
+                    )
+                send_far = relay_later(stage, arrived_far[-1], pooled, state_far)
             arrived.append(lax.ppermute(send, "epoch", link))
             arrived_far.append(lax.ppermute(send_far, "epoch", link))
     else:
@@ -814,7 +834,7 @@
         incoming_far = along(state_far, channels - early * LANES)
         _, pooled = relay(incoming, send_far)
         blank = jnp.zeros((tail * channels // LANES, LANES), BF16)
-        told = relay_later(0, jnp.concatenate([incoming_far, blank]), pooled)[pixels:]
+        told = relay_later(0, jnp.concatenate([incoming_far, blank]), pooled, state_far)[pixels:]
         told = jnp.concatenate(jnp.split(told, channels // LANES, axis=0), axis=1)
         known = lax.all_gather(told[:epochs], "epoch", axis=0, tiled=True)
         known = jnp.concatenate([known, jnp.zeros((tail - total, channels), BF16)])

time: 37.4 us -> 36.4 us (0.973)
  Pallas kernels: 20 us -> 19.1 us
    pallas_call x2 -> x3, Pallas kernels: 3.37 us -> 2.55 us  [run_later(): pl.pallas_call(functools.partial(later_kernel, early, turn, 6 + len(kept)...]
  transfers between devices with their start and end apart: 8 -> 8, of which waited for: 1 -> 1; matrix products, arithmetic and copies ran while one was open for 0% -> 0% of each run, Pallas kernels for 45% -> 43%
where the time goes in v7:
time: 36.4 us; the launch traced here: 35.9 us
  Pallas kernels  19.1 us (52%)
  waiting for transfers between devices  7.92 us (22%)
  starting transfers between devices  7.84 us (22%)
  between operations  0.97 us (3%)
    pallas_call x2, Pallas kernels, run_block(): pl.pallas_call(functools.partial(block_kernel, tiles, turn, 12 + len(kept...  8.56 us
    ppermute x3, waiting for transfers between devices, body(): arrived_far.append(lax.ppermute(send_far, 'epoch', link))  7.91 us
    pallas_call x1, Pallas kernels, run_stage(): pl.pallas_call(stage_kernel, name='stage', out_shape=out_shape, in_specs=...  3.73 us
    ppermute x3, starting transfers between devices, body(): arrived.append(lax.ppermute(send, 'epoch', link))  2.63 us
    ppermute x3, starting transfers between devices, body(): arrived_far.append(lax.ppermute(send_far, 'epoch', link))  2.61 us
    pallas_call x3, Pallas kernels, run_later(): pl.pallas_call(functools.partial(later_kernel, early, turn, 6 + len(kept)...  2.55 us
    ppermute x1, starting transfers between devices, body(): recv_next = lax.ppermute(to_next, 'tile', pairs(tiles, 1))  2.53 us
    pallas_call x1, Pallas kernels, body(): pl.pallas_call(functools.partial(final_kernel, len(arrived)), name='final...  2.34 us
  transfers between devices with their start and end apart: 8, of which 1 were waited for; matrix products, arithmetic and copies ran while one was open for 0% of the time, Pallas kernels for 43%

profile of v7, /device:TPU:30, one launch (start us, length us, event | category | flops | bytes accessed | tf_op | source)
XLA Modules:
  0.0 35.9 jit_solution(17439128590800675171)
XLA Ops:
  0.6 1.2 %near.1 = (bf16[2,16,16,384]{3,2,1,0:T(8,128)(2,1)S(1)}, f32[7,7,384]{2,1,0:T(8,128)S(1)}, s32[2,16,16]{2,1,0:T(8,128)S(1)}, s32[8]{0:T(128)S(1)}, f32[8]{0:T(12...) custom-call(bf16[2,16,16,384]{3,2,1,0:T(8,128)(2,1)} %refs_0_.1, ...), custom_call_target="tpu_custom_call" | custom-call | tf_op jit(solution)/shard_map/near/pallas_call | solution.py:53
  1.8 0.1 collective-permute-start
  1.9 2.5 %collective-permute-start.1 = (bf16[2,4,16,384]{3,2,1,0:T(8,128)(2,1)S(1)}, bf16[2,4,16,384]{3,2,1,0:T(8,128)(2,1)S(1)}, u32[]{:S(2)}, u32[]{:S(2)}) collective-permute-start(bf16[2,4,16,384]{3,2,1,0:T(8,128)(2,1)S(1)} %get-tuple-element.86), channel_id=1, source_target_pairs={{1,2},{2,1},{5,6},{6,5},{9,10},{10,9},{13,14},{14,13},{17,18},{18,... | collective-permute-start | bytes 294920 | tf_op jit(solution)/shard_map/ppermute | solution.py:745
  4.4 3.7 %stage.1 = (f32[2,288,384]{2,1,0:T(8,128)S(1)}, f32[512,128]{1,0:T(8,128)S(1)}, f32[8,384]{1,0:T(8,128)S(1)}, f32[8,1536]{1,0:T(8,128)S(1)}, f32[8,128]{1,0:T(8,...) custom-call(bf16[2,16,16,384]{3,2,1,0:T(8,128)(2,1)S(1)} %get-tuple-, ...), custom_call_target="tpu_custom_call" | custom-call | flops 10000000000 | bytes 4718592 | tf_op jit(solution)/shard_map/stage/pallas_call | solution.py:200
  8.2 0.0 collective-permute-done.refs_1_
  8.2 0.0 collective-permute-done.1.refs_2_
  8.2 0.7 %collective-permute-start.2 = (bf16[256,256]{1,0:T(8,128)(2,1)S(1)}, bf16[256,256]{1,0:T(8,128)(2,1)S(1)}, u32[]{:S(2)}, u32[]{:S(2)}) collective-permute-start(bf16[256,256]{1,0:T(8,128)(2,1)S(1)} %get-tuple-element.93.refs_6_), channel_id=1, source_target_pairs={{0,4},{1,5},{2,6},{3,7},{16,20},{17,21},{18,22},{19,23}} | collective-permute-start | bytes 393224 | tf_op jit(solution)/shard_map/ppermute | solution.py:815
  8.9 0.7 %collective-permute-start.4 = (bf16[304,128]{1,0:T(8,128)(2,1)S(1)}, bf16[304,128]{1,0:T(8,128)(2,1)S(1)}, u32[]{:S(2)}, u32[]{:S(2)}) collective-permute-start(bf16[304,128]{1,0:T(8,128)(2,1)S(1)} %get-tuple-element.103.refs_18_.before), channel_id=1, source_target_pairs={{0,4},{1,5},{2,6},{3,7},{16,20},{17,21},{18,22},{19,23}} | collective-permute-start | bytes 233480 | tf_op jit(solution)/shard_map/ppermute | solution.py:816
  9.6 8.5 %block.3 = (f32[256,256]{1,0:T(8,128)S(1)}, f32[256,256]{1,0:T(8,128)S(1)}, f32[256,256]{1,0:T(8,128)S(1)}, f32[256,256]{1,0:T(8,128)S(1)}, f32[256,256]{1,0:T(8...) custom-call(f32[2,288,384]{2,1,0:T(8,128)S(1)} %get-tuple-element.84, ...), custom_call_target="tpu_custom_call", output_to_operand_aliasing={{0}: (12, {}), {1}: (13, {}), {2}: (14, {}), {3}: (15, {}),... | custom-call | flops 6643777536 | bytes 10616832 | tf_op jit(solution)/shard_map/block/pallas_call | solution.py:497
  18.2 0.0 collective-permute-done.2.arrived.refs_0_
  18.2 0.1 relay.2
  18.3 0.7 %collective-permute-start.3 = (bf16[256,256]{1,0:T(8,128)(2,1)S(1)}, bf16[256,256]{1,0:T(8,128)(2,1)S(1)}, u32[]{:S(2)}, u32[]{:S(2)}) collective-permute-start(bf16[256,256]{1,0:T(8,128)(2,1)S(1)} %get-tuple-element.110.refs_12_), channel_id=1, source_target_pairs={{4,8},{5,9},{6,10},{7,11},{20,24},{21,25},{22,26},{23,27}} | collective-permute-start | bytes 393224 | tf_op jit(solution)/shard_map/ppermute | solution.py:815
  19.0 2.5 %later.5 = (f32[256,128]{1,0:T(8,128)S(1)}, f32[256,128]{1,0:T(8,128)S(1)}, f32[256,128]{1,0:T(8,128)S(1)}, f32[256,128]{1,0:T(8,128)S(1)}, f32[256,128]{1,0:T(8,128)S(1)}, /*index=5*/f32[256,128]{1,0:T(8,128)S(1)}) custom-call(bf16[512,3456]{1,0:T(8,128)(2,1)S(1)} %get-tuple-element.1, ...), custom_call_target="tpu_custom_call", output_to_operand_aliasing={{0}: (6, {}), {1}: (7, {}), {2}: (8, {}), {3}: (9, {}), {4}... | custom-call | flops 10000000000 | tf_op jit(solution)/shard_map/later/pallas_call | solution.py:546
  21.5 0.0 collective-permute-done.4.arrived.refs_3_
  21.5 0.3 relay_later.2.before
  21.8 0.7 %collective-permute-start.6 = (bf16[304,128]{1,0:T(8,128)(2,1)S(1)}, bf16[304,128]{1,0:T(8,128)(2,1)S(1)}, u32[]{:S(2)}, u32[]{:S(2)}) collective-permute-start(bf16[304,128]{1,0:T(8,128)(2,1)S(1)} %relay_later.2.before), channel_id=1, source_target_pairs={{4,8},{5,9},{6,10},{7,11},{20,24},{21,25},{22,26},{23,27}} | collective-permute-start | bytes 233480 | tf_op jit(solution)/shard_map/ppermute | solution.py:816
  22.4 0.0 collective-permute-done.3.arrived.refs_1_
  22.5 0.1 relay.3
  22.6 1.3 %collective-permute-start.5 = (bf16[256,256]{1,0:T(8,128)(2,1)S(1)}, bf16[256,256]{1,0:T(8,128)(2,1)S(1)}, u32[]{:S(2)}, u32[]{:S(2)}) collective-permute-start(bf16[256,256]{1,0:T(8,128)(2,1)S(1)} %get-tuple-element.132), channel_id=1, source_target_pairs={{8,12},{9,13},{10,14},{11,15},{24,28},{25,29},{26,30},{27,31}} | collective-permute-start | bytes 393224 | tf_op jit(solution)/shard_map/ppermute | solution.py:815
  23.9 0.0 collective-permute-done.6.arrived.refs_4_
  23.9 0.3 relay_later.3
  24.2 1.3 %collective-permute-start.7 = (bf16[304,128]{1,0:T(8,128)(2,1)S(1)}, bf16[304,128]{1,0:T(8,128)(2,1)S(1)}, u32[]{:S(2)}, u32[]{:S(2)}) collective-permute-start(bf16[304,128]{1,0:T(8,128)(2,1)S(1)} %relay_later.3), channel_id=1, source_target_pairs={{8,12},{9,13},{10,14},{11,15},{24,28},{25,29},{26,30},{27,31}} | collective-permute-start | bytes 233480 | tf_op jit(solution)/shard_map/ppermute | solution.py:816
  25.5 7.9 %collective-permute-done.7.refs_5_ = bf16[304,128]{1,0:T(8,128)(2,1)S(1)} collective-permute-done((bf16[304,128]{1,0:T(8,128)(2,1)S(1)}, bf16[304,128]{1,0:T(8,128)(2,1)S(1)}, u32[]{:S(2)}, u32[]{:S(2)}) %collective-permute-start.7) | collective-permute-done | bytes 77856 | tf_op jit(solution)/shard_map/ppermute | solution.py:816
  33.4 0.0 collective-permute-done.5.refs_2_
  33.4 2.3 %final.1 = (bf16[2,256,384]{2,1,0:T(8,128)(2,1)}, bf16[2,384]{1,0:T(2,128)(2,1)}) custom-call(bf16[256,256]{1,0:T(8,128)(2,1)S(1)} %collective-permute-done.2.arrived.refs_0_, bf16[256,256]{1,0:T(8,128)(2,1)S(1)} %collective-permute-done.3.arrived.refs_1_, bf16[256,256]{1,0:T(8,128)(2,1)S(1)} %collective-permute-done.5.refs_2_, ...), custom_call_target="tpu_custom_call" | custom-call | tf_op jit(solution)/shard_map/final/pallas_call | solution.py:844
  (3 shorter events, 0.1 us)
Async XLA Ops:
  1.8 6.4 %collective-permute-start = (bf16[2,4,16,384]{3,2,1,0:T(8,128)(2,1)S(1)}, bf16[2,4,16,384]{3,2,1,0:T(8,128)(2,1)S(1)}, u32[]{:S(2)}, u32[]{:S(2)}) collective-permute-start(bf16[2,4,16,384]{3,2,1,0:T(8,128)(2,1)S(1)} %get-tuple-element.85), channel_id=1, source_target_pairs={{0,1},{1,0},{2,3},{3,2},{4,5},{5,4},{6,7},{7,6},{8,9},{9,8},{10,11... | collective-permute-start | bytes 294920 | tf_op jit(solution)/shard_map/ppermute | solution.py:744
  1.9 6.3 %collective-permute-start.1 = (bf16[2,4,16,384]{3,2,1,0:T(8,128)(2,1)S(1)}, bf16[2,4,16,384]{3,2,1,0:T(8,128)(2,1)S(1)}, u32[]{:S(2)}, u32[]{:S(2)}) collective-permute-start(bf16[2,4,16,384]{3,2,1,0:T(8,128)(2,1)S(1)} %get-tuple-element.86), channel_id=1, source_target_pairs={{1,2},{2,1},{5,6},{6,5},{9,10},{10,9},{13,14},{14,13},{17,18},{18,... | collective-permute-start | bytes 294920 | tf_op jit(solution)/shard_map/ppermute | solution.py:745
  8.2 9.9 %collective-permute-start.2 = (bf16[256,256]{1,0:T(8,128)(2,1)S(1)}, bf16[256,256]{1,0:T(8,128)(2,1)S(1)}, u32[]{:S(2)}, u32[]{:S(2)}) collective-permute-start(bf16[256,256]{1,0:T(8,128)(2,1)S(1)} %get-tuple-element.93.refs_6_), channel_id=1, source_target_pairs={{0,4},{1,5},{2,6},{3,7},{16,20},{17,21},{18,22},{19,23}} | collective-permute-start | bytes 393224 | tf_op jit(solution)/shard_map/ppermute | solution.py:815
  8.9 12.6 %collective-permute-start.4 = (bf16[304,128]{1,0:T(8,128)(2,1)S(1)}, bf16[304,128]{1,0:T(8,128)(2,1)S(1)}, u32[]{:S(2)}, u32[]{:S(2)}) collective-permute-start(bf16[304,128]{1,0:T(8,128)(2,1)S(1)} %get-tuple-element.103.refs_18_.before), channel_id=1, source_target_pairs={{0,4},{1,5},{2,6},{3,7},{16,20},{17,21},{18,22},{19,23}} | collective-permute-start | bytes 233480 | tf_op jit(solution)/shard_map/ppermute | solution.py:816
  18.3 4.1 %collective-permute-start.3 = (bf16[256,256]{1,0:T(8,128)(2,1)S(1)}, bf16[256,256]{1,0:T(8,128)(2,1)S(1)}, u32[]{:S(2)}, u32[]{:S(2)}) collective-permute-start(bf16[256,256]{1,0:T(8,128)(2,1)S(1)} %get-tuple-element.110.refs_12_), channel_id=1, source_target_pairs={{4,8},{5,9},{6,10},{7,11},{20,24},{21,25},{22,26},{23,27}} | collective-permute-start | bytes 393224 | tf_op jit(solution)/shard_map/ppermute | solution.py:815
  21.8 2.1 %collective-permute-start.6 = (bf16[304,128]{1,0:T(8,128)(2,1)S(1)}, bf16[304,128]{1,0:T(8,128)(2,1)S(1)}, u32[]{:S(2)}, u32[]{:S(2)}) collective-permute-start(bf16[304,128]{1,0:T(8,128)(2,1)S(1)} %relay_later.2.before), channel_id=1, source_target_pairs={{4,8},{5,9},{6,10},{7,11},{20,24},{21,25},{22,26},{23,27}} | collective-permute-start | bytes 233480 | tf_op jit(solution)/shard_map/ppermute | solution.py:816
  22.6 10.8 %collective-permute-start.5 = (bf16[256,256]{1,0:T(8,128)(2,1)S(1)}, bf16[256,256]{1,0:T(8,128)(2,1)S(1)}, u32[]{:S(2)}, u32[]{:S(2)}) collective-permute-start(bf16[256,256]{1,0:T(8,128)(2,1)S(1)} %get-tuple-element.132), channel_id=1, source_target_pairs={{8,12},{9,13},{10,14},{11,15},{24,28},{25,29},{26,30},{27,31}} | collective-permute-start | bytes 393224 | tf_op jit(solution)/shard_map/ppermute | solution.py:815
  24.2 9.2 %collective-permute-start.7 = (bf16[304,128]{1,0:T(8,128)(2,1)S(1)}, bf16[304,128]{1,0:T(8,128)(2,1)S(1)}, u32[]{:S(2)}, u32[]{:S(2)}) collective-permute-start(bf16[304,128]{1,0:T(8,128)(2,1)S(1)} %relay_later.3), channel_id=1, source_target_pairs={{8,12},{9,13},{10,14},{11,15},{24,28},{25,29},{26,30},{27,31}} | collective-permute-start | bytes 233480 | tf_op jit(solution)/shard_map/ppermute | solution.py:816

commit v8 on v7

--- a/solution.py
+++ b/solution.py
@@ -600,39 +600,53 @@
     write_tail(send, pixels, put_tokens(known, own, 2 * stage))
 
 
-def final_kernel(
-    count,
-    *refs,
-):
-    halves = [
-        (refs[:count], refs[2 * count : 2 * count + 6]),
-        (refs[count : 2 * count], refs[2 * count + 6 : 2 * count + 12]),
-    ]
-    short_rows, months, slope, w_qkv, w_out = refs[2 * count + 12 : 2 * count + 17]
-    memory_hbm, change, memory, sems = refs[2 * count + 17 :]
-    epochs, pixels, channels = memory.shape
+def finish(arrived, state, memory):
+    decay0, inflow0, keep, block, open0, open1 = state
+    pixels = keep.shape[0]
+    incoming = arrived[0][:pixels].astype(F32)
+    for more in arrived[1:]:
+        incoming = incoming + more[:pixels].astype(F32)
+    cell0 = decay0[...] * incoming + inflow0[...]
+    cell1 = keep[...] * incoming + block[...]
+    pooled = []
+    for e, (gate, cell) in enumerate(((open0, cell0), (open1, cell1))):
+        out = (gate[...] * jnp.tanh(cell)).astype(BF16)
+        memory[e] = out
+        pooled.append(pool(out))
+    return jnp.concatenate(pooled, axis=0)
+
+
+def final_early_kernel(count, *refs):
+    arrived, state = refs[:count], refs[count : count + 6]
+    memory_hbm, pooled, head_of, channel_of, memory, sem = refs[count + 6 :]
+    pooled[0:2, :] = finish(arrived, state, memory)
+    copy = pltpu.make_async_copy(memory, memory_hbm.at[:, :, pl.ds(0, memory.shape[2])], sem)
+    copy.start()
+    channels, heads = head_of.shape
+    depth = channels // heads
+    member = lax.broadcasted_iota(jnp.int32, (channels, heads), 0) // depth
+    head = lax.broadcasted_iota(jnp.int32, (channels, heads), 1)
+    head_of[...] = jnp.where(member == head, 1.0, 0.0).astype(BF16)
+    member = lax.broadcasted_iota(jnp.int32, (heads, channels), 1) // depth
+    head = lax.broadcasted_iota(jnp.int32, (heads, channels), 0)
+    channel_of[...] = jnp.where(member == head, 1.0, 0.0).astype(BF16)
+    copy.wait()
+
+
+def final_kernel(count, *refs):
+    arrived, state = refs[:count], refs[count : count + 6]
+    short_rows, months, slope, w_qkv, w_out, pooled_early, head_of, channel_of = refs[count + 6 : count + 14]
+    memory_hbm, change, memory, sem = refs[count + 15 :]
+    epochs, pixels, far = memory.shape
+    channels = short_rows.shape[1]
     total = months.shape[0]
-    pooled = [[], []]
-    at = 0
-    for arrived, (decay0, inflow0, keep, block, open0, open1) in halves:
-        lanes = slice(at, at + keep.shape[1])
-        at += keep.shape[1]
-        state = arrived[0][:pixels].astype(F32)
-        for more in arrived[1:]:
-            state = state + more[:pixels].astype(F32)
-        cell0 = decay0[...] * state + inflow0[...]
-        cell1 = keep[...] * state + block[...]
-        for e, (gate, cell) in enumerate(((open0, cell0), (open1, cell1))):
-            out = (gate[...] * jnp.tanh(cell)).astype(BF16)
-            memory[e, :, lanes] = out
-            pooled[e].append(pool(out))
-    copies = [pltpu.make_async_copy(memory.at[e], memory_hbm.at[e], sems.at[e]) for e in range(epochs)]
-    for copy in copies:
-        copy.start()
-    known = read_tail(halves[1][0][0], pixels, channels)
-    for more in halves[1][0][1:]:
+    pooled = finish(arrived, state, memory)
+    copy = pltpu.make_async_copy(memory, memory_hbm.at[:, :, pl.ds(channels - far, far)], sem)
+    copy.start()
+    known = read_tail(arrived[0], pixels, channels)
+    for more in arrived[1:]:
         known = known + read_tail(more, pixels, channels)
-    both = jnp.concatenate([jnp.concatenate(parts, axis=1) for parts in pooled], axis=0)
+    both = jnp.concatenate([pooled_early[0:2, :], pooled], axis=1)
     own = tokens_of(both, short_rows[5:6, :])
     stage = lax.axis_index("epoch")
     tokens = put_tokens(known, own, 2 * stage).astype(BF16)
@@ -642,20 +656,13 @@
     queries = qkv[:, :channels]
     keys = qkv[:, channels : 2 * channels]
     values = qkv[:, 2 * channels :]
-    member = lax.broadcasted_iota(jnp.int32, (channels, heads), 0) // depth
-    head_of = jnp.where(member == lax.broadcasted_iota(jnp.int32, (channels, heads), 1), 1.0, 0.0)
-    member_t = lax.broadcasted_iota(jnp.int32, (heads, channels), 1) // depth
-    channel_of = jnp.where(
-        member_t == lax.broadcasted_iota(jnp.int32, (heads, channels), 0), 1.0, 0.0
-    )
-
     def exact_dot(x, zero_one):
         high = x.astype(BF16)
         rest = x - high.astype(F32)
         low = rest.astype(BF16)
         least = (rest - low.astype(F32)).astype(BF16)
         out = jnp.dot(
-            jnp.concatenate([high, low, least], axis=0), zero_one.astype(BF16), preferred_element_type=F32
+            jnp.concatenate([high, low, least], axis=0), zero_one[...], preferred_element_type=F32
         )
         count = x.shape[0]
         return out[:count] + out[count : 2 * count] + out[2 * count :]
@@ -683,8 +690,7 @@
     ]
     mixed = jnp.concatenate(results, axis=0).astype(BF16)
     change[...] = jnp.dot(mixed, w_out[...], preferred_element_type=F32).astype(BF16)
-    for copy in copies:
-        copy.wait()
+    copy.wait()
 
 
 def pairs(count, start):
@@ -841,6 +847,26 @@
         arrived.append(incoming)
         arrived_far.append(jnp.concatenate([incoming_far, unfold(known)]))
 
+    hbm = pl.BlockSpec(memory_space=pltpu.HBM)
+    heads = head_slope.size
+    memory, pooled, head_of, channel_of = pl.pallas_call(
+        functools.partial(final_early_kernel, len(arrived)),
+        name="final_early",
+        out_shape=[
+            jax.ShapeDtypeStruct((epochs, pixels, channels), BF16),
+            jax.ShapeDtypeStruct((8, early * LANES), F32),
+            jax.ShapeDtypeStruct((channels, heads), BF16),
+            jax.ShapeDtypeStruct((heads, channels), BF16),
+        ],
+        in_specs=[vmem] * (len(arrived) + 6),
+        out_specs=[hbm] + [vmem] * 3,
+        scratch_shapes=[
+            pltpu.VMEM((epochs, pixels, early * LANES), BF16),
+            pltpu.SemaphoreType.DMA,
+        ],
+        compiler_params=params,
+        cost_estimate=cost,
+    )(*arrived, *state_near)
     memory, change = pl.pallas_call(
         functools.partial(final_kernel, len(arrived)),
         name="final",
@@ -848,14 +874,27 @@
             jax.ShapeDtypeStruct((epochs, pixels, channels), BF16),
             jax.ShapeDtypeStruct((epochs, channels), BF16),
         ],
-        in_specs=[vmem] * (2 * len(arrived) + 17),
-        out_specs=[pl.BlockSpec(memory_space=pltpu.HBM), vmem],
+        in_specs=[vmem] * (len(arrived) + 14) + [hbm],
+        out_specs=[hbm, vmem],
+        input_output_aliases={len(arrived) + 14: 0},
         scratch_shapes=[
-            pltpu.VMEM((epochs, pixels, channels), BF16),
-            pltpu.SemaphoreType.DMA((epochs,)),
+            pltpu.VMEM((epochs, pixels, channels - early * LANES), BF16),
+            pltpu.SemaphoreType.DMA,
         ],
         compiler_params=pltpu.CompilerParams(vmem_limit_bytes=24 * 2**20),
-    )(*arrived, *arrived_far, *state_near, *state_far, short_rows, months, slope, qkv_near, out_near)
+    )(
+        *arrived_far,
+        *state_far,
+        short_rows,
+        months,
+        slope,
+        qkv_near,
+        out_near,
+        pooled,
+        head_of,
+        channel_of,
+        pltpu.with_memory_space_constraint(memory, pltpu.HBM),
+    )
     return (
         memory.reshape(epochs, height, width, channels),
         change.reshape(epochs, 1, 1, channels),

time: 36.4 us -> 35.7 us (0.981)
  waiting for transfers between devices: 7.92 us -> 7.07 us
    ppermute x3, waiting for transfers between devices: 7.91 us -> 0.15 us  [body(): arrived_far.append(lax.ppermute(send_far, 'epoch', link))]
    ppermute x3, waiting for transfers between devices: 0.01 us -> 6.92 us  [body(): arrived.append(lax.ppermute(send, 'epoch', link))]
    pallas_call x0 -> x1, Pallas kernels: none -> 0.89 us  [body(): pl.pallas_call(functools.partial(final_early_kernel, len(arrived)), name=...]
    pallas_call x1, Pallas kernels: 2.34 us -> 1.49 us  [body(): pl.pallas_call(functools.partial(final_kernel, len(arrived)), name='final...]
  transfers between devices with their start and end apart: 8 -> 8, of which waited for: 1 -> 2; matrix products, arithmetic and copies ran while one was open for 0% -> 0% of each run, Pallas kernels for 43% -> 47%
where the time goes in v8:
time: 35.7 us; the launch traced here: 35.1 us
  Pallas kernels  19.2 us (54%)
  starting transfers between devices  7.84 us (22%)
  waiting for transfers between devices  7.07 us (20%)
  between operations  0.98 us (3%)
    pallas_call x2, Pallas kernels, run_block(): pl.pallas_call(functools.partial(block_kernel, tiles, turn, 12 + len(kept...  8.56 us
    ppermute x3, waiting for transfers between devices, body(): arrived.append(lax.ppermute(send, 'epoch', link))  6.92 us
    pallas_call x1, Pallas kernels, run_stage(): pl.pallas_call(stage_kernel, name='stage', out_shape=out_shape, in_specs=...  3.73 us
    ppermute x3, starting transfers between devices, body(): arrived.append(lax.ppermute(send, 'epoch', link))  2.63 us
    ppermute x3, starting transfers between devices, body(): arrived_far.append(lax.ppermute(send_far, 'epoch', link))  2.61 us
    ppermute x1, starting transfers between devices, body(): recv_next = lax.ppermute(to_next, 'tile', pairs(tiles, 1))  2.53 us
    pallas_call x3, Pallas kernels, run_later(): pl.pallas_call(functools.partial(later_kernel, early, turn, 6 + len(kept)...  2.52 us
    pallas_call x1, Pallas kernels, body(): pl.pallas_call(functools.partial(final_kernel, len(arrived)), name='final...  1.49 us
  transfers between devices with their start and end apart: 8, of which 2 were waited for; matrix products, arithmetic and copies ran while one was open for 0% of the time, Pallas kernels for 47%

profile of v8, /device:TPU:30, one launch (start us, length us, event | category | flops | bytes accessed | tf_op | source)
XLA Modules:
  0.0 35.1 jit_solution(10811491131442630954)
XLA Ops:
  0.6 1.2 %near.1 = (bf16[2,16,16,384]{3,2,1,0:T(8,128)(2,1)S(1)}, f32[7,7,384]{2,1,0:T(8,128)S(1)}, s32[2,16,16]{2,1,0:T(8,128)S(1)}, s32[8]{0:T(128)S(1)}, f32[8]{0:T(12...) custom-call(bf16[2,16,16,384]{3,2,1,0:T(8,128)(2,1)} %refs_0_.1, ...), custom_call_target="tpu_custom_call" | custom-call | tf_op jit(solution)/shard_map/near/pallas_call | solution.py:53
  1.8 0.1 collective-permute-start
  1.9 2.5 %collective-permute-start.1 = (bf16[2,4,16,384]{3,2,1,0:T(8,128)(2,1)S(1)}, bf16[2,4,16,384]{3,2,1,0:T(8,128)(2,1)S(1)}, u32[]{:S(2)}, u32[]{:S(2)}) collective-permute-start(bf16[2,4,16,384]{3,2,1,0:T(8,128)(2,1)S(1)} %get-tuple-element.90), channel_id=1, source_target_pairs={{1,2},{2,1},{5,6},{6,5},{9,10},{10,9},{13,14},{14,13},{17,18},{18,... | collective-permute-start | bytes 294920 | tf_op jit(solution)/shard_map/ppermute | solution.py:751
  4.4 3.7 %stage.1 = (f32[2,288,384]{2,1,0:T(8,128)S(1)}, f32[512,128]{1,0:T(8,128)S(1)}, f32[8,384]{1,0:T(8,128)S(1)}, f32[8,1536]{1,0:T(8,128)S(1)}, f32[8,128]{1,0:T(8,...) custom-call(bf16[2,16,16,384]{3,2,1,0:T(8,128)(2,1)S(1)} %get-tuple-, ...), custom_call_target="tpu_custom_call" | custom-call | flops 10000000000 | bytes 4718592 | tf_op jit(solution)/shard_map/stage/pallas_call | solution.py:200
  8.2 0.0 collective-permute-done.refs_1_
  8.2 0.0 collective-permute-done.1.refs_2_
  8.2 0.7 %collective-permute-start.3 = (bf16[256,256]{1,0:T(8,128)(2,1)S(1)}, bf16[256,256]{1,0:T(8,128)(2,1)S(1)}, u32[]{:S(2)}, u32[]{:S(2)}) collective-permute-start(bf16[256,256]{1,0:T(8,128)(2,1)S(1)} %get-tuple-element.100.refs_6_), channel_id=1, source_target_pairs={{0,4},{1,5},{2,6},{3,7},{16,20},{17,21},{18,22},{19,23}} | collective-permute-start | bytes 393224 | tf_op jit(solution)/shard_map/ppermute | solution.py:821
  8.9 0.7 %collective-permute-start.2 = (bf16[304,128]{1,0:T(8,128)(2,1)S(1)}, bf16[304,128]{1,0:T(8,128)(2,1)S(1)}, u32[]{:S(2)}, u32[]{:S(2)}) collective-permute-start(bf16[304,128]{1,0:T(8,128)(2,1)S(1)} %get-tuple-element.101.refs_18_.before), channel_id=1, source_target_pairs={{0,4},{1,5},{2,6},{3,7},{16,20},{17,21},{18,22},{19,23}} | collective-permute-start | bytes 233480 | tf_op jit(solution)/shard_map/ppermute | solution.py:822
  9.6 8.5 %block.3 = (f32[256,256]{1,0:T(8,128)S(1)}, f32[256,256]{1,0:T(8,128)S(1)}, f32[256,256]{1,0:T(8,128)S(1)}, f32[256,256]{1,0:T(8,128)S(1)}, f32[256,256]{1,0:T(8...) custom-call(f32[2,288,384]{2,1,0:T(8,128)S(1)} %get-tuple-element.88, ...), custom_call_target="tpu_custom_call", output_to_operand_aliasing={{0}: (12, {}), {1}: (13, {}), {2}: (14, {}), {3}: (15, {}),... | custom-call | flops 6643777536 | bytes 10616832 | tf_op jit(solution)/shard_map/block/pallas_call | solution.py:497
  18.2 0.0 collective-permute-done.3.arrived.refs_0_
  18.2 0.2 relay.2
  18.3 0.7 %collective-permute-start.5 = (bf16[256,256]{1,0:T(8,128)(2,1)S(1)}, bf16[256,256]{1,0:T(8,128)(2,1)S(1)}, u32[]{:S(2)}, u32[]{:S(2)}) collective-permute-start(bf16[256,256]{1,0:T(8,128)(2,1)S(1)} %get-tuple-element.129.refs_12_), channel_id=1, source_target_pairs={{4,8},{5,9},{6,10},{7,11},{20,24},{21,25},{22,26},{23,27}} | collective-permute-start | bytes 393224 | tf_op jit(solution)/shard_map/ppermute | solution.py:821
  19.0 2.5 %later.5 = (f32[256,128]{1,0:T(8,128)S(1)}, f32[256,128]{1,0:T(8,128)S(1)}, f32[256,128]{1,0:T(8,128)S(1)}, f32[256,128]{1,0:T(8,128)S(1)}, f32[256,128]{1,0:T(8,128)S(1)}, /*index=5*/f32[256,128]{1,0:T(8,128)S(1)}) custom-call(bf16[512,3456]{1,0:T(8,128)(2,1)S(1)} %get-tuple-element.1, ...), custom_call_target="tpu_custom_call", output_to_operand_aliasing={{0}: (6, {}), {1}: (7, {}), {2}: (8, {}), {3}: (9, {}), {4}... | custom-call | flops 10000000000 | tf_op jit(solution)/shard_map/later/pallas_call | solution.py:546
  21.5 0.0 collective-permute-done.2.arrived.refs_0_
  21.5 0.3 relay_later.2.before
  21.8 0.7 %collective-permute-start.4 = (bf16[304,128]{1,0:T(8,128)(2,1)S(1)}, bf16[304,128]{1,0:T(8,128)(2,1)S(1)}, u32[]{:S(2)}, u32[]{:S(2)}) collective-permute-start(bf16[304,128]{1,0:T(8,128)(2,1)S(1)} %relay_later.2.before), channel_id=1, source_target_pairs={{4,8},{5,9},{6,10},{7,11},{20,24},{21,25},{22,26},{23,27}} | collective-permute-start | bytes 233480 | tf_op jit(solution)/shard_map/ppermute | solution.py:822
  22.4 0.0 collective-permute-done.5.arrived.refs_1_
  22.4 0.2 relay.3
  22.6 1.3 %collective-permute-start.7 = (bf16[256,256]{1,0:T(8,128)(2,1)S(1)}, bf16[256,256]{1,0:T(8,128)(2,1)S(1)}, u32[]{:S(2)}, u32[]{:S(2)}) collective-permute-start(bf16[256,256]{1,0:T(8,128)(2,1)S(1)} %get-tuple-element.141), channel_id=1, source_target_pairs={{8,12},{9,13},{10,14},{11,15},{24,28},{25,29},{26,30},{27,31}} | collective-permute-start | bytes 393224 | tf_op jit(solution)/shard_map/ppermute | solution.py:821
  23.9 0.0 collective-permute-done.4.arrived.refs_1_
  23.9 0.3 relay_later.3
  24.2 1.3 %collective-permute-start.6 = (bf16[304,128]{1,0:T(8,128)(2,1)S(1)}, bf16[304,128]{1,0:T(8,128)(2,1)S(1)}, u32[]{:S(2)}, u32[]{:S(2)}) collective-permute-start(bf16[304,128]{1,0:T(8,128)(2,1)S(1)} %relay_later.3), channel_id=1, source_target_pairs={{8,12},{9,13},{10,14},{11,15},{24,28},{25,29},{26,30},{27,31}} | collective-permute-start | bytes 233480 | tf_op jit(solution)/shard_map/ppermute | solution.py:822
  25.5 6.9 %collective-permute-done.7.refs_2_ = bf16[256,256]{1,0:T(8,128)(2,1)S(1)} collective-permute-done((bf16[256,256]{1,0:T(8,128)(2,1)S(1)}, bf16[256,256]{1,0:T(8,128)(2,1)S(1)}, u32[]{:S(2)}, u32[]{:S(2)}) %collective-permute-start.7) | collective-permute-done | bytes 131104 | tf_op jit(solution)/shard_map/ppermute | solution.py:821
  32.4 0.9 %final_early.1 = (bf16[2,256,384]{2,1,0:T(8,128)(2,1)}, f32[8,256]{1,0:T(8,128)S(1)}, bf16[384,8]{1,0:T(8,128)(2,1)S(1)}, bf16[8,384]{1,0:T(8,128)(2,1)S(1)}) custom-call(bf16[256,256]{1,0:T(8,128)(2,1)S(1)} %collective-permute-done.3.arrived.refs_0_, bf16[256,256]{1,0:T(8,128)(2,1)S(1)} %collective-permute-done.5.arrived.refs_1_, ...), custom_call_target="tpu_custom_call" | custom-call | flops 10000000000 | tf_op jit(solution)/shard_map/final_early/pallas_call | solution.py:852
  33.3 0.1 collective-permute-done.6.refs_2_
  33.4 1.5 %final.1 = (bf16[2,256,384]{2,1,0:T(8,128)(2,1)}, bf16[2,384]{1,0:T(2,128)(2,1)}) custom-call(bf16[304,128]{1,0:T(8,128)(2,1)S(1)} %collective-permute-done.2.arrived.refs_0_, bf16[304,128]{1,0:T(8,128)(2,1)S(1)} %collective-permute-done.4.arrived.refs_1_, bf16[304,128]{1,0:T(8,128)(2,1)S(1)} %collective-permute-done.6.refs_2_, ...), custom_call_target="tpu_custom_call", output_to_operand_aliasing={{0}: (17, {})} | custom-call | tf_op jit(solution)/shard_map/final/pallas_call | solution.py:870
  (3 shorter events, 0.1 us)
Async XLA Ops:
  1.8 6.4 %collective-permute-start = (bf16[2,4,16,384]{3,2,1,0:T(8,128)(2,1)S(1)}, bf16[2,4,16,384]{3,2,1,0:T(8,128)(2,1)S(1)}, u32[]{:S(2)}, u32[]{:S(2)}) collective-permute-start(bf16[2,4,16,384]{3,2,1,0:T(8,128)(2,1)S(1)} %get-tuple-element.89), channel_id=1, source_target_pairs={{0,1},{1,0},{2,3},{3,2},{4,5},{5,4},{6,7},{7,6},{8,9},{9,8},{10,11... | collective-permute-start | bytes 294920 | tf_op jit(solution)/shard_map/ppermute | solution.py:750
  1.9 6.3 %collective-permute-start.1 = (bf16[2,4,16,384]{3,2,1,0:T(8,128)(2,1)S(1)}, bf16[2,4,16,384]{3,2,1,0:T(8,128)(2,1)S(1)}, u32[]{:S(2)}, u32[]{:S(2)}) collective-permute-start(bf16[2,4,16,384]{3,2,1,0:T(8,128)(2,1)S(1)} %get-tuple-element.90), channel_id=1, source_target_pairs={{1,2},{2,1},{5,6},{6,5},{9,10},{10,9},{13,14},{14,13},{17,18},{18,... | collective-permute-start | bytes 294920 | tf_op jit(solution)/shard_map/ppermute | solution.py:751
  8.2 9.9 %collective-permute-start.3 = (bf16[256,256]{1,0:T(8,128)(2,1)S(1)}, bf16[256,256]{1,0:T(8,128)(2,1)S(1)}, u32[]{:S(2)}, u32[]{:S(2)}) collective-permute-start(bf16[256,256]{1,0:T(8,128)(2,1)S(1)} %get-tuple-element.100.refs_6_), channel_id=1, source_target_pairs={{0,4},{1,5},{2,6},{3,7},{16,20},{17,21},{18,22},{19,23}} | collective-permute-start | bytes 393224 | tf_op jit(solution)/shard_map/ppermute | solution.py:821
  8.9 12.6 %collective-permute-start.2 = (bf16[304,128]{1,0:T(8,128)(2,1)S(1)}, bf16[304,128]{1,0:T(8,128)(2,1)S(1)}, u32[]{:S(2)}, u32[]{:S(2)}) collective-permute-start(bf16[304,128]{1,0:T(8,128)(2,1)S(1)} %get-tuple-element.101.refs_18_.before), channel_id=1, source_target_pairs={{0,4},{1,5},{2,6},{3,7},{16,20},{17,21},{18,22},{19,23}} | collective-permute-start | bytes 233480 | tf_op jit(solution)/shard_map/ppermute | solution.py:822
  18.3 4.1 %collective-permute-start.5 = (bf16[256,256]{1,0:T(8,128)(2,1)S(1)}, bf16[256,256]{1,0:T(8,128)(2,1)S(1)}, u32[]{:S(2)}, u32[]{:S(2)}) collective-permute-start(bf16[256,256]{1,0:T(8,128)(2,1)S(1)} %get-tuple-element.129.refs_12_), channel_id=1, source_target_pairs={{4,8},{5,9},{6,10},{7,11},{20,24},{21,25},{22,26},{23,27}} | collective-permute-start | bytes 393224 | tf_op jit(solution)/shard_map/ppermute | solution.py:821
  21.8 2.1 %collective-permute-start.4 = (bf16[304,128]{1,0:T(8,128)(2,1)S(1)}, bf16[304,128]{1,0:T(8,128)(2,1)S(1)}, u32[]{:S(2)}, u32[]{:S(2)}) collective-permute-start(bf16[304,128]{1,0:T(8,128)(2,1)S(1)} %relay_later.2.before), channel_id=1, source_target_pairs={{4,8},{5,9},{6,10},{7,11},{20,24},{21,25},{22,26},{23,27}} | collective-permute-start | bytes 233480 | tf_op jit(solution)/shard_map/ppermute | solution.py:822
  22.6 9.8 %collective-permute-start.7 = (bf16[256,256]{1,0:T(8,128)(2,1)S(1)}, bf16[256,256]{1,0:T(8,128)(2,1)S(1)}, u32[]{:S(2)}, u32[]{:S(2)}) collective-permute-start(bf16[256,256]{1,0:T(8,128)(2,1)S(1)} %get-tuple-element.141), channel_id=1, source_target_pairs={{8,12},{9,13},{10,14},{11,15},{24,28},{25,29},{26,30},{27,31}} | collective-permute-start | bytes 393224 | tf_op jit(solution)/shard_map/ppermute | solution.py:821
  24.2 9.2 %collective-permute-start.6 = (bf16[304,128]{1,0:T(8,128)(2,1)S(1)}, bf16[304,128]{1,0:T(8,128)(2,1)S(1)}, u32[]{:S(2)}, u32[]{:S(2)}) collective-permute-start(bf16[304,128]{1,0:T(8,128)(2,1)S(1)} %relay_later.3), channel_id=1, source_target_pairs={{8,12},{9,13},{10,14},{11,15},{24,28},{25,29},{26,30},{27,31}} | collective-permute-start | bytes 233480 | tf_op jit(solution)/shard_map/ppermute | solution.py:822

commit v9 on v8

--- a/solution.py
+++ b/solution.py
@@ -775,8 +775,7 @@
     (send, pooled), state_near, weighed = blocks(first, [], [])
     (send_far,), state_far = run_later(early, first, staged, pooled, weighed, tail, [], [send])
     if short_chain:
-        _, state_near, weighed = blocks((1, stages), state_near, [send_far])
-        _, state_far = run_later(early, (1, 2), staged, pooled, weighed, tail, state_far, [])
+        _, state_near, weighed = blocks((1, 2), state_near, [send_far])
     vmem = pl.BlockSpec(memory_space=pltpu.VMEM)
     params = pltpu.CompilerParams(vmem_limit_bytes=16 * 2**20)
     cost = pl.CostEstimate(flops=10**10, bytes_accessed=0, transcendentals=0)
@@ -813,9 +812,15 @@
             link = [(stage, stage + 1)]
             if stage > 0:
                 send, pooled = relay(arrived[-1], send_far)
+                if stage == 1:
+                    _, state_far = run_later(
+                        early, (1, 2), staged, pooled, weighed, tail, state_far, [send]
+                    )
                 if stage == 1 and stages > 2:
+                    turn = (2, stages)
+                    _, state_near, weighed = blocks(turn, state_near, [send])
                     _, state_far = run_later(
-                        early, (2, stages), staged, pooled, weighed, tail, state_far, [send]
+                        early, turn, staged, pooled, weighed, tail, state_far, []
                     )
                 send_far = relay_later(stage, arrived_far[-1], pooled, state_far)
             arrived.append(lax.ppermute(send, "epoch", link))

time: 35.7 us -> 36.1 us (1.011); the launches traced: 35.1 us -> 35.9 us
  waiting for transfers between devices: 7.07 us -> 7.6 us
    ppermute x3, waiting for transfers between devices: 0.15 us -> 1.55 us  [body(): arrived_far.append(lax.ppermute(send_far, 'epoch', link))]
    ppermute x3, waiting for transfers between devices: 6.92 us -> 6.04 us  [body(): arrived.append(lax.ppermute(send, 'epoch', link))]
    pallas_call x2 -> x3, Pallas kernels: 8.56 us -> 8.82 us  [run_block(): pl.pallas_call(functools.partial(block_kernel, tiles, turn, 12 + len(kept...]
where the time goes in v9:
time: 36.1 us; the launch traced here: 35.9 us
  Pallas kernels  19.4 us (54%)
  starting transfers between devices  7.84 us (22%)
  waiting for transfers between devices  7.6 us (21%)
  between operations  1.01 us (3%)
    pallas_call x3, Pallas kernels, run_block(): pl.pallas_call(functools.partial(block_kernel, tiles, turn, 12 + len(kept...  8.82 us
    ppermute x3, waiting for transfers between devices, body(): arrived.append(lax.ppermute(send, 'epoch', link))  6.04 us
    pallas_call x1, Pallas kernels, run_stage(): pl.pallas_call(stage_kernel, name='stage', out_shape=out_shape, in_specs=...  3.72 us
    ppermute x3, starting transfers between devices, body(): arrived.append(lax.ppermute(send, 'epoch', link))  2.63 us
    ppermute x3, starting transfers between devices, body(): arrived_far.append(lax.ppermute(send_far, 'epoch', link))  2.61 us
    ppermute x1, starting transfers between devices, body(): recv_next = lax.ppermute(to_next, 'tile', pairs(tiles, 1))  2.53 us
    pallas_call x3, Pallas kernels, run_later(): pl.pallas_call(functools.partial(later_kernel, early, turn, 6 + len(kept)...  2.52 us
    ppermute x3, waiting for transfers between devices, body(): arrived_far.append(lax.ppermute(send_far, 'epoch', link))  1.55 us
  transfers between devices with their start and end apart: 8, of which 2 were waited for; matrix products, arithmetic and copies ran while one was open for 0% of the time, Pallas kernels for 47%

profile of v9, /device:TPU:30, one launch (start us, length us, event | category | flops | bytes accessed | tf_op | source)
XLA Modules:
  0.0 35.9 jit_solution(3344490098513338046)
XLA Ops:
  0.6 1.2 %near.1 = (bf16[2,16,16,384]{3,2,1,0:T(8,128)(2,1)S(1)}, f32[7,7,384]{2,1,0:T(8,128)S(1)}, s32[2,16,16]{2,1,0:T(8,128)S(1)}, s32[8]{0:T(128)S(1)}, f32[8]{0:T(12...) custom-call(bf16[2,16,16,384]{3,2,1,0:T(8,128)(2,1)} %refs_0_.1, ...), custom_call_target="tpu_custom_call" | custom-call | tf_op jit(solution)/shard_map/near/pallas_call | solution.py:53
  1.8 0.1 collective-permute-start
  1.9 2.5 %collective-permute-start.1 = (bf16[2,4,16,384]{3,2,1,0:T(8,128)(2,1)S(1)}, bf16[2,4,16,384]{3,2,1,0:T(8,128)(2,1)S(1)}, u32[]{:S(2)}, u32[]{:S(2)}) collective-permute-start(bf16[2,4,16,384]{3,2,1,0:T(8,128)(2,1)S(1)} %get-tuple-element.98), channel_id=1, source_target_pairs={{1,2},{2,1},{5,6},{6,5},{9,10},{10,9},{13,14},{14,13},{17,18},{18,... | collective-permute-start | bytes 294920 | tf_op jit(solution)/shard_map/ppermute | solution.py:751
  4.4 3.7 %stage.1 = (f32[2,288,384]{2,1,0:T(8,128)S(1)}, f32[512,128]{1,0:T(8,128)S(1)}, f32[8,384]{1,0:T(8,128)S(1)}, f32[8,1536]{1,0:T(8,128)S(1)}, f32[8,128]{1,0:T(8,...) custom-call(bf16[2,16,16,384]{3,2,1,0:T(8,128)(2,1)S(1)} %get-tuple-, ...), custom_call_target="tpu_custom_call" | custom-call | flops 10000000000 | bytes 4718592 | tf_op jit(solution)/shard_map/stage/pallas_call | solution.py:200
  8.2 0.0 collective-permute-done.refs_1_
  8.2 0.0 collective-permute-done.1.refs_2_
  8.2 0.7 %collective-permute-start.3 = (bf16[256,256]{1,0:T(8,128)(2,1)S(1)}, bf16[256,256]{1,0:T(8,128)(2,1)S(1)}, u32[]{:S(2)}, u32[]{:S(2)}) collective-permute-start(bf16[256,256]{1,0:T(8,128)(2,1)S(1)} %get-tuple-element.108.refs_6_), channel_id=1, source_target_pairs={{0,4},{1,5},{2,6},{3,7},{16,20},{17,21},{18,22},{19,23}} | collective-permute-start | bytes 393224 | tf_op jit(solution)/shard_map/ppermute | solution.py:826
  8.9 0.7 %collective-permute-start.2 = (bf16[304,128]{1,0:T(8,128)(2,1)S(1)}, bf16[304,128]{1,0:T(8,128)(2,1)S(1)}, u32[]{:S(2)}, u32[]{:S(2)}) collective-permute-start(bf16[304,128]{1,0:T(8,128)(2,1)S(1)} %get-tuple-element.109.refs_18_.before), channel_id=1, source_target_pairs={{0,4},{1,5},{2,6},{3,7},{16,20},{17,21},{18,22},{19,23}} | collective-permute-start | bytes 233480 | tf_op jit(solution)/shard_map/ppermute | solution.py:827
  9.6 0.2 block.4
  9.8 0.0 collective-permute-done.3.arrived.refs_0_
  9.8 0.2 relay.2
  10.0 0.7 %collective-permute-start.5 = (bf16[256,256]{1,0:T(8,128)(2,1)S(1)}, bf16[256,256]{1,0:T(8,128)(2,1)S(1)}, u32[]{:S(2)}, u32[]{:S(2)}) collective-permute-start(bf16[256,256]{1,0:T(8,128)(2,1)S(1)} %get-tuple-element.122.refs_18_.refs_12_), channel_id=1, source_target_pairs={{4,8},{5,9},{6,10},{7,11},{20,24},{21,25},{22,26},{23,27}} | collective-permute-start | bytes 393224 | tf_op jit(solution)/shard_map/ppermute | solution.py:826
  10.7 8.6 %block.5 = (f32[256,256]{1,0:T(8,128)S(1)}, f32[256,256]{1,0:T(8,128)S(1)}, f32[256,256]{1,0:T(8,128)S(1)}, f32[256,256]{1,0:T(8,128)S(1)}, f32[256,256]{1,0:T(8...) custom-call(f32[2,288,384]{2,1,0:T(8,128)S(1)} %get-tuple-element.96, ...), custom_call_target="tpu_custom_call", output_to_operand_aliasing={{0}: (12, {}), {1}: (13, {}), {2}: (14, {}), {3}: (15, {}),... | custom-call | flops 6643777536 | bytes 10616832 | tf_op jit(solution)/shard_map/block/pallas_call | solution.py:497
  19.3 2.5 %later.5 = (f32[256,128]{1,0:T(8,128)S(1)}, f32[256,128]{1,0:T(8,128)S(1)}, f32[256,128]{1,0:T(8,128)S(1)}, f32[256,128]{1,0:T(8,128)S(1)}, f32[256,128]{1,0:T(8,128)S(1)}, /*index=5*/f32[256,128]{1,0:T(8,128)S(1)}) custom-call(bf16[512,3456]{1,0:T(8,128)(2,1)S(1)} %get-tuple-element.1, ...), custom_call_target="tpu_custom_call", output_to_operand_aliasing={{0}: (6, {}), {1}: (7, {}), {2}: (8, {}), {3}: (9, {}), {4}... | custom-call | flops 10000000000 | tf_op jit(solution)/shard_map/later/pallas_call | solution.py:546
  21.8 0.0 collective-permute-done.2.arrived.refs_0_
  21.8 0.3 relay_later.2.before
  22.0 0.7 %collective-permute-start.4 = (bf16[304,128]{1,0:T(8,128)(2,1)S(1)}, bf16[304,128]{1,0:T(8,128)(2,1)S(1)}, u32[]{:S(2)}, u32[]{:S(2)}) collective-permute-start(bf16[304,128]{1,0:T(8,128)(2,1)S(1)} %relay_later.2.before), channel_id=1, source_target_pairs={{4,8},{5,9},{6,10},{7,11},{20,24},{21,25},{22,26},{23,27}} | collective-permute-start | bytes 233480 | tf_op jit(solution)/shard_map/ppermute | solution.py:827
  22.7 0.0 collective-permute-done.5.arrived.refs_1_
  22.7 0.2 relay.3
  22.9 1.3 %collective-permute-start.7 = (bf16[256,256]{1,0:T(8,128)(2,1)S(1)}, bf16[256,256]{1,0:T(8,128)(2,1)S(1)}, u32[]{:S(2)}, u32[]{:S(2)}) collective-permute-start(bf16[256,256]{1,0:T(8,128)(2,1)S(1)} %get-tuple-element.157), channel_id=1, source_target_pairs={{8,12},{9,13},{10,14},{11,15},{24,28},{25,29},{26,30},{27,31}} | collective-permute-start | bytes 393224 | tf_op jit(solution)/shard_map/ppermute | solution.py:826
  24.2 0.0 collective-permute-done.4.arrived.refs_1_
  24.2 0.3 relay_later.3
  24.4 1.3 %collective-permute-start.6 = (bf16[304,128]{1,0:T(8,128)(2,1)S(1)}, bf16[304,128]{1,0:T(8,128)(2,1)S(1)}, u32[]{:S(2)}, u32[]{:S(2)}) collective-permute-start(bf16[304,128]{1,0:T(8,128)(2,1)S(1)} %relay_later.3), channel_id=1, source_target_pairs={{8,12},{9,13},{10,14},{11,15},{24,28},{25,29},{26,30},{27,31}} | collective-permute-start | bytes 233480 | tf_op jit(solution)/shard_map/ppermute | solution.py:827
  25.7 6.0 %collective-permute-done.7.refs_2_ = bf16[256,256]{1,0:T(8,128)(2,1)S(1)} collective-permute-done((bf16[256,256]{1,0:T(8,128)(2,1)S(1)}, bf16[256,256]{1,0:T(8,128)(2,1)S(1)}, u32[]{:S(2)}, u32[]{:S(2)}) %collective-permute-start.7) | collective-permute-done | bytes 131104 | tf_op jit(solution)/shard_map/ppermute | solution.py:826
  31.8 0.9 %final_early.1 = (bf16[2,256,384]{2,1,0:T(8,128)(2,1)}, f32[8,256]{1,0:T(8,128)S(1)}, bf16[384,8]{1,0:T(8,128)(2,1)S(1)}, bf16[8,384]{1,0:T(8,128)(2,1)S(1)}) custom-call(bf16[256,256]{1,0:T(8,128)(2,1)S(1)} %collective-permute-done.3.arrived.refs_0_, bf16[256,256]{1,0:T(8,128)(2,1)S(1)} %collective-permute-done.5.arrived.refs_1_, ...), custom_call_target="tpu_custom_call" | custom-call | flops 10000000000 | tf_op jit(solution)/shard_map/final_early/pallas_call | solution.py:857
  32.7 1.5 %collective-permute-done.6.refs_2_ = bf16[304,128]{1,0:T(8,128)(2,1)S(1)} collective-permute-done((bf16[304,128]{1,0:T(8,128)(2,1)S(1)}, bf16[304,128]{1,0:T(8,128)(2,1)S(1)}, u32[]{:S(2)}, u32[]{:S(2)}) %collective-permute-start.6) | collective-permute-done | bytes 77856 | tf_op jit(solution)/shard_map/ppermute | solution.py:827
  34.2 1.5 %final.1 = (bf16[2,256,384]{2,1,0:T(8,128)(2,1)}, bf16[2,384]{1,0:T(2,128)(2,1)}) custom-call(bf16[304,128]{1,0:T(8,128)(2,1)S(1)} %collective-permute-done.2.arrived.refs_0_, bf16[304,128]{1,0:T(8,128)(2,1)S(1)} %collective-permute-done.4.arrived.refs_1_, bf16[304,128]{1,0:T(8,128)(2,1)S(1)} %collective-permute-done.6.refs_2_, ...), custom_call_target="tpu_custom_call", output_to_operand_aliasing={{0}: (17, {})} | custom-call | tf_op jit(solution)/shard_map/final/pallas_call | solution.py:875
  (3 shorter events, 0.1 us)
Async XLA Ops:
  1.8 6.4 %collective-permute-start = (bf16[2,4,16,384]{3,2,1,0:T(8,128)(2,1)S(1)}, bf16[2,4,16,384]{3,2,1,0:T(8,128)(2,1)S(1)}, u32[]{:S(2)}, u32[]{:S(2)}) collective-permute-start(bf16[2,4,16,384]{3,2,1,0:T(8,128)(2,1)S(1)} %get-tuple-element.97), channel_id=1, source_target_pairs={{0,1},{1,0},{2,3},{3,2},{4,5},{5,4},{6,7},{7,6},{8,9},{9,8},{10,11... | collective-permute-start | bytes 294920 | tf_op jit(solution)/shard_map/ppermute | solution.py:750
  1.9 6.3 %collective-permute-start.1 = (bf16[2,4,16,384]{3,2,1,0:T(8,128)(2,1)S(1)}, bf16[2,4,16,384]{3,2,1,0:T(8,128)(2,1)S(1)}, u32[]{:S(2)}, u32[]{:S(2)}) collective-permute-start(bf16[2,4,16,384]{3,2,1,0:T(8,128)(2,1)S(1)} %get-tuple-element.98), channel_id=1, source_target_pairs={{1,2},{2,1},{5,6},{6,5},{9,10},{10,9},{13,14},{14,13},{17,18},{18,... | collective-permute-start | bytes 294920 | tf_op jit(solution)/shard_map/ppermute | solution.py:751
  8.2 1.6 %collective-permute-start.3 = (bf16[256,256]{1,0:T(8,128)(2,1)S(1)}, bf16[256,256]{1,0:T(8,128)(2,1)S(1)}, u32[]{:S(2)}, u32[]{:S(2)}) collective-permute-start(bf16[256,256]{1,0:T(8,128)(2,1)S(1)} %get-tuple-element.108.refs_6_), channel_id=1, source_target_pairs={{0,4},{1,5},{2,6},{3,7},{16,20},{17,21},{18,22},{19,23}} | collective-permute-start | bytes 393224 | tf_op jit(solution)/shard_map/ppermute | solution.py:826
  8.9 12.8 %collective-permute-start.2 = (bf16[304,128]{1,0:T(8,128)(2,1)S(1)}, bf16[304,128]{1,0:T(8,128)(2,1)S(1)}, u32[]{:S(2)}, u32[]{:S(2)}) collective-permute-start(bf16[304,128]{1,0:T(8,128)(2,1)S(1)} %get-tuple-element.109.refs_18_.before), channel_id=1, source_target_pairs={{0,4},{1,5},{2,6},{3,7},{16,20},{17,21},{18,22},{19,23}} | collective-permute-start | bytes 233480 | tf_op jit(solution)/shard_map/ppermute | solution.py:827
  10.0 12.7 %collective-permute-start.5 = (bf16[256,256]{1,0:T(8,128)(2,1)S(1)}, bf16[256,256]{1,0:T(8,128)(2,1)S(1)}, u32[]{:S(2)}, u32[]{:S(2)}) collective-permute-start(bf16[256,256]{1,0:T(8,128)(2,1)S(1)} %get-tuple-element.122.refs_18_.refs_12_), channel_id=1, source_target_pairs={{4,8},{5,9},{6,10},{7,11},{20,24},{21,25},{22,26},{23,27}} | collective-permute-start | bytes 393224 | tf_op jit(solution)/shard_map/ppermute | solution.py:826
  22.0 2.1 %collective-permute-start.4 = (bf16[304,128]{1,0:T(8,128)(2,1)S(1)}, bf16[304,128]{1,0:T(8,128)(2,1)S(1)}, u32[]{:S(2)}, u32[]{:S(2)}) collective-permute-start(bf16[304,128]{1,0:T(8,128)(2,1)S(1)} %relay_later.2.before), channel_id=1, source_target_pairs={{4,8},{5,9},{6,10},{7,11},{20,24},{21,25},{22,26},{23,27}} | collective-permute-start | bytes 233480 | tf_op jit(solution)/shard_map/ppermute | solution.py:827
  22.9 8.9 %collective-permute-start.7 = (bf16[256,256]{1,0:T(8,128)(2,1)S(1)}, bf16[256,256]{1,0:T(8,128)(2,1)S(1)}, u32[]{:S(2)}, u32[]{:S(2)}) collective-permute-start(bf16[256,256]{1,0:T(8,128)(2,1)S(1)} %get-tuple-element.157), channel_id=1, source_target_pairs={{8,12},{9,13},{10,14},{11,15},{24,28},{25,29},{26,30},{27,31}} | collective-permute-start | bytes 393224 | tf_op jit(solution)/shard_map/ppermute | solution.py:826
  24.4 9.8 %collective-permute-start.6 = (bf16[304,128]{1,0:T(8,128)(2,1)S(1)}, bf16[304,128]{1,0:T(8,128)(2,1)S(1)}, u32[]{:S(2)}, u32[]{:S(2)}) collective-permute-start(bf16[304,128]{1,0:T(8,128)(2,1)S(1)} %relay_later.3), channel_id=1, source_target_pairs={{8,12},{9,13},{10,14},{11,15},{24,28},{25,29},{26,30},{27,31}} | collective-permute-start | bytes 233480 | tf_op jit(solution)/shard_map/ppermute | solution.py:827

commit v10 on v8

--- a/solution.py
+++ b/solution.py
@@ -364,12 +364,11 @@
                     ]
 
     state = (decay0, inflow0, keep, block, open0, open1)
+    for copy in gate_copies:
+        copy.wait()
     cells_of(0, 0, taps, w_first, mask, short_rows, long_rows, send, pooled, state)
     for j in range(1, early):
-        gate_copies[j - 1].wait()
         cells_of(j, j, taps, w_gates.at[j - 1], mask, short_rows, long_rows, send, pooled, state)
-    for copy in gate_copies[early - 1 :]:
-        copy.wait()
 
 
 def gates_of(preact):

time: 35.7 us -> 35.5 us (level)
  the two profiles are of different devices: /device:TPU:30 before, /device:TPU:29 now
where the time goes in v10:
time: 35.5 us; the launch traced here: 35.3 us
  Pallas kernels  18.9 us (53%)
  starting transfers between devices  9 us (25%)
  waiting for transfers between devices  6.38 us (18%)
  between operations  0.98 us (3%)
    pallas_call x2, Pallas kernels, run_block(): pl.pallas_call(functools.partial(block_kernel, tiles, turn, 12 + len(kept...  8.3 us
    ppermute x3, waiting for transfers between devices, body(): arrived.append(lax.ppermute(send, 'epoch', link))  6.37 us
    pallas_call x1, Pallas kernels, run_stage(): pl.pallas_call(stage_kernel, name='stage', out_shape=out_shape, in_specs=...  3.73 us
    ppermute x1, starting transfers between devices, body(): recv_next = lax.ppermute(to_next, 'tile', pairs(tiles, 1))  3.02 us
    ppermute x3, starting transfers between devices, body(): arrived.append(lax.ppermute(send, 'epoch', link))  2.63 us
    ppermute x3, starting transfers between devices, body(): arrived_far.append(lax.ppermute(send_far, 'epoch', link))  2.61 us
    pallas_call x3, Pallas kernels, run_later(): pl.pallas_call(functools.partial(later_kernel, early, turn, 6 + len(kept)...  2.52 us
    pallas_call x1, Pallas kernels, body(): pl.pallas_call(functools.partial(final_kernel, len(arrived)), name='final...  1.51 us
  transfers between devices with their start and end apart: 8, of which 1 were waited for; matrix products, arithmetic and copies ran while one was open for 0% of the time, Pallas kernels for 46%

profile of v10, /device:TPU:29, one launch (start us, length us, event | category | flops | bytes accessed | tf_op | source)
XLA Modules:
  0.0 35.3 jit_solution(12021517117989508100)
XLA Ops:
  0.6 1.2 %near.1 = (bf16[2,16,16,384]{3,2,1,0:T(8,128)(2,1)S(1)}, f32[7,7,384]{2,1,0:T(8,128)S(1)}, s32[2,16,16]{2,1,0:T(8,128)S(1)}, s32[8]{0:T(128)S(1)}, f32[8]{0:T(12...) custom-call(bf16[2,16,16,384]{3,2,1,0:T(8,128)(2,1)} %refs_0_.1, ...), custom_call_target="tpu_custom_call" | custom-call | tf_op jit(solution)/shard_map/near/pallas_call | solution.py:53
  1.8 0.7 %collective-permute-start = (bf16[2,4,16,384]{3,2,1,0:T(8,128)(2,1)S(1)}, bf16[2,4,16,384]{3,2,1,0:T(8,128)(2,1)S(1)}, u32[]{:S(2)}, u32[]{:S(2)}) collective-permute-start(bf16[2,4,16,384]{3,2,1,0:T(8,128)(2,1)S(1)} %get-tuple-element.89), channel_id=1, source_target_pairs={{0,1},{1,0},{2,3},{3,2},{4,5},{5,4},{6,7},{7,6},{8,9},{9,8},{10,11... | collective-permute-start | bytes 294920 | tf_op jit(solution)/shard_map/ppermute | solution.py:749
  2.5 3.0 %collective-permute-start.1 = (bf16[2,4,16,384]{3,2,1,0:T(8,128)(2,1)S(1)}, bf16[2,4,16,384]{3,2,1,0:T(8,128)(2,1)S(1)}, u32[]{:S(2)}, u32[]{:S(2)}) collective-permute-start(bf16[2,4,16,384]{3,2,1,0:T(8,128)(2,1)S(1)} %get-tuple-element.90), channel_id=1, source_target_pairs={{1,2},{2,1},{5,6},{6,5},{9,10},{10,9},{13,14},{14,13},{17,18},{18,... | collective-permute-start | bytes 294920 | tf_op jit(solution)/shard_map/ppermute | solution.py:750
  5.6 3.7 %stage.1 = (f32[2,288,384]{2,1,0:T(8,128)S(1)}, f32[512,128]{1,0:T(8,128)S(1)}, f32[8,384]{1,0:T(8,128)S(1)}, f32[8,1536]{1,0:T(8,128)S(1)}, f32[8,128]{1,0:T(8,...) custom-call(bf16[2,16,16,384]{3,2,1,0:T(8,128)(2,1)S(1)} %get-tuple-, ...), custom_call_target="tpu_custom_call" | custom-call | flops 10000000000 | bytes 4718592 | tf_op jit(solution)/shard_map/stage/pallas_call | solution.py:200
  9.3 0.0 collective-permute-done.refs_1_
  9.3 0.0 collective-permute-done.1.refs_2_
  9.4 0.7 %collective-permute-start.3 = (bf16[256,256]{1,0:T(8,128)(2,1)S(1)}, bf16[256,256]{1,0:T(8,128)(2,1)S(1)}, u32[]{:S(2)}, u32[]{:S(2)}) collective-permute-start(bf16[256,256]{1,0:T(8,128)(2,1)S(1)} %get-tuple-element.100.refs_6_), channel_id=1, source_target_pairs={{0,4},{1,5},{2,6},{3,7},{16,20},{17,21},{18,22},{19,23}} | collective-permute-start | bytes 393224 | tf_op jit(solution)/shard_map/ppermute | solution.py:820
  10.1 0.7 %collective-permute-start.2 = (bf16[304,128]{1,0:T(8,128)(2,1)S(1)}, bf16[304,128]{1,0:T(8,128)(2,1)S(1)}, u32[]{:S(2)}, u32[]{:S(2)}) collective-permute-start(bf16[304,128]{1,0:T(8,128)(2,1)S(1)} %get-tuple-element.101.refs_18_.before), channel_id=1, source_target_pairs={{0,4},{1,5},{2,6},{3,7},{16,20},{17,21},{18,22},{19,23}} | collective-permute-start | bytes 233480 | tf_op jit(solution)/shard_map/ppermute | solution.py:821
  10.8 8.3 %block.3 = (f32[256,256]{1,0:T(8,128)S(1)}, f32[256,256]{1,0:T(8,128)S(1)}, f32[256,256]{1,0:T(8,128)S(1)}, f32[256,256]{1,0:T(8,128)S(1)}, f32[256,256]{1,0:T(8...) custom-call(f32[2,288,384]{2,1,0:T(8,128)S(1)} %get-tuple-element.88, ...), custom_call_target="tpu_custom_call", output_to_operand_aliasing={{0}: (12, {}), {1}: (13, {}), {2}: (14, {}), {3}: (15, {}),... | custom-call | flops 6643777536 | bytes 10616832 | tf_op jit(solution)/shard_map/block/pallas_call | solution.py:496
  19.0 0.0 collective-permute-done.3.arrived.refs_0_
  19.1 0.2 relay.2
  19.2 0.7 %collective-permute-start.5 = (bf16[256,256]{1,0:T(8,128)(2,1)S(1)}, bf16[256,256]{1,0:T(8,128)(2,1)S(1)}, u32[]{:S(2)}, u32[]{:S(2)}) collective-permute-start(bf16[256,256]{1,0:T(8,128)(2,1)S(1)} %get-tuple-element.129.refs_12_), channel_id=1, source_target_pairs={{4,8},{5,9},{6,10},{7,11},{20,24},{21,25},{22,26},{23,27}} | collective-permute-start | bytes 393224 | tf_op jit(solution)/shard_map/ppermute | solution.py:820
  19.9 2.5 %later.5 = (f32[256,128]{1,0:T(8,128)S(1)}, f32[256,128]{1,0:T(8,128)S(1)}, f32[256,128]{1,0:T(8,128)S(1)}, f32[256,128]{1,0:T(8,128)S(1)}, f32[256,128]{1,0:T(8,128)S(1)}, /*index=5*/f32[256,128]{1,0:T(8,128)S(1)}) custom-call(bf16[512,3456]{1,0:T(8,128)(2,1)S(1)} %get-tuple-element.1, ...), custom_call_target="tpu_custom_call", output_to_operand_aliasing={{0}: (6, {}), {1}: (7, {}), {2}: (8, {}), {3}: (9, {}), {4}... | custom-call | flops 10000000000 | tf_op jit(solution)/shard_map/later/pallas_call | solution.py:545
  22.4 0.0 collective-permute-done.2.arrived.refs_0_
  22.4 0.3 relay_later.2.before
  22.6 0.7 %collective-permute-start.4 = (bf16[304,128]{1,0:T(8,128)(2,1)S(1)}, bf16[304,128]{1,0:T(8,128)(2,1)S(1)}, u32[]{:S(2)}, u32[]{:S(2)}) collective-permute-start(bf16[304,128]{1,0:T(8,128)(2,1)S(1)} %relay_later.2.before), channel_id=1, source_target_pairs={{4,8},{5,9},{6,10},{7,11},{20,24},{21,25},{22,26},{23,27}} | collective-permute-start | bytes 233480 | tf_op jit(solution)/shard_map/ppermute | solution.py:821
  23.3 0.0 collective-permute-done.5.arrived.refs_1_
  23.3 0.2 relay.3
  23.5 1.3 %collective-permute-start.7 = (bf16[256,256]{1,0:T(8,128)(2,1)S(1)}, bf16[256,256]{1,0:T(8,128)(2,1)S(1)}, u32[]{:S(2)}, u32[]{:S(2)}) collective-permute-start(bf16[256,256]{1,0:T(8,128)(2,1)S(1)} %get-tuple-element.141), channel_id=1, source_target_pairs={{8,12},{9,13},{10,14},{11,15},{24,28},{25,29},{26,30},{27,31}} | collective-permute-start | bytes 393224 | tf_op jit(solution)/shard_map/ppermute | solution.py:820
  24.8 0.0 collective-permute-done.4.arrived.refs_1_
  24.8 0.3 relay_later.3
  25.0 1.3 %collective-permute-start.6 = (bf16[304,128]{1,0:T(8,128)(2,1)S(1)}, bf16[304,128]{1,0:T(8,128)(2,1)S(1)}, u32[]{:S(2)}, u32[]{:S(2)}) collective-permute-start(bf16[304,128]{1,0:T(8,128)(2,1)S(1)} %relay_later.3), channel_id=1, source_target_pairs={{8,12},{9,13},{10,14},{11,15},{24,28},{25,29},{26,30},{27,31}} | collective-permute-start | bytes 233480 | tf_op jit(solution)/shard_map/ppermute | solution.py:821
  26.3 6.4 %collective-permute-done.7.refs_2_ = bf16[256,256]{1,0:T(8,128)(2,1)S(1)} collective-permute-done((bf16[256,256]{1,0:T(8,128)(2,1)S(1)}, bf16[256,256]{1,0:T(8,128)(2,1)S(1)}, u32[]{:S(2)}, u32[]{:S(2)}) %collective-permute-start.7) | collective-permute-done | bytes 131104 | tf_op jit(solution)/shard_map/ppermute | solution.py:820
  32.7 0.9 %final_early.1 = (bf16[2,256,384]{2,1,0:T(8,128)(2,1)}, f32[8,256]{1,0:T(8,128)S(1)}, bf16[384,8]{1,0:T(8,128)(2,1)S(1)}, bf16[8,384]{1,0:T(8,128)(2,1)S(1)}) custom-call(bf16[256,256]{1,0:T(8,128)(2,1)S(1)} %collective-permute-done.3.arrived.refs_0_, bf16[256,256]{1,0:T(8,128)(2,1)S(1)} %collective-permute-done.5.arrived.refs_1_, ...), custom_call_target="tpu_custom_call" | custom-call | flops 10000000000 | tf_op jit(solution)/shard_map/final_early/pallas_call | solution.py:851
  33.6 0.0 collective-permute-done.6.refs_2_
  33.6 1.5 %final.1 = (bf16[2,256,384]{2,1,0:T(8,128)(2,1)}, bf16[2,384]{1,0:T(2,128)(2,1)}) custom-call(bf16[304,128]{1,0:T(8,128)(2,1)S(1)} %collective-permute-done.2.arrived.refs_0_, bf16[304,128]{1,0:T(8,128)(2,1)S(1)} %collective-permute-done.4.arrived.refs_1_, bf16[304,128]{1,0:T(8,128)(2,1)S(1)} %collective-permute-done.6.refs_2_, ...), custom_call_target="tpu_custom_call", output_to_operand_aliasing={{0}: (17, {})} | custom-call | tf_op jit(solution)/shard_map/final/pallas_call | solution.py:869
  (3 shorter events, 0.1 us)
Async XLA Ops:
  1.8 7.5 %collective-permute-start = (bf16[2,4,16,384]{3,2,1,0:T(8,128)(2,1)S(1)}, bf16[2,4,16,384]{3,2,1,0:T(8,128)(2,1)S(1)}, u32[]{:S(2)}, u32[]{:S(2)}) collective-permute-start(bf16[2,4,16,384]{3,2,1,0:T(8,128)(2,1)S(1)} %get-tuple-element.89), channel_id=1, source_target_pairs={{0,1},{1,0},{2,3},{3,2},{4,5},{5,4},{6,7},{7,6},{8,9},{9,8},{10,11... | collective-permute-start | bytes 294920 | tf_op jit(solution)/shard_map/ppermute | solution.py:749
  2.5 6.8 %collective-permute-start.1 = (bf16[2,4,16,384]{3,2,1,0:T(8,128)(2,1)S(1)}, bf16[2,4,16,384]{3,2,1,0:T(8,128)(2,1)S(1)}, u32[]{:S(2)}, u32[]{:S(2)}) collective-permute-start(bf16[2,4,16,384]{3,2,1,0:T(8,128)(2,1)S(1)} %get-tuple-element.90), channel_id=1, source_target_pairs={{1,2},{2,1},{5,6},{6,5},{9,10},{10,9},{13,14},{14,13},{17,18},{18,... | collective-permute-start | bytes 294920 | tf_op jit(solution)/shard_map/ppermute | solution.py:750
  9.4 9.7 %collective-permute-start.3 = (bf16[256,256]{1,0:T(8,128)(2,1)S(1)}, bf16[256,256]{1,0:T(8,128)(2,1)S(1)}, u32[]{:S(2)}, u32[]{:S(2)}) collective-permute-start(bf16[256,256]{1,0:T(8,128)(2,1)S(1)} %get-tuple-element.100.refs_6_), channel_id=1, source_target_pairs={{0,4},{1,5},{2,6},{3,7},{16,20},{17,21},{18,22},{19,23}} | collective-permute-start | bytes 393224 | tf_op jit(solution)/shard_map/ppermute | solution.py:820
  10.1 12.3 %collective-permute-start.2 = (bf16[304,128]{1,0:T(8,128)(2,1)S(1)}, bf16[304,128]{1,0:T(8,128)(2,1)S(1)}, u32[]{:S(2)}, u32[]{:S(2)}) collective-permute-start(bf16[304,128]{1,0:T(8,128)(2,1)S(1)} %get-tuple-element.101.refs_18_.before), channel_id=1, source_target_pairs={{0,4},{1,5},{2,6},{3,7},{16,20},{17,21},{18,22},{19,23}} | collective-permute-start | bytes 233480 | tf_op jit(solution)/shard_map/ppermute | solution.py:821
  19.2 4.1 %collective-permute-start.5 = (bf16[256,256]{1,0:T(8,128)(2,1)S(1)}, bf16[256,256]{1,0:T(8,128)(2,1)S(1)}, u32[]{:S(2)}, u32[]{:S(2)}) collective-permute-start(bf16[256,256]{1,0:T(8,128)(2,1)S(1)} %get-tuple-element.129.refs_12_), channel_id=1, source_target_pairs={{4,8},{5,9},{6,10},{7,11},{20,24},{21,25},{22,26},{23,27}} | collective-permute-start | bytes 393224 | tf_op jit(solution)/shard_map/ppermute | solution.py:820
  22.6 2.1 %collective-permute-start.4 = (bf16[304,128]{1,0:T(8,128)(2,1)S(1)}, bf16[304,128]{1,0:T(8,128)(2,1)S(1)}, u32[]{:S(2)}, u32[]{:S(2)}) collective-permute-start(bf16[304,128]{1,0:T(8,128)(2,1)S(1)} %relay_later.2.before), channel_id=1, source_target_pairs={{4,8},{5,9},{6,10},{7,11},{20,24},{21,25},{22,26},{23,27}} | collective-permute-start | bytes 233480 | tf_op jit(solution)/shard_map/ppermute | solution.py:821
  23.5 9.2 %collective-permute-start.7 = (bf16[256,256]{1,0:T(8,128)(2,1)S(1)}, bf16[256,256]{1,0:T(8,128)(2,1)S(1)}, u32[]{:S(2)}, u32[]{:S(2)}) collective-permute-start(bf16[256,256]{1,0:T(8,128)(2,1)S(1)} %get-tuple-element.141), channel_id=1, source_target_pairs={{8,12},{9,13},{10,14},{11,15},{24,28},{25,29},{26,30},{27,31}} | collective-permute-start | bytes 393224 | tf_op jit(solution)/shard_map/ppermute | solution.py:820
  25.0 8.6 %collective-permute-start.6 = (bf16[304,128]{1,0:T(8,128)(2,1)S(1)}, bf16[304,128]{1,0:T(8,128)(2,1)S(1)}, u32[]{:S(2)}, u32[]{:S(2)}) collective-permute-start(bf16[304,128]{1,0:T(8,128)(2,1)S(1)} %relay_later.3), channel_id=1, source_target_pairs={{8,12},{9,13},{10,14},{11,15},{24,28},{25,29},{26,30},{27,31}} | collective-permute-start | bytes 233480 | tf_op jit(solution)/shard_map/ppermute | solution.py:821

commit v11 on v10

--- a/solution.py
+++ b/solution.py
@@ -340,7 +340,7 @@
         variance = jnp.mean(centred * centred, axis=-1, keepdims=True)
         normed = (centred * lax.rsqrt(variance + 1e-06) * norm_gain + norm_shift).astype(BF16)
         grown = jnp.dot(normed, w_expand[...], preferred_element_type=F32) + b_expand
-        reduced = jnp.dot(gelu_twice(grown).astype(BF16), w_reduce[...], preferred_element_type=F32)
+        reduced = jnp.dot(gelu_twice(grown.astype(BF16)), w_reduce[...], preferred_element_type=F32)
         for c in range(groups):
             lanes = slice(c * LANES, (c + 1) * LANES)
             centre = jnp.concatenate(

time: 35.5 us -> 35.1 us (0.989)
  Pallas kernels: 18.9 us -> 18.5 us
    pallas_call x2, Pallas kernels: 8.3 us -> 7.91 us  [run_block(): pl.pallas_call(functools.partial(block_kernel, tiles, turn, 12 + len(kept...]
  transfers between devices with their start and end apart: 8 -> 8, of which waited for: 1 -> 1; matrix products, arithmetic and copies ran while one was open for 0% -> 0% of each run, Pallas kernels for 46% -> 45%
where the time goes in v11:
time: 35.1 us; the launch traced here: 34.9 us
  Pallas kernels  18.5 us (53%)
  starting transfers between devices  9 us (26%)
  waiting for transfers between devices  6.38 us (18%)
  between operations  0.98 us (3%)
    pallas_call x2, Pallas kernels, run_block(): pl.pallas_call(functools.partial(block_kernel, tiles, turn, 12 + len(kept...  7.91 us
    ppermute x3, waiting for transfers between devices, body(): arrived.append(lax.ppermute(send, 'epoch', link))  6.37 us
    pallas_call x1, Pallas kernels, run_stage(): pl.pallas_call(stage_kernel, name='stage', out_shape=out_shape, in_specs=...  3.73 us
    ppermute x1, starting transfers between devices, body(): recv_next = lax.ppermute(to_next, 'tile', pairs(tiles, 1))  3.02 us
    ppermute x3, starting transfers between devices, body(): arrived.append(lax.ppermute(send, 'epoch', link))  2.63 us
    ppermute x3, starting transfers between devices, body(): arrived_far.append(lax.ppermute(send_far, 'epoch', link))  2.61 us
    pallas_call x3, Pallas kernels, run_later(): pl.pallas_call(functools.partial(later_kernel, early, turn, 6 + len(kept)...  2.52 us
    pallas_call x1, Pallas kernels, body(): pl.pallas_call(functools.partial(final_kernel, len(arrived)), name='final...  1.5 us
  transfers between devices with their start and end apart: 8, of which 1 were waited for; matrix products, arithmetic and copies ran while one was open for 0% of the time, Pallas kernels for 45%

profile of v11, /device:TPU:29, one launch (start us, length us, event | category | flops | bytes accessed | tf_op | source)
XLA Modules:
  0.0 34.9 jit_solution(326208952071276315)
XLA Ops:
  0.6 1.2 %near.1 = (bf16[2,16,16,384]{3,2,1,0:T(8,128)(2,1)S(1)}, f32[7,7,384]{2,1,0:T(8,128)S(1)}, s32[2,16,16]{2,1,0:T(8,128)S(1)}, s32[8]{0:T(128)S(1)}, f32[8]{0:T(12...) custom-call(bf16[2,16,16,384]{3,2,1,0:T(8,128)(2,1)} %refs_0_.1, ...), custom_call_target="tpu_custom_call" | custom-call | tf_op jit(solution)/shard_map/near/pallas_call | solution.py:53
  1.8 0.7 %collective-permute-start = (bf16[2,4,16,384]{3,2,1,0:T(8,128)(2,1)S(1)}, bf16[2,4,16,384]{3,2,1,0:T(8,128)(2,1)S(1)}, u32[]{:S(2)}, u32[]{:S(2)}) collective-permute-start(bf16[2,4,16,384]{3,2,1,0:T(8,128)(2,1)S(1)} %get-tuple-element.89), channel_id=1, source_target_pairs={{0,1},{1,0},{2,3},{3,2},{4,5},{5,4},{6,7},{7,6},{8,9},{9,8},{10,11... | collective-permute-start | bytes 294920 | tf_op jit(solution)/shard_map/ppermute | solution.py:749
  2.5 3.0 %collective-permute-start.1 = (bf16[2,4,16,384]{3,2,1,0:T(8,128)(2,1)S(1)}, bf16[2,4,16,384]{3,2,1,0:T(8,128)(2,1)S(1)}, u32[]{:S(2)}, u32[]{:S(2)}) collective-permute-start(bf16[2,4,16,384]{3,2,1,0:T(8,128)(2,1)S(1)} %get-tuple-element.90), channel_id=1, source_target_pairs={{1,2},{2,1},{5,6},{6,5},{9,10},{10,9},{13,14},{14,13},{17,18},{18,... | collective-permute-start | bytes 294920 | tf_op jit(solution)/shard_map/ppermute | solution.py:750
  5.6 3.7 %stage.1 = (f32[2,288,384]{2,1,0:T(8,128)S(1)}, f32[512,128]{1,0:T(8,128)S(1)}, f32[8,384]{1,0:T(8,128)S(1)}, f32[8,1536]{1,0:T(8,128)S(1)}, f32[8,128]{1,0:T(8,...) custom-call(bf16[2,16,16,384]{3,2,1,0:T(8,128)(2,1)S(1)} %get-tuple-, ...), custom_call_target="tpu_custom_call" | custom-call | flops 10000000000 | bytes 4718592 | tf_op jit(solution)/shard_map/stage/pallas_call | solution.py:200
  9.3 0.0 collective-permute-done.refs_1_
  9.3 0.0 collective-permute-done.1.refs_2_
  9.4 0.7 %collective-permute-start.3 = (bf16[256,256]{1,0:T(8,128)(2,1)S(1)}, bf16[256,256]{1,0:T(8,128)(2,1)S(1)}, u32[]{:S(2)}, u32[]{:S(2)}) collective-permute-start(bf16[256,256]{1,0:T(8,128)(2,1)S(1)} %get-tuple-element.100.refs_6_), channel_id=1, source_target_pairs={{0,4},{1,5},{2,6},{3,7},{16,20},{17,21},{18,22},{19,23}} | collective-permute-start | bytes 393224 | tf_op jit(solution)/shard_map/ppermute | solution.py:820
  10.1 0.7 %collective-permute-start.2 = (bf16[304,128]{1,0:T(8,128)(2,1)S(1)}, bf16[304,128]{1,0:T(8,128)(2,1)S(1)}, u32[]{:S(2)}, u32[]{:S(2)}) collective-permute-start(bf16[304,128]{1,0:T(8,128)(2,1)S(1)} %get-tuple-element.101.refs_18_.before), channel_id=1, source_target_pairs={{0,4},{1,5},{2,6},{3,7},{16,20},{17,21},{18,22},{19,23}} | collective-permute-start | bytes 233480 | tf_op jit(solution)/shard_map/ppermute | solution.py:821
  10.8 7.9 %block.3 = (f32[256,256]{1,0:T(8,128)S(1)}, f32[256,256]{1,0:T(8,128)S(1)}, f32[256,256]{1,0:T(8,128)S(1)}, f32[256,256]{1,0:T(8,128)S(1)}, f32[256,256]{1,0:T(8...) custom-call(f32[2,288,384]{2,1,0:T(8,128)S(1)} %get-tuple-element.88, ...), custom_call_target="tpu_custom_call", output_to_operand_aliasing={{0}: (12, {}), {1}: (13, {}), {2}: (14, {}), {3}: (15, {}),... | custom-call | flops 6643777536 | bytes 10616832 | tf_op jit(solution)/shard_map/block/pallas_call | solution.py:496
  18.7 0.0 collective-permute-done.3.arrived.refs_0_
  18.7 0.2 relay.2
  18.8 0.7 %collective-permute-start.5 = (bf16[256,256]{1,0:T(8,128)(2,1)S(1)}, bf16[256,256]{1,0:T(8,128)(2,1)S(1)}, u32[]{:S(2)}, u32[]{:S(2)}) collective-permute-start(bf16[256,256]{1,0:T(8,128)(2,1)S(1)} %get-tuple-element.129.refs_12_), channel_id=1, source_target_pairs={{4,8},{5,9},{6,10},{7,11},{20,24},{21,25},{22,26},{23,27}} | collective-permute-start | bytes 393224 | tf_op jit(solution)/shard_map/ppermute | solution.py:820
  19.5 2.5 %later.5 = (f32[256,128]{1,0:T(8,128)S(1)}, f32[256,128]{1,0:T(8,128)S(1)}, f32[256,128]{1,0:T(8,128)S(1)}, f32[256,128]{1,0:T(8,128)S(1)}, f32[256,128]{1,0:T(8,128)S(1)}, /*index=5*/f32[256,128]{1,0:T(8,128)S(1)}) custom-call(bf16[512,3456]{1,0:T(8,128)(2,1)S(1)} %get-tuple-element.1, ...), custom_call_target="tpu_custom_call", output_to_operand_aliasing={{0}: (6, {}), {1}: (7, {}), {2}: (8, {}), {3}: (9, {}), {4}... | custom-call | flops 10000000000 | tf_op jit(solution)/shard_map/later/pallas_call | solution.py:545
  22.0 0.0 collective-permute-done.2.arrived.refs_0_
  22.0 0.3 relay_later.2.before
  22.3 0.7 %collective-permute-start.4 = (bf16[304,128]{1,0:T(8,128)(2,1)S(1)}, bf16[304,128]{1,0:T(8,128)(2,1)S(1)}, u32[]{:S(2)}, u32[]{:S(2)}) collective-permute-start(bf16[304,128]{1,0:T(8,128)(2,1)S(1)} %relay_later.2.before), channel_id=1, source_target_pairs={{4,8},{5,9},{6,10},{7,11},{20,24},{21,25},{22,26},{23,27}} | collective-permute-start | bytes 233480 | tf_op jit(solution)/shard_map/ppermute | solution.py:821
  22.9 0.0 collective-permute-done.5.arrived.refs_1_
  22.9 0.2 relay.3
  23.1 1.3 %collective-permute-start.7 = (bf16[256,256]{1,0:T(8,128)(2,1)S(1)}, bf16[256,256]{1,0:T(8,128)(2,1)S(1)}, u32[]{:S(2)}, u32[]{:S(2)}) collective-permute-start(bf16[256,256]{1,0:T(8,128)(2,1)S(1)} %get-tuple-element.141), channel_id=1, source_target_pairs={{8,12},{9,13},{10,14},{11,15},{24,28},{25,29},{26,30},{27,31}} | collective-permute-start | bytes 393224 | tf_op jit(solution)/shard_map/ppermute | solution.py:820
  24.4 0.0 collective-permute-done.4.arrived.refs_1_
  24.4 0.3 relay_later.3
  24.7 1.3 %collective-permute-start.6 = (bf16[304,128]{1,0:T(8,128)(2,1)S(1)}, bf16[304,128]{1,0:T(8,128)(2,1)S(1)}, u32[]{:S(2)}, u32[]{:S(2)}) collective-permute-start(bf16[304,128]{1,0:T(8,128)(2,1)S(1)} %relay_later.3), channel_id=1, source_target_pairs={{8,12},{9,13},{10,14},{11,15},{24,28},{25,29},{26,30},{27,31}} | collective-permute-start | bytes 233480 | tf_op jit(solution)/shard_map/ppermute | solution.py:821
  26.0 6.4 %collective-permute-done.7.refs_2_ = bf16[256,256]{1,0:T(8,128)(2,1)S(1)} collective-permute-done((bf16[256,256]{1,0:T(8,128)(2,1)S(1)}, bf16[256,256]{1,0:T(8,128)(2,1)S(1)}, u32[]{:S(2)}, u32[]{:S(2)}) %collective-permute-start.7) | collective-permute-done | bytes 131104 | tf_op jit(solution)/shard_map/ppermute | solution.py:820
  32.3 0.9 %final_early.1 = (bf16[2,256,384]{2,1,0:T(8,128)(2,1)}, f32[8,256]{1,0:T(8,128)S(1)}, bf16[384,8]{1,0:T(8,128)(2,1)S(1)}, bf16[8,384]{1,0:T(8,128)(2,1)S(1)}) custom-call(bf16[256,256]{1,0:T(8,128)(2,1)S(1)} %collective-permute-done.3.arrived.refs_0_, bf16[256,256]{1,0:T(8,128)(2,1)S(1)} %collective-permute-done.5.arrived.refs_1_, ...), custom_call_target="tpu_custom_call" | custom-call | flops 10000000000 | tf_op jit(solution)/shard_map/final_early/pallas_call | solution.py:851
  33.2 0.0 collective-permute-done.6.refs_2_
  33.2 1.5 %final.1 = (bf16[2,256,384]{2,1,0:T(8,128)(2,1)}, bf16[2,384]{1,0:T(2,128)(2,1)}) custom-call(bf16[304,128]{1,0:T(8,128)(2,1)S(1)} %collective-permute-done.2.arrived.refs_0_, bf16[304,128]{1,0:T(8,128)(2,1)S(1)} %collective-permute-done.4.arrived.refs_1_, bf16[304,128]{1,0:T(8,128)(2,1)S(1)} %collective-permute-done.6.refs_2_, ...), custom_call_target="tpu_custom_call", output_to_operand_aliasing={{0}: (17, {})} | custom-call | tf_op jit(solution)/shard_map/final/pallas_call | solution.py:869
  (3 shorter events, 0.1 us)
Async XLA Ops:
  1.8 7.5 %collective-permute-start = (bf16[2,4,16,384]{3,2,1,0:T(8,128)(2,1)S(1)}, bf16[2,4,16,384]{3,2,1,0:T(8,128)(2,1)S(1)}, u32[]{:S(2)}, u32[]{:S(2)}) collective-permute-start(bf16[2,4,16,384]{3,2,1,0:T(8,128)(2,1)S(1)} %get-tuple-element.89), channel_id=1, source_target_pairs={{0,1},{1,0},{2,3},{3,2},{4,5},{5,4},{6,7},{7,6},{8,9},{9,8},{10,11... | collective-permute-start | bytes 294920 | tf_op jit(solution)/shard_map/ppermute | solution.py:749
  2.5 6.8 %collective-permute-start.1 = (bf16[2,4,16,384]{3,2,1,0:T(8,128)(2,1)S(1)}, bf16[2,4,16,384]{3,2,1,0:T(8,128)(2,1)S(1)}, u32[]{:S(2)}, u32[]{:S(2)}) collective-permute-start(bf16[2,4,16,384]{3,2,1,0:T(8,128)(2,1)S(1)} %get-tuple-element.90), channel_id=1, source_target_pairs={{1,2},{2,1},{5,6},{6,5},{9,10},{10,9},{13,14},{14,13},{17,18},{18,... | collective-permute-start | bytes 294920 | tf_op jit(solution)/shard_map/ppermute | solution.py:750
  9.4 9.3 %collective-permute-start.3 = (bf16[256,256]{1,0:T(8,128)(2,1)S(1)}, bf16[256,256]{1,0:T(8,128)(2,1)S(1)}, u32[]{:S(2)}, u32[]{:S(2)}) collective-permute-start(bf16[256,256]{1,0:T(8,128)(2,1)S(1)} %get-tuple-element.100.refs_6_), channel_id=1, source_target_pairs={{0,4},{1,5},{2,6},{3,7},{16,20},{17,21},{18,22},{19,23}} | collective-permute-start | bytes 393224 | tf_op jit(solution)/shard_map/ppermute | solution.py:820
  10.1 11.9 %collective-permute-start.2 = (bf16[304,128]{1,0:T(8,128)(2,1)S(1)}, bf16[304,128]{1,0:T(8,128)(2,1)S(1)}, u32[]{:S(2)}, u32[]{:S(2)}) collective-permute-start(bf16[304,128]{1,0:T(8,128)(2,1)S(1)} %get-tuple-element.101.refs_18_.before), channel_id=1, source_target_pairs={{0,4},{1,5},{2,6},{3,7},{16,20},{17,21},{18,22},{19,23}} | collective-permute-start | bytes 233480 | tf_op jit(solution)/shard_map/ppermute | solution.py:821
  18.8 4.1 %collective-permute-start.5 = (bf16[256,256]{1,0:T(8,128)(2,1)S(1)}, bf16[256,256]{1,0:T(8,128)(2,1)S(1)}, u32[]{:S(2)}, u32[]{:S(2)}) collective-permute-start(bf16[256,256]{1,0:T(8,128)(2,1)S(1)} %get-tuple-element.129.refs_12_), channel_id=1, source_target_pairs={{4,8},{5,9},{6,10},{7,11},{20,24},{21,25},{22,26},{23,27}} | collective-permute-start | bytes 393224 | tf_op jit(solution)/shard_map/ppermute | solution.py:820
  22.3 2.1 %collective-permute-start.4 = (bf16[304,128]{1,0:T(8,128)(2,1)S(1)}, bf16[304,128]{1,0:T(8,128)(2,1)S(1)}, u32[]{:S(2)}, u32[]{:S(2)}) collective-permute-start(bf16[304,128]{1,0:T(8,128)(2,1)S(1)} %relay_later.2.before), channel_id=1, source_target_pairs={{4,8},{5,9},{6,10},{7,11},{20,24},{21,25},{22,26},{23,27}} | collective-permute-start | bytes 233480 | tf_op jit(solution)/shard_map/ppermute | solution.py:821
  23.1 9.2 %collective-permute-start.7 = (bf16[256,256]{1,0:T(8,128)(2,1)S(1)}, bf16[256,256]{1,0:T(8,128)(2,1)S(1)}, u32[]{:S(2)}, u32[]{:S(2)}) collective-permute-start(bf16[256,256]{1,0:T(8,128)(2,1)S(1)} %get-tuple-element.141), channel_id=1, source_target_pairs={{8,12},{9,13},{10,14},{11,15},{24,28},{25,29},{26,30},{27,31}} | collective-permute-start | bytes 393224 | tf_op jit(solution)/shard_map/ppermute | solution.py:820
  24.7 8.6 %collective-permute-start.6 = (bf16[304,128]{1,0:T(8,128)(2,1)S(1)}, bf16[304,128]{1,0:T(8,128)(2,1)S(1)}, u32[]{:S(2)}, u32[]{:S(2)}) collective-permute-start(bf16[304,128]{1,0:T(8,128)(2,1)S(1)} %relay_later.3), channel_id=1, source_target_pairs={{8,12},{9,13},{10,14},{11,15},{24,28},{25,29},{26,30},{27,31}} | collective-permute-start | bytes 233480 | tf_op jit(solution)/shard_map/ppermute | solution.py:821

commit v12 on v11

--- a/solution.py
+++ b/solution.py
@@ -400,8 +400,14 @@
     cell = None
     for e, opens in enumerate((open0, open1)):
         rows = slice(e * pixels, (e + 1) * pixels)
-        preact = jnp.dot(taps[rows, :], weights[...], preferred_element_type=F32) + bias
-        gate_in, gate_keep, gate_new, gate_out = gates_of(preact)
+        pieces = []
+        for part in range(2):
+            at_rows = slice(e * pixels + part * pixels // 2, e * pixels + (part + 1) * pixels // 2)
+            preact = jnp.dot(taps[at_rows, :], weights[...], preferred_element_type=F32) + bias
+            pieces.append(gates_of(preact))
+        gate_in, gate_keep, gate_new, gate_out = [
+            jnp.concatenate(both, axis=0) for both in zip(*pieces)
+        ]
         good = mask[rows, :] > 0.5
         decay = jnp.where(good, jnp.exp(-rate * softplus(gate_keep)), 1.0)
         inflow = jnp.where(good, sigmoid(gate_in) * jnp.tanh(gate_new), 0.0)

time: 35.1 us -> 35 us (level)
  no operation moved by 1% of the time
where the time goes in v12:
time: 35 us; the launch traced here: 34.8 us
  Pallas kernels  18.5 us (53%)
  starting transfers between devices  9 us (26%)
  waiting for transfers between devices  6.35 us (18%)
  between operations  0.98 us (3%)
    pallas_call x2, Pallas kernels, run_block(): pl.pallas_call(functools.partial(block_kernel, tiles, turn, 12 + len(kept...  7.92 us
    ppermute x3, waiting for transfers between devices, body(): arrived.append(lax.ppermute(send, 'epoch', link))  6.34 us
    pallas_call x1, Pallas kernels, run_stage(): pl.pallas_call(stage_kernel, name='stage', out_shape=out_shape, in_specs=...  3.73 us
    ppermute x1, starting transfers between devices, body(): recv_next = lax.ppermute(to_next, 'tile', pairs(tiles, 1))  3.02 us
    ppermute x3, starting transfers between devices, body(): arrived.append(lax.ppermute(send, 'epoch', link))  2.63 us
    ppermute x3, starting transfers between devices, body(): arrived_far.append(lax.ppermute(send_far, 'epoch', link))  2.61 us
    pallas_call x3, Pallas kernels, run_later(): pl.pallas_call(functools.partial(later_kernel, early, turn, 6 + len(kept)...  2.42 us
    pallas_call x1, Pallas kernels, body(): pl.pallas_call(functools.partial(final_kernel, len(arrived)), name='final...  1.5 us
  transfers between devices with their start and end apart: 8, of which 1 were waited for; matrix products, arithmetic and copies ran while one was open for 0% of the time, Pallas kernels for 45%

profile of v12, /device:TPU:29, one launch (start us, length us, event | category | flops | bytes accessed | tf_op | source)
XLA Modules:
  0.0 34.8 jit_solution(15168206306591337435)
XLA Ops:
  0.6 1.2 %near.1 = (bf16[2,16,16,384]{3,2,1,0:T(8,128)(2,1)S(1)}, f32[7,7,384]{2,1,0:T(8,128)S(1)}, s32[2,16,16]{2,1,0:T(8,128)S(1)}, s32[8]{0:T(128)S(1)}, f32[8]{0:T(12...) custom-call(bf16[2,16,16,384]{3,2,1,0:T(8,128)(2,1)} %refs_0_.1, ...), custom_call_target="tpu_custom_call" | custom-call | tf_op jit(solution)/shard_map/near/pallas_call | solution.py:53
  1.8 0.7 %collective-permute-start = (bf16[2,4,16,384]{3,2,1,0:T(8,128)(2,1)S(1)}, bf16[2,4,16,384]{3,2,1,0:T(8,128)(2,1)S(1)}, u32[]{:S(2)}, u32[]{:S(2)}) collective-permute-start(bf16[2,4,16,384]{3,2,1,0:T(8,128)(2,1)S(1)} %get-tuple-element.89), channel_id=1, source_target_pairs={{0,1},{1,0},{2,3},{3,2},{4,5},{5,4},{6,7},{7,6},{8,9},{9,8},{10,11... | collective-permute-start | bytes 294920 | tf_op jit(solution)/shard_map/ppermute | solution.py:755
  2.5 3.0 %collective-permute-start.1 = (bf16[2,4,16,384]{3,2,1,0:T(8,128)(2,1)S(1)}, bf16[2,4,16,384]{3,2,1,0:T(8,128)(2,1)S(1)}, u32[]{:S(2)}, u32[]{:S(2)}) collective-permute-start(bf16[2,4,16,384]{3,2,1,0:T(8,128)(2,1)S(1)} %get-tuple-element.90), channel_id=1, source_target_pairs={{1,2},{2,1},{5,6},{6,5},{9,10},{10,9},{13,14},{14,13},{17,18},{18,... | collective-permute-start | bytes 294920 | tf_op jit(solution)/shard_map/ppermute | solution.py:756
  5.6 3.7 %stage.1 = (f32[2,288,384]{2,1,0:T(8,128)S(1)}, f32[512,128]{1,0:T(8,128)S(1)}, f32[8,384]{1,0:T(8,128)S(1)}, f32[8,1536]{1,0:T(8,128)S(1)}, f32[8,128]{1,0:T(8,...) custom-call(bf16[2,16,16,384]{3,2,1,0:T(8,128)(2,1)S(1)} %get-tuple-, ...), custom_call_target="tpu_custom_call" | custom-call | flops 10000000000 | bytes 4718592 | tf_op jit(solution)/shard_map/stage/pallas_call | solution.py:200
  9.3 0.0 collective-permute-done.refs_1_
  9.3 0.0 collective-permute-done.1.refs_2_
  9.4 0.7 %collective-permute-start.3 = (bf16[256,256]{1,0:T(8,128)(2,1)S(1)}, bf16[256,256]{1,0:T(8,128)(2,1)S(1)}, u32[]{:S(2)}, u32[]{:S(2)}) collective-permute-start(bf16[256,256]{1,0:T(8,128)(2,1)S(1)} %get-tuple-element.100.refs_6_), channel_id=1, source_target_pairs={{0,4},{1,5},{2,6},{3,7},{16,20},{17,21},{18,22},{19,23}} | collective-permute-start | bytes 393224 | tf_op jit(solution)/shard_map/ppermute | solution.py:826
  10.1 0.7 %collective-permute-start.2 = (bf16[304,128]{1,0:T(8,128)(2,1)S(1)}, bf16[304,128]{1,0:T(8,128)(2,1)S(1)}, u32[]{:S(2)}, u32[]{:S(2)}) collective-permute-start(bf16[304,128]{1,0:T(8,128)(2,1)S(1)} %get-tuple-element.101.refs_18_.before), channel_id=1, source_target_pairs={{0,4},{1,5},{2,6},{3,7},{16,20},{17,21},{18,22},{19,23}} | collective-permute-start | bytes 233480 | tf_op jit(solution)/shard_map/ppermute | solution.py:827
  10.8 7.9 %block.3 = (f32[256,256]{1,0:T(8,128)S(1)}, f32[256,256]{1,0:T(8,128)S(1)}, f32[256,256]{1,0:T(8,128)S(1)}, f32[256,256]{1,0:T(8,128)S(1)}, f32[256,256]{1,0:T(8...) custom-call(f32[2,288,384]{2,1,0:T(8,128)S(1)} %get-tuple-element.88, ...), custom_call_target="tpu_custom_call", output_to_operand_aliasing={{0}: (12, {}), {1}: (13, {}), {2}: (14, {}), {3}: (15, {}),... | custom-call | flops 6643777536 | bytes 10616832 | tf_op jit(solution)/shard_map/block/pallas_call | solution.py:502
  18.7 0.0 collective-permute-done.3.arrived.refs_0_
  18.7 0.2 relay.2
  18.8 0.7 %collective-permute-start.5 = (bf16[256,256]{1,0:T(8,128)(2,1)S(1)}, bf16[256,256]{1,0:T(8,128)(2,1)S(1)}, u32[]{:S(2)}, u32[]{:S(2)}) collective-permute-start(bf16[256,256]{1,0:T(8,128)(2,1)S(1)} %get-tuple-element.129.refs_12_), channel_id=1, source_target_pairs={{4,8},{5,9},{6,10},{7,11},{20,24},{21,25},{22,26},{23,27}} | collective-permute-start | bytes 393224 | tf_op jit(solution)/shard_map/ppermute | solution.py:826
  19.5 2.4 %later.5 = (f32[256,128]{1,0:T(8,128)S(1)}, f32[256,128]{1,0:T(8,128)S(1)}, f32[256,128]{1,0:T(8,128)S(1)}, f32[256,128]{1,0:T(8,128)S(1)}, f32[256,128]{1,0:T(8,128)S(1)}, /*index=5*/f32[256,128]{1,0:T(8,128)S(1)}) custom-call(bf16[512,3456]{1,0:T(8,128)(2,1)S(1)} %get-tuple-element.1, ...), custom_call_target="tpu_custom_call", output_to_operand_aliasing={{0}: (6, {}), {1}: (7, {}), {2}: (8, {}), {3}: (9, {}), {4}... | custom-call | flops 10000000000 | tf_op jit(solution)/shard_map/later/pallas_call | solution.py:551
  21.9 0.0 collective-permute-done.2.arrived.refs_0_
  21.9 0.3 relay_later.2.before
  22.2 0.7 %collective-permute-start.4 = (bf16[304,128]{1,0:T(8,128)(2,1)S(1)}, bf16[304,128]{1,0:T(8,128)(2,1)S(1)}, u32[]{:S(2)}, u32[]{:S(2)}) collective-permute-start(bf16[304,128]{1,0:T(8,128)(2,1)S(1)} %relay_later.2.before), channel_id=1, source_target_pairs={{4,8},{5,9},{6,10},{7,11},{20,24},{21,25},{22,26},{23,27}} | collective-permute-start | bytes 233480 | tf_op jit(solution)/shard_map/ppermute | solution.py:827
  22.8 0.0 collective-permute-done.5.arrived.refs_1_
  22.9 0.2 relay.3
  23.0 1.3 %collective-permute-start.7 = (bf16[256,256]{1,0:T(8,128)(2,1)S(1)}, bf16[256,256]{1,0:T(8,128)(2,1)S(1)}, u32[]{:S(2)}, u32[]{:S(2)}) collective-permute-start(bf16[256,256]{1,0:T(8,128)(2,1)S(1)} %get-tuple-element.141), channel_id=1, source_target_pairs={{8,12},{9,13},{10,14},{11,15},{24,28},{25,29},{26,30},{27,31}} | collective-permute-start | bytes 393224 | tf_op jit(solution)/shard_map/ppermute | solution.py:826
  24.3 0.0 collective-permute-done.4.arrived.refs_1_
  24.3 0.3 relay_later.3
  24.6 1.3 %collective-permute-start.6 = (bf16[304,128]{1,0:T(8,128)(2,1)S(1)}, bf16[304,128]{1,0:T(8,128)(2,1)S(1)}, u32[]{:S(2)}, u32[]{:S(2)}) collective-permute-start(bf16[304,128]{1,0:T(8,128)(2,1)S(1)} %relay_later.3), channel_id=1, source_target_pairs={{8,12},{9,13},{10,14},{11,15},{24,28},{25,29},{26,30},{27,31}} | collective-permute-start | bytes 233480 | tf_op jit(solution)/shard_map/ppermute | solution.py:827
  25.9 6.3 %collective-permute-done.7.refs_2_ = bf16[256,256]{1,0:T(8,128)(2,1)S(1)} collective-permute-done((bf16[256,256]{1,0:T(8,128)(2,1)S(1)}, bf16[256,256]{1,0:T(8,128)(2,1)S(1)}, u32[]{:S(2)}, u32[]{:S(2)}) %collective-permute-start.7) | collective-permute-done | bytes 131104 | tf_op jit(solution)/shard_map/ppermute | solution.py:826
  32.2 0.9 %final_early.1 = (bf16[2,256,384]{2,1,0:T(8,128)(2,1)}, f32[8,256]{1,0:T(8,128)S(1)}, bf16[384,8]{1,0:T(8,128)(2,1)S(1)}, bf16[8,384]{1,0:T(8,128)(2,1)S(1)}) custom-call(bf16[256,256]{1,0:T(8,128)(2,1)S(1)} %collective-permute-done.3.arrived.refs_0_, bf16[256,256]{1,0:T(8,128)(2,1)S(1)} %collective-permute-done.5.arrived.refs_1_, ...), custom_call_target="tpu_custom_call" | custom-call | flops 10000000000 | tf_op jit(solution)/shard_map/final_early/pallas_call | solution.py:857
  33.1 0.0 collective-permute-done.6.refs_2_
  33.1 1.5 %final.1 = (bf16[2,256,384]{2,1,0:T(8,128)(2,1)}, bf16[2,384]{1,0:T(2,128)(2,1)}) custom-call(bf16[304,128]{1,0:T(8,128)(2,1)S(1)} %collective-permute-done.2.arrived.refs_0_, bf16[304,128]{1,0:T(8,128)(2,1)S(1)} %collective-permute-done.4.arrived.refs_1_, bf16[304,128]{1,0:T(8,128)(2,1)S(1)} %collective-permute-done.6.refs_2_, ...), custom_call_target="tpu_custom_call", output_to_operand_aliasing={{0}: (17, {})} | custom-call | tf_op jit(solution)/shard_map/final/pallas_call | solution.py:875
  (3 shorter events, 0.1 us)
Async XLA Ops:
  1.8 7.5 %collective-permute-start = (bf16[2,4,16,384]{3,2,1,0:T(8,128)(2,1)S(1)}, bf16[2,4,16,384]{3,2,1,0:T(8,128)(2,1)S(1)}, u32[]{:S(2)}, u32[]{:S(2)}) collective-permute-start(bf16[2,4,16,384]{3,2,1,0:T(8,128)(2,1)S(1)} %get-tuple-element.89), channel_id=1, source_target_pairs={{0,1},{1,0},{2,3},{3,2},{4,5},{5,4},{6,7},{7,6},{8,9},{9,8},{10,11... | collective-permute-start | bytes 294920 | tf_op jit(solution)/shard_map/ppermute | solution.py:755
  2.5 6.8 %collective-permute-start.1 = (bf16[2,4,16,384]{3,2,1,0:T(8,128)(2,1)S(1)}, bf16[2,4,16,384]{3,2,1,0:T(8,128)(2,1)S(1)}, u32[]{:S(2)}, u32[]{:S(2)}) collective-permute-start(bf16[2,4,16,384]{3,2,1,0:T(8,128)(2,1)S(1)} %get-tuple-element.90), channel_id=1, source_target_pairs={{1,2},{2,1},{5,6},{6,5},{9,10},{10,9},{13,14},{14,13},{17,18},{18,... | collective-permute-start | bytes 294920 | tf_op jit(solution)/shard_map/ppermute | solution.py:756
  9.4 9.3 %collective-permute-start.3 = (bf16[256,256]{1,0:T(8,128)(2,1)S(1)}, bf16[256,256]{1,0:T(8,128)(2,1)S(1)}, u32[]{:S(2)}, u32[]{:S(2)}) collective-permute-start(bf16[256,256]{1,0:T(8,128)(2,1)S(1)} %get-tuple-element.100.refs_6_), channel_id=1, source_target_pairs={{0,4},{1,5},{2,6},{3,7},{16,20},{17,21},{18,22},{19,23}} | collective-permute-start | bytes 393224 | tf_op jit(solution)/shard_map/ppermute | solution.py:826
  10.1 11.8 %collective-permute-start.2 = (bf16[304,128]{1,0:T(8,128)(2,1)S(1)}, bf16[304,128]{1,0:T(8,128)(2,1)S(1)}, u32[]{:S(2)}, u32[]{:S(2)}) collective-permute-start(bf16[304,128]{1,0:T(8,128)(2,1)S(1)} %get-tuple-element.101.refs_18_.before), channel_id=1, source_target_pairs={{0,4},{1,5},{2,6},{3,7},{16,20},{17,21},{18,22},{19,23}} | collective-permute-start | bytes 233480 | tf_op jit(solution)/shard_map/ppermute | solution.py:827
  18.8 4.0 %collective-permute-start.5 = (bf16[256,256]{1,0:T(8,128)(2,1)S(1)}, bf16[256,256]{1,0:T(8,128)(2,1)S(1)}, u32[]{:S(2)}, u32[]{:S(2)}) collective-permute-start(bf16[256,256]{1,0:T(8,128)(2,1)S(1)} %get-tuple-element.129.refs_12_), channel_id=1, source_target_pairs={{4,8},{5,9},{6,10},{7,11},{20,24},{21,25},{22,26},{23,27}} | collective-permute-start | bytes 393224 | tf_op jit(solution)/shard_map/ppermute | solution.py:826
  22.2 2.1 %collective-permute-start.4 = (bf16[304,128]{1,0:T(8,128)(2,1)S(1)}, bf16[304,128]{1,0:T(8,128)(2,1)S(1)}, u32[]{:S(2)}, u32[]{:S(2)}) collective-permute-start(bf16[304,128]{1,0:T(8,128)(2,1)S(1)} %relay_later.2.before), channel_id=1, source_target_pairs={{4,8},{5,9},{6,10},{7,11},{20,24},{21,25},{22,26},{23,27}} | collective-permute-start | bytes 233480 | tf_op jit(solution)/shard_map/ppermute | solution.py:827
  23.0 9.2 %collective-permute-start.7 = (bf16[256,256]{1,0:T(8,128)(2,1)S(1)}, bf16[256,256]{1,0:T(8,128)(2,1)S(1)}, u32[]{:S(2)}, u32[]{:S(2)}) collective-permute-start(bf16[256,256]{1,0:T(8,128)(2,1)S(1)} %get-tuple-element.141), channel_id=1, source_target_pairs={{8,12},{9,13},{10,14},{11,15},{24,28},{25,29},{26,30},{27,31}} | collective-permute-start | bytes 393224 | tf_op jit(solution)/shard_map/ppermute | solution.py:826
  24.6 8.5 %collective-permute-start.6 = (bf16[304,128]{1,0:T(8,128)(2,1)S(1)}, bf16[304,128]{1,0:T(8,128)(2,1)S(1)}, u32[]{:S(2)}, u32[]{:S(2)}) collective-permute-start(bf16[304,128]{1,0:T(8,128)(2,1)S(1)} %relay_later.3), channel_id=1, source_target_pairs={{8,12},{9,13},{10,14},{11,15},{24,28},{25,29},{26,30},{27,31}} | collective-permute-start | bytes 233480 | tf_op jit(solution)/shard_map/ppermute | solution.py:827
